TPU v7x, 512 devices: a whole 4x8x8 slice. The times are simulated.
512 devices in a mesh: prow: 32 (over z, x), pcol: 16 (over y, core).
Axes of the slice: x: 4, y: 8, z: 8, core: 2. Of those that a mesh axis runs over, the one named last changes fastest.
Arguments:
- matrix: float32 [24576, 12288], P('prow', 'pcol'), may hold values from -6 to 6
- pivots: int32 [2, 256], replicated, may hold values from 0 to 24575, as said below
- lower_inv: float32 [2, 256, 256], replicated, as said below
- upper_inv: float32 [2, 256, 256], replicated, as said below
Outputs:
- factored: float32 [24576, 12288], P('prow', 'pcol')
Inputs may be any that keep to these rules, and one draw needn't show every extreme that they name: `pivots`: for each panel p the 256 entries are distinct; entry j is either the row p * 768 + j itself or a row that lies outside the diagonal rows of panels 0..p. `lower_inv`: each block is unit lower triangular. `upper_inv`: each block is upper triangular with positive diagonal.
All inputs are finite; a program needn't handle non-finite values.
Results may differ from a plain program's by a relative error of at most 0.0001.
Values sent between devices are 32-bit elements; how exact they have to be, the bound alone decides.
No kernel may reach another device: no remote copies, remote signals or barrier semaphores. Data moves between devices by JAX's collectives and lax.ppermute only.
A program may use at most 64 MiB of HBM per device.

v0:
```python
import functools

import jax
import jax.numpy as jnp
from jax import lax
from jax.experimental import pallas as pl
from jax.experimental.layout import Layout, with_layout_constraint
from jax.experimental.pallas import tpu as pltpu
from jax.sharding import Mesh, PartitionSpec as P

HIGHEST = lax.Precision.HIGHEST
F32 = jnp.float32
BF16 = jnp.bfloat16
NB = 256
RD = 768
PROW = ("z", "x")
PCOL = ("y", "core")
NP = 32
ROW_MAJOR = Layout((0, 1))


def hdot(a, b):
    return jnp.dot(a, b, precision=HIGHEST, preferred_element_type=F32)


def iota(shape, dim):
    return lax.broadcasted_iota(jnp.int32, shape, dim)


def f(mask):
    return jnp.where(mask, F32(1.0), F32(0.0))


def sum_rows(x):
    return jnp.sum(x, axis=0, keepdims=True)


def sum_cols(x):
    return jnp.sum(x, axis=1, keepdims=True)


def owner_of(row):
    return ((row >> 8) * 171) >> 9


def slot_of(rank, g):
    return ((rank & 3) * 128 + ((rank >> 2) & 7) * 16 + g * 8 + (rank >> 5)).astype(F32)


def index_math(pr, pc):
    p0r, p1r = pr[0:1, :], pr[1:2, :]
    p0c, p1c = pc[:, 0:1], pc[:, 1:2]
    sub, lane = iota((NB, NB), 0), iota((NB, NB), 1)
    lr, lc = iota((1, NB), 1), iota((NB, 1), 0)
    m_kj = f(p0c == lane + RD)
    n_kj = f(p0c == p1r)
    m_jk = f(p0r == sub + RD)
    n_jk = f(p0r == p1c)
    p1rf, p1cf = p1r.astype(F32), p1c.astype(F32)

    def dest(p0, p1, ids, has_m, has_n, piv_m, has_mk):
        stay0 = (p0 == ids) | (has_n > 0)
        end0 = jnp.where(has_m > 0, piv_m.astype(jnp.int32), p0)
        stay1 = (p1 == ids + RD) | (has_mk > 0)
        out = []
        for stay, end in ((stay0, end0), (stay1, p1)):
            own = owner_of(end)
            out.append((jnp.where(stay, NP, own), end - own * RD))
        return out

    has_m_c, has_n_c = sum_cols(m_kj), sum_cols(n_kj)
    has_m_r, has_n_r = sum_rows(m_jk), sum_rows(n_jk)
    has_mk_r, has_nk_r = sum_rows(m_kj), sum_rows(n_kj)
    has_mk_c, has_nk_c = sum_cols(m_jk), sum_cols(n_jk)
    dest_r = dest(p0r, p1r, lr, has_m_r, has_n_r, sum_rows(m_jk * p1cf), has_mk_r)
    dest_c = dest(p0c, p1c, lc, has_m_c, has_n_c, sum_cols(m_kj * p1rf), has_mk_c)
    ranks_r, ranks_c, pos_r, pos_c = [], [], [], []
    for g in range(2):
        key_r = dest_r[g][0] * NB + lr
        key_c = dest_c[g][0] * NB + lc
        rank_r = sum_rows(f(key_c < key_r)).astype(jnp.int32)
        rank_c = sum_cols(f(key_r < key_c)).astype(jnp.int32)
        ranks_r.append(rank_r)
        ranks_c.append(rank_c)
        pos_r.append(slot_of(rank_r, g))
        pos_c.append(slot_of(rank_c, g))
    w_r = jnp.where(has_mk_r > 0, sum_rows(m_kj * pos_c[0]), pos_r[1])
    w_c = jnp.where(has_mk_c > 0, sum_cols(m_jk * pos_r[0]), pos_c[1])
    src0 = jnp.where(
        has_m_c > 0,
        sum_cols(m_kj * pos_r[1]),
        jnp.where(has_n_c > 0, sum_cols(n_kj * w_r), pos_c[0]),
    )
    src1 = jnp.where(has_nk_c > 0, sum_cols(n_jk * pos_r[0]), w_c)
    rows, cols = [], []
    for g in range(2):
        rows += [ranks_r[g], dest_r[g][0], dest_r[g][1]]
        cols += [ranks_c[g], dest_c[g][0], dest_c[g][1]]
    cols += [src0.astype(jnp.int32), src1.astype(jnp.int32)]
    return rows, cols


def bdot(a, b):
    return jnp.dot(a, b, preferred_element_type=F32)


def halves(x):
    hi = x.astype(BF16)
    return hi, (x - hi.astype(F32)).astype(BF16)


def dot3(a, b):
    ah, al = halves(a)
    bh, bl = halves(b)
    return bdot(jnp.concatenate([ah, ah, al], axis=1), jnp.concatenate([bh, bl, bh], axis=0))


def pick2(p, x):
    p = p.astype(BF16)
    hi, lo = halves(x)
    return bdot(jnp.concatenate([p, p], axis=1), jnp.concatenate([hi, lo], axis=0))


def pick3(p, x):
    p = p.astype(BF16)
    hi = x.astype(BF16)
    rest = x - hi.astype(F32)
    mid = rest.astype(BF16)
    low = (rest - mid.astype(F32)).astype(BF16)
    return bdot(p, hi) + (bdot(p, mid) + bdot(p, low))


def pack_kernel(ids, pr_ref, pc_ref, a_ref, send_ref, ir_ref, ic_ref):
    me = ids[0]
    rows, cols = index_math(pr_ref[...], pc_ref[...])
    for n, v in enumerate(rows):
        ir_ref[n : n + 1, :] = v
    ir_ref[6:8, :] = jnp.zeros((2, NB), jnp.int32)
    for n, v in enumerate(cols):
        ic_ref[:, n : n + 1] = v
    line = iota((NB, NB), 0)
    rank = jnp.where(me == 1, rows[3], rows[0])
    perm = f(rank == (line >> 3) + NP * (line & 7))
    old = pick3(perm, a_ref[0:NB, :])
    line = iota((2 * NP, NB), 0)
    pick = jnp.zeros((2 * NP, RD), F32)
    for g in range(2):
        rank, own = rows[3 * g], rows[3 * g + 1]
        s = f(((line & 1) == g) & ((rank & 31) == (line >> 1)) & (own == me))
        t = f(cols[3 * g + 2] == iota((NB, RD), 1))
        pick = pick + bdot(s.astype(BF16), t.astype(BF16))
    ext = pick3(pick, a_ref[...])
    for m in range(NP):
        send_ref[m, 0:8, :] = old[8 * m : 8 * m + 8]
        send_ref[m, 8:10, :] = ext[2 * m : 2 * m + 2]


def turn_kernel(ids, ir_ref, ic_ref, ext_ref, old0_ref, old1_ref, send_ref):
    me = ids[0]
    line = iota((16, NB), 0)
    want = me + NP * (line & 7)
    own = jnp.zeros((16, 1), F32)
    for g in range(2):
        hit = f((ir_ref[3 * g : 3 * g + 1, :] == want) & ((line >> 3) == g))
        own = own + sum_cols(hit * ir_ref[3 * g + 1 : 3 * g + 2, :].astype(F32))
    own = own.astype(jnp.int32)
    old = jnp.concatenate([old0_ref[...], old1_ref[...]], axis=0)
    lane = iota((16, 2 * NP), 1)
    pick = f((own == (lane >> 1)) & ((iota((16, 2 * NP), 0) >> 3) == (lane & 1)))
    slots = jnp.where(own == NP, old, pick3(pick, ext_ref[...]))
    want = me + NP * (iota((NB, 16), 1) & 7)
    own = jnp.zeros((1, 16), F32)
    for g in range(2):
        hit = f((ic_ref[:, 3 * g : 3 * g + 1] == want) & ((iota((NB, 16), 1) >> 3) == g))
        own = own + sum_rows(hit * ic_ref[:, 3 * g + 1 : 3 * g + 2].astype(F32))
    own = own.astype(jnp.int32)
    line = iota((2 * NP, 16), 0)
    give = f((own == (line >> 1)) & ((iota((2 * NP, 16), 1) >> 3) == (line & 1)))
    back = pick3(give, old)
    for z in range(8):
        send_ref[z, 0:16, :] = slots
        send_ref[z, 16:24, :] = back[8 * z : 8 * z + 8]


def arrange(get, out_ref):
    for x in range(4):
        for z in range(8):
            out_ref[x, 16 * z : 16 * z + 16, :] = get(z, 0, 16)
            out_ref[x, 128 + 2 * z : 130 + 2 * z, :] = get(z, 16 + 2 * x, 18 + 2 * x)


def mid_kernel(in_ref, out_ref, side_ref):
    arrange(lambda z, a, b: in_ref[z, a:b, :], out_ref)
    for z in range(8):
        side_ref[24 * z : 24 * z + 24, :] = in_ref[z, :, 0:NB]


def side_kernel(ids, *refs):
    own, out, sums = refs[0], refs[8], refs[9]
    total = jnp.where(ids[2] == 0, own[...], F32(0.0))
    for r in refs[1:8]:
        total = total + r[...]
    sums[...] = total
    arrange(lambda z, a, b: sums[24 * z + a : 24 * z + b, :], out)


def slots_of(ref):
    return jnp.concatenate([ref[x, 0:128, :] for x in range(4)], axis=0)


def back_of(ref):
    return jnp.concatenate([ref[x, 128:144, :] for x in range(4)], axis=0)


def main_kernel(ids, ir_ref, ic_ref, a_ref, x_ref, li_ref, base_ref, put_ref, new0_ref, new1_ref, u0_ref):
    me = ids[0]
    put = jnp.zeros((RD, 2 * NP), F32)
    lane = iota((NB, 2 * NP), 1)
    m = ((lane >> 1) & 7) * 4 + (lane >> 4)
    for g in range(2):
        own, loc = ir_ref[3 * g + 1 : 3 * g + 2, :], ir_ref[3 * g + 2 : 3 * g + 3, :]
        t = f((own == me) & (loc == iota((RD, NB), 0)))
        s = f(((ic_ref[:, 3 * g : 3 * g + 1] & 31) == m) & ((lane & 1) == g))
        put = put + bdot(t.astype(BF16), s.astype(BF16))
    put_ref[...] = put
    x = slots_of(x_ref)
    new = []
    for n in range(2):
        new.append(pick3(f(ic_ref[:, 6 + n : 7 + n] == iota((NB, 2 * NB), 1)), x))
    new0_ref[...], new1_ref[...] = new
    u0_ref[...] = dot3(li_ref[0], new[0])
    back = back_of(x_ref)
    for r in range(3):
        part = put[NB * r : NB * r + NB]
        rows = pl.ds(NB * r, NB)
        base_ref[rows, :] = jnp.where(sum_cols(part) > 0, pick3(part, back), a_ref[rows, :])


def final_kernel(
    ids, ic_ref, raw_ref, mine_ref, there_ref, base_ref, put_ref, new0_ref, new1_ref, u0_ref,
    li_ref, ui_ref, out_ref, low_ref, up_ref,
):
    me, col, core = ids[0], ids[1], ids[3]
    mine, there = mine_ref[...], there_ref[...]
    s0 = jnp.where(core == 0, mine, there)
    s1 = jnp.where(core == 0, there, mine)
    slots0, slots1 = slots_of(s0), slots_of(s1)
    back0, back1 = back_of(s0), back_of(s1)
    perm0 = f(ic_ref[:, 6:7] == iota((NB, 2 * NB), 1))
    perm1 = f(ic_ref[:, 7:8] == iota((NB, 2 * NB), 1))
    u0 = u0_ref[...]
    u0c1 = dot3(li_ref[0], pick2(perm0, slots1))
    diag = dot3(pick2(perm1, slots0), ui_ref[0])
    next1 = new1_ref[...] - dot3(diag, u0)
    u1 = dot3(li_ref[1], next1)
    for n, u in enumerate((u0, u1)):
        hi, lo = halves(u)
        for k, v in enumerate((hi, lo, hi)):
            up_ref[NB * (3 * n + k) : NB * (3 * n + k + 1), :] = v
    raw0 = jnp.concatenate([raw_ref[y, 0] for y in range(8)], axis=0)
    raw1 = jnp.concatenate([raw_ref[y, 1] for y in range(8)], axis=0)
    for r in range(3):
        rows = pl.ds(NB * r, NB)
        part = put_ref[rows, :]
        moved = sum_cols(part) > 0
        c0 = jnp.where(moved, pick2(part, back0), raw0[NB * r : NB * r + NB])
        c1 = jnp.where(moved, pick2(part, back1), raw1[NB * r : NB * r + NB])
        low0 = dot3(c0, ui_ref[0])
        low1 = dot3(c1 - dot3(low0, u0c1), ui_ref[1])
        for n, low in enumerate((low0, low1)):
            hi, lo = halves(low)
            for k, v in enumerate((hi, hi, lo)):
                low_ref[:, NB * (3 * n + k) : NB * (3 * n + k + 1)] = v
        out_ref[rows, :] = base_ref[rows, :] - bdot(low_ref[...], up_ref[...])

        @pl.when(col == 0)
        def _():
            out_ref[rows, 0:NB] = low0

        @pl.when(col == 1)
        def _():
            out_ref[rows, 0:NB] = low1

    @pl.when(me == 0)
    def _():
        out_ref[0:NB, :] = u0

        @pl.when(col == 0)
        def _():
            out_ref[0:NB, 0:NB] = new0_ref[:, 0:NB]

    @pl.when(me == 1)
    def _():
        out_ref[0:NB, :] = u1

        @pl.when(col == 0)
        def _():
            out_ref[0:NB, 0:NB] = diag

        @pl.when(col == 1)
        def _():
            out_ref[0:NB, 0:NB] = next1[:, 0:NB]


def call(kernel, outs, ids, *args, scratch=(), flops=0):
    vmem = pl.BlockSpec(memory_space=pltpu.VMEM)
    smem = [] if ids is None else [pl.BlockSpec(memory_space=pltpu.SMEM)]
    sizes = [4 * o.size for o in jax.tree.leaves((outs, args))]
    return pl.pallas_call(
        kernel,
        out_shape=outs,
        in_specs=smem + [vmem] * len(args),
        out_specs=jax.tree.map(lambda _: vmem, outs),
        scratch_shapes=scratch,
        compiler_params=pltpu.CompilerParams(vmem_limit_bytes=40 * 1024 * 1024),
        cost_estimate=pl.CostEstimate(flops=flops, bytes_accessed=sum(sizes), transcendentals=0),
    )(*([] if ids is None else [ids]), *args)


def shape(*dims, dtype=F32):
    return jax.ShapeDtypeStruct(dims, dtype)


AROUND = (4, 3, 5, 2, 6, 1, 7)


def fast(matrix, pivots, lower_inv, upper_inv):
    prow_idx = lax.axis_index(PROW).astype(jnp.int32)
    pcol_idx = lax.axis_index(PCOL).astype(jnp.int32)
    y_idx, core_idx = lax.axis_index("y"), lax.axis_index("core")
    ids = jnp.stack([prow_idx, pcol_idx, y_idx, core_idx]).astype(jnp.int32)
    rows, ir, ic = call(
        pack_kernel,
        (shape(NP, 10, RD), shape(8, NB, dtype=jnp.int32), shape(NB, 8, dtype=jnp.int32)),
        ids, pivots, pivots.T, matrix, flops=2 * 10**9,
    )
    part = RD // 8
    panel, rows = lax.optimization_barrier((matrix[:, :NB], rows))
    piece = jnp.where(y_idx == 0, panel[:part], F32(0.0))
    for k in AROUND:
        piece = piece + lax.ppermute(panel[part * k : part * (k + 1)], "y", [(0, k)])
    raw = lax.all_gather(piece, PCOL, tiled=True).reshape(8, 2, part, NB)
    rows_in = lax.all_to_all(rows.reshape(NP, 5, 2, RD), PROW, 0, 0)
    old_in = rows_in[:2, :4].reshape(2, 8, RD)
    ext_in = rows_in[:, 4].reshape(2 * NP, RD)
    send = call(
        turn_kernel, shape(8, 24, RD), ids, ir, ic, ext_in, old_in[0], old_in[1], flops=10**8
    )
    main_z = lax.all_to_all(send, "z", 0, 0)
    main_send, side = call(mid_kernel, (shape(4, 144, RD), shape(192, NB)), None, main_z)
    main_x = lax.all_to_all(main_send, "x", 0, 0)
    parts = [lax.ppermute(side, "y", [(0, k)]) for k in AROUND]
    side_send = call(
        side_kernel, shape(4, 144, NB), ids, side, *parts, scratch=[pltpu.VMEM((192, NB), F32)]
    )
    side_send, main_x, raw = lax.optimization_barrier((side_send, main_x, raw))
    mine = lax.all_to_all(side_send, "x", 0, 0)
    base, put, new0, new1, u0 = call(
        main_kernel,
        (shape(RD, RD), shape(RD, 2 * NP), shape(NB, RD), shape(NB, RD), shape(NB, RD)),
        ids, ir, ic, matrix, main_x, lower_inv, flops=5 * 10**9,
    )
    there = lax.ppermute(mine, "core", [(0, 1), (1, 0)])
    return call(
        final_kernel, shape(RD, RD), ids, ic, raw, mine, there, base, put, new0, new1, u0,
        lower_inv, upper_inv, scratch=[pltpu.VMEM((NB, 6 * NB), BF16), pltpu.VMEM((6 * NB, RD), BF16)],
        flops=6 * 10**9,
    )


def broadcast(value, axis, root):
    mine = lax.axis_index(axis) == root
    return lax.psum(jnp.where(mine, value, jnp.zeros_like(value)), axis)


def general(matrix, pivots, lower_inv, upper_inv):
    current = matrix
    rows_dev = current.shape[0]
    cols_dev = current.shape[1]
    panel_width = pivots.shape[1]
    prow_idx = lax.axis_index(PROW)
    pcol_idx = lax.axis_index(PCOL)
    row_pos = jnp.arange(rows_dev)
    col_pos = jnp.arange(cols_dev)
    row_done = jnp.zeros((rows_dev,), bool)
    col_done = jnp.zeros((cols_dev,), bool)
    for panel_no in range(2):
        row_done = row_done | (prow_idx == panel_no) & (row_pos < panel_width)
        col_done = col_done | (pcol_idx == panel_no) & (col_pos < panel_width)
        pivot_list = pivots[panel_no]
        owner_row = pivot_list // rows_dev
        local_row = pivot_list % rows_dev
        is_owned = owner_row == prow_idx
        on_root = prow_idx == panel_no
        old_block = broadcast(current[:panel_width], PROW, panel_no)
        pivot_data = jnp.where(is_owned[:, None], current[local_row], F32(0.0))
        new_rows = lax.psum(pivot_data, PROW)
        upper_rows = hdot(lower_inv[panel_no], new_rows)
        row_block = jnp.where(col_done[None, :], new_rows, upper_rows)
        target = jnp.where(is_owned, local_row, rows_dev)
        current = current.at[target].set(old_block, mode="drop")
        current = current.at[:panel_width].set(jnp.where(on_root, row_block, current[:panel_width]))
        lower_here = hdot(current[:, :panel_width], upper_inv[panel_no])
        lower_cols = broadcast(lower_here, PCOL, panel_no)
        rank_update = hdot(lower_cols, row_block)
        keep_mask = (~row_done)[:, None] & (~col_done)[None, :]
        current = jnp.where(keep_mask, current - rank_update, current)
        panel_mask = (pcol_idx == panel_no) & (~row_done)[:, None]
        current = current.at[:, :panel_width].set(
            jnp.where(panel_mask, lower_cols, current[:, :panel_width])
        )
    return current


def local(matrix, pivots, lower_inv, upper_inv):
    rows = jnp.arange(NB, dtype=jnp.int32)
    moves = jnp.stack([pivots[0] != rows, pivots[1] != rows + RD])
    owners = jnp.where(moves, pivots // RD, NP)
    counts = jnp.sum(owners.reshape(-1, 1) == jnp.arange(NP)[None, :], axis=0)
    fits = jnp.max(counts) <= NP
    def body(state):
        out = general(with_layout_constraint(matrix, ROW_MAJOR), pivots, lower_inv, upper_inv)
        return jnp.zeros((), bool), with_layout_constraint(out, ROW_MAJOR)

    quick = fast(matrix, pivots, lower_inv, upper_inv)
    return lax.while_loop(lambda state: state[0], body, (~fits, quick))[1]


def solution(mesh):
    grid = Mesh(mesh.devices.reshape(8, 4, 8, 2), ("z", "x", "y", "core"))
    in_specs = (P(PROW, PCOL), P(), P(), P())
    return jax.shard_map(local, mesh=grid, in_specs=in_specs, out_specs=P(PROW, PCOL), check_vma=False)
```

profile of v0, /device:TPU:1, one launch (start us, length us, event | category | flops | bytes accessed | tf_op | source)
XLA Modules:
  0.0 144.4 jit_solution(1734077376207346234)
XLA Ops:
  7.3 1.2 slice.159
  8.6 4.1 %shard_map.46 = (f32[32,10,768]{2,1,0:T(8,128)S(1)}, s32[8,256]{1,0:T(8,128)S(1)}, s32[256,8]{1,0:T(8,128)S(1)}) custom-call(s32[4]{0:T(128)S(1)} %pad_add_fusion.ids, s32[2,256]{1,0:T(2,128)} %pr_ref.1, s32[256,2]{1,0:T(8,128)S(1)} %bitcast.84, f32[768,768]{1,0:T(8,128)} %a_ref.3), custom_call_target="tpu_custom_call" | custom-call | flops 2000000000 | bytes 3362816 | tf_op jit(solution)/shard_map/pallas_call | solution.py:309
  13.3 1.7 %copy.22 = f32[32,5,2,768]{3,2,1,0:T(2,128)} copy(f32[32,5,2,768]{3,0,2,1:T(8,128)S(1)} %bitcast.86) | data formatting | bytes 1966080 | tf_op jit(solution)/shard_map/reshape | solution.py:343
  15.0 13.7 %all-to-all-start = ((f32[32,5,2,768]{3,2,1,0:T(2,128)}), f32[32,5,2,768]{3,2,1,0:T(2,128)S(1)}, u32[]{:S(2)}, u32[]{:S(2)}) async-start(f32[32,5,2,768]{3,2,1,0:T(2,128)} %copy.22), calls=%async_computation | async-start | bytes 1966080 | tf_op jit(solution)/shard_map/all_to_all | solution.py:343
  28.8 4.2 %collective-permute-start.10 = (f32[96,256]{1,0:T(8,128)S(1)}, f32[96,256]{1,0:T(8,128)S(1)}, u32[]{:S(2)}, u32[]{:S(2)}) collective-permute-start(f32[96,256]{1,0:T(8,128)S(1)} %get-tuple-element.156), channel_id=1, source_target_pairs={{0,4},{1,5},{16,20},{17,21},{32,36},{33,37},{48,52},{49,53},{64,68... | collective-permute-start | bytes 294920 | tf_op jit(solution)/shard_map/ppermute | solution.py:341
  33.1 2.3 %collective-permute-start.11 = (f32[96,256]{1,0:T(8,128)S(1)}, f32[96,256]{1,0:T(8,128)S(1)}, u32[]{:S(2)}, u32[]{:S(2)}) collective-permute-start(f32[96,256]{1,0:T(8,128)S(1)} %get-tuple-element.155), channel_id=1, source_target_pairs={{0,12},{1,13},{16,28},{17,29},{32,44},{33,45},{48,60},{49,61},{64,... | collective-permute-start | bytes 294920 | tf_op jit(solution)/shard_map/ppermute | solution.py:341
  35.4 1.3 collective-permute-start.12
  36.7 1.3 collective-permute-start.13
  38.0 1.3 collective-permute-start.7
  39.3 1.3 collective-permute-start.8
  40.6 1.3 collective-permute-start.9
  42.0 1.1 collective-permute-done.8
  44.3 9.3 %all-to-all-done = f32[32,5,2,768]{3,2,1,0:T(2,128)S(1)} async-done(((f32[32,5,2,768]{3,2,1,0:T(2,128)}), f32[32,5,2,768]{3,2,1,0:T(2,128)S(1)}, u32[]{:S(2)}, u32[]{:S(2)}) %all-to-all-start) | async-done | bytes 983072 | tf_op jit(solution)/shard_map/all_to_all | solution.py:343
  53.8 1.1 shard_map.47
  54.9 19.5 %all_to_all.20.in_ref = f32[8,24,768]{2,1,0:T(8,128)S(1)} all-to-all(f32[8,24,768]{2,1,0:T(8,128)S(1)} %shard_map.47), channel_id=1, replica_groups=mesh['z'=8,'x'=4,'y'=8,'core'=2] {'z'}, dimensions={0} | all-to-all | bytes 1179648 | tf_op jit(solution)/shard_map/all_to_all | solution.py:349
  74.4 1.4 shard_map.48
  75.8 4.4 %all-to-all-start.2 = ((f32[4,144,768]{2,1,0:T(8,128)}), f32[4,144,768]{2,1,0:T(8,128)S(1)}, u32[]{:S(2)}, u32[]{:S(2)}) async-start(f32[4,144,768]{2,1,0:T(8,128)} %get-tuple-element.103), calls=%async_computation.2 | async-start | bytes 3538944 | tf_op jit(solution)/shard_map/all_to_all | solution.py:351
  80.1 7.6 %collective-permute-start = (f32[192,256]{1,0:T(8,128)S(1)}, f32[192,256]{1,0:T(8,128)S(1)}, u32[]{:S(2)}, u32[]{:S(2)}) collective-permute-start(f32[192,256]{1,0:T(8,128)S(1)} %get-tuple-element.102.refs_0_), channel_id=1, source_target_pairs={{0,8},{1,9},{16,24},{17,25},{32,40},{33,41},{48,56},{49,57},{64,72... | collective-permute-start | bytes 589832 | tf_op jit(solution)/shard_map/ppermute | solution.py:352
  87.7 1.3 collective-permute-start.1
  89.0 1.3 collective-permute-start.2
  90.3 1.3 collective-permute-start.3
  91.6 1.3 collective-permute-start.4
  92.9 1.3 collective-permute-start.5
  94.3 1.3 collective-permute-start.6
  95.6 1.3 collective-permute-done.3.refs_4_
  96.9 4.2 %collective-permute-done.5.refs_6_ = f32[192,256]{1,0:T(8,128)S(1)} collective-permute-done((f32[192,256]{1,0:T(8,128)S(1)}, f32[192,256]{1,0:T(8,128)S(1)}, u32[]{:S(2)}, u32[]{:S(2)}) %collective-permute-start.5) | collective-permute-done | bytes 196640 | tf_op jit(solution)/shard_map/ppermute | solution.py:352
  101.1 1.5 %shard_map.49 = f32[4,144,256]{2,1,0:T(8,128)} custom-call(s32[4]{0:T(128)S(1)} %pad_add_fusion.ids, f32[192,256]{1,0:T(8,128)S(1)} %get-tuple-element.102.refs_0_, f32[192,256]{1,0:T(8,128)S(1)} %collective-permute-done.refs_1_, f32[192,256]{1,0:T(8,128)S(1)} %collective-permute-done.1.refs_2_, f32[192,256]{1,0:T(8,128)S(1)} %collective-permute-done.2.refs_3_, ...), custom_call_target="tpu_custom_call" | custom-call | bytes 2162688 | tf_op jit(solution)/shard_map/pallas_call | solution.py:309
  102.6 4.0 %all-to-all-start.3 = ((f32[4,144,256]{2,1,0:T(8,128)}), f32[4,144,256]{2,1,0:T(8,128)S(1)}, u32[]{:S(2)}, u32[]{:S(2)}) async-start(f32[4,144,256]{2,1,0:T(8,128)} %shard_map.49), calls=%async_computation.3 | async-start | bytes 1179648 | tf_op jit(solution)/shard_map/all_to_all | solution.py:357
  106.6 7.3 %all-to-all-done.3.mine_ref = f32[4,144,256]{2,1,0:T(8,128)S(1)} async-done(((f32[4,144,256]{2,1,0:T(8,128)}), f32[4,144,256]{2,1,0:T(8,128)S(1)}, u32[]{:S(2)}, u32[]{:S(2)}) %all-to-all-start.3) | async-done | bytes 589856 | tf_op jit(solution)/shard_map/all_to_all | solution.py:357
  113.9 8.3 %collective-permute-start.14 = (f32[4,144,256]{2,1,0:T(8,128)S(1)}, f32[4,144,256]{2,1,0:T(8,128)S(1)}, u32[]{:S(2)}, u32[]{:S(2)}) collective-permute-start(f32[4,144,256]{2,1,0:T(8,128)S(1)} %all-to-all-done.3.mine_ref), channel_id=1, source_target_pairs={{0,1},{1,0},{2,3},{3,2},{4,5},{5,4},{6,7},{7,6},{8,9},{9,8},{10,11... | collective-permute-start | bytes 1769480 | tf_op jit(solution)/shard_map/ppermute | solution.py:363
  123.7 4.9 %shard_map.50 = (f32[768,768]{1,0:T(8,128)S(1)}, f32[768,64]{1,0:T(8,128)S(1)}, f32[256,768]{1,0:T(8,128)S(1)}, f32[256,768]{1,0:T(8,128)S(1)}, f32[256,768]{1,0:T(8,128)S(1)}) custom-call(s32[4]{0:T(128)S(1)} %pad_add_fusion.ids, s32[8,256]{1,0:T(8,128)S(1)} %get-tuple-element.99.ir_ref, s32[256,8]{1,0:T(8,128)S(1)} %get-tuple-element.98.ic_ref, ...), custom_call_target="tpu_custom_call" | custom-call | flops 5000000000 | bytes 9584640 | tf_op jit(solution)/shard_map/pallas_call | solution.py:309
  128.6 8.9 %shard_map.51 = f32[768,768]{1,0:T(8,128)} custom-call(s32[4]{0:T(128)S(1)} %pad_add_fusion.ids, s32[256,8]{1,0:T(8,128)S(1)} %get-tuple-element.98.ic_ref, f32[8,2,96,256]{3,2,1,0:T(8,128)S(1)} %bitcast.85, f32[4,144,256]{2,1,0:T(8,128)S(1)} %all-to-all-done.3.mine_ref, f32[4,144,256]{2,1,0:T(8,128)S(1)} %collective-permute-done.14.there_ref, ...), custom_call_target="tpu_custom_call" | custom-call | flops 6000000000 | bytes 11083776 | tf_op jit(solution)/shard_map/pallas_call | solution.py:309
  (40 shorter events, 3.7 us)
Async XLA Ops:
  15.0 38.5 %all-to-all-start = ((f32[32,5,2,768]{3,2,1,0:T(2,128)}), f32[32,5,2,768]{3,2,1,0:T(2,128)S(1)}, u32[]{:S(2)}, u32[]{:S(2)}) async-start(f32[32,5,2,768]{3,2,1,0:T(2,128)} %copy.22), calls=%async_computation | async-start | bytes 1966080 | tf_op jit(solution)/shard_map/all_to_all | solution.py:343
  28.7 73.9 %all-gather.2.cloned.1.call-start = ((), (), s32[]{:S(2)}) async-start(), calls=%async_computation.8 | async-start | bytes 1671168 | tf_op jit(solution)/shard_map/all_gather | solution.py:342
  28.8 10.5 %collective-permute-start.10 = (f32[96,256]{1,0:T(8,128)S(1)}, f32[96,256]{1,0:T(8,128)S(1)}, u32[]{:S(2)}, u32[]{:S(2)}) collective-permute-start(f32[96,256]{1,0:T(8,128)S(1)} %get-tuple-element.156), channel_id=1, source_target_pairs={{0,4},{1,5},{16,20},{17,21},{32,36},{33,37},{48,52},{49,53},{64,68... | collective-permute-start | bytes 294920 | tf_op jit(solution)/shard_map/ppermute | solution.py:341
  33.1 7.6 %collective-permute-start.11 = (f32[96,256]{1,0:T(8,128)S(1)}, f32[96,256]{1,0:T(8,128)S(1)}, u32[]{:S(2)}, u32[]{:S(2)}) collective-permute-start(f32[96,256]{1,0:T(8,128)S(1)} %get-tuple-element.155), channel_id=1, source_target_pairs={{0,12},{1,13},{16,28},{17,29},{32,44},{33,45},{48,60},{49,61},{64,... | collective-permute-start | bytes 294920 | tf_op jit(solution)/shard_map/ppermute | solution.py:341
  35.4 6.5 %collective-permute-start.12 = (f32[96,256]{1,0:T(8,128)S(1)}, f32[96,256]{1,0:T(8,128)S(1)}, u32[]{:S(2)}, u32[]{:S(2)}) collective-permute-start(f32[96,256]{1,0:T(8,128)S(1)} %get-tuple-element.154), channel_id=1, source_target_pairs={{0,2},{1,3},{16,18},{17,19},{32,34},{33,35},{48,50},{49,51},{64,66... | collective-permute-start | bytes 294920 | tf_op jit(solution)/shard_map/ppermute | solution.py:341
  36.7 5.3 %collective-permute-start.13 = (f32[96,256]{1,0:T(8,128)S(1)}, f32[96,256]{1,0:T(8,128)S(1)}, u32[]{:S(2)}, u32[]{:S(2)}) collective-permute-start(f32[96,256]{1,0:T(8,128)S(1)} %get-tuple-element.153), channel_id=1, source_target_pairs={{0,14},{1,15},{16,30},{17,31},{32,46},{33,47},{48,62},{49,63},{64,... | collective-permute-start | bytes 294920 | tf_op jit(solution)/shard_map/ppermute | solution.py:341
  38.0 4.0 %collective-permute-start.7 = (f32[96,256]{1,0:T(8,128)S(1)}, f32[96,256]{1,0:T(8,128)S(1)}, u32[]{:S(2)}, u32[]{:S(2)}) collective-permute-start(f32[96,256]{1,0:T(8,128)S(1)} %get-tuple-element.152), channel_id=1, source_target_pairs={{0,8},{1,9},{16,24},{17,25},{32,40},{33,41},{48,56},{49,57},{64,72... | collective-permute-start | bytes 294920 | tf_op jit(solution)/shard_map/ppermute | solution.py:341
  39.3 3.8 %collective-permute-start.8 = (f32[96,256]{1,0:T(8,128)S(1)}, f32[96,256]{1,0:T(8,128)S(1)}, u32[]{:S(2)}, u32[]{:S(2)}) collective-permute-start(f32[96,256]{1,0:T(8,128)S(1)} %get-tuple-element.158), channel_id=1, source_target_pairs={{0,6},{1,7},{16,22},{17,23},{32,38},{33,39},{48,54},{49,55},{64,70... | collective-permute-start | bytes 294920 | tf_op jit(solution)/shard_map/ppermute | solution.py:341
  40.6 2.9 %collective-permute-start.9 = (f32[96,256]{1,0:T(8,128)S(1)}, f32[96,256]{1,0:T(8,128)S(1)}, u32[]{:S(2)}, u32[]{:S(2)}) collective-permute-start(f32[96,256]{1,0:T(8,128)S(1)} %get-tuple-element.157), channel_id=1, source_target_pairs={{0,10},{1,11},{16,26},{17,27},{32,42},{33,43},{48,58},{49,59},{64,... | collective-permute-start | bytes 294920 | tf_op jit(solution)/shard_map/ppermute | solution.py:341
  75.8 26.9 %all-to-all-start.2 = ((f32[4,144,768]{2,1,0:T(8,128)}), f32[4,144,768]{2,1,0:T(8,128)S(1)}, u32[]{:S(2)}, u32[]{:S(2)}) async-start(f32[4,144,768]{2,1,0:T(8,128)} %get-tuple-element.103), calls=%async_computation.2 | async-start | bytes 3538944 | tf_op jit(solution)/shard_map/all_to_all | solution.py:351
  80.1 26.5 %copy-start.11 = (s32[2,256]{1,0:T(2,128)S(1)}, s32[2,256]{1,0:T(2,128)}, u32[]{:S(2)}) copy-start(s32[2,256]{1,0:T(2,128)} %pr_ref.1) | copy-start | bytes 6148
  80.1 12.8 %collective-permute-start = (f32[192,256]{1,0:T(8,128)S(1)}, f32[192,256]{1,0:T(8,128)S(1)}, u32[]{:S(2)}, u32[]{:S(2)}) collective-permute-start(f32[192,256]{1,0:T(8,128)S(1)} %get-tuple-element.102.refs_0_), channel_id=1, source_target_pairs={{0,8},{1,9},{16,24},{17,25},{32,40},{33,41},{48,56},{49,57},{64,72... | collective-permute-start | bytes 589832 | tf_op jit(solution)/shard_map/ppermute | solution.py:352
  87.7 6.6 %collective-permute-start.1 = (f32[192,256]{1,0:T(8,128)S(1)}, f32[192,256]{1,0:T(8,128)S(1)}, u32[]{:S(2)}, u32[]{:S(2)}) collective-permute-start(f32[192,256]{1,0:T(8,128)S(1)} %get-tuple-element.102.refs_0_), channel_id=1, source_target_pairs={{0,6},{1,7},{16,22},{17,23},{32,38},{33,39},{48,54},{49,55},{64,70... | collective-permute-start | bytes 589832 | tf_op jit(solution)/shard_map/ppermute | solution.py:352
  89.0 6.6 %collective-permute-start.2 = (f32[192,256]{1,0:T(8,128)S(1)}, f32[192,256]{1,0:T(8,128)S(1)}, u32[]{:S(2)}, u32[]{:S(2)}) collective-permute-start(f32[192,256]{1,0:T(8,128)S(1)} %get-tuple-element.102.refs_0_), channel_id=1, source_target_pairs={{0,10},{1,11},{16,26},{17,27},{32,42},{33,43},{48,58},{49,59},{64,... | collective-permute-start | bytes 589832 | tf_op jit(solution)/shard_map/ppermute | solution.py:352
  90.3 6.6 %collective-permute-start.3 = (f32[192,256]{1,0:T(8,128)S(1)}, f32[192,256]{1,0:T(8,128)S(1)}, u32[]{:S(2)}, u32[]{:S(2)}) collective-permute-start(f32[192,256]{1,0:T(8,128)S(1)} %get-tuple-element.102.refs_0_), channel_id=1, source_target_pairs={{0,4},{1,5},{16,20},{17,21},{32,36},{33,37},{48,52},{49,53},{64,68... | collective-permute-start | bytes 589832 | tf_op jit(solution)/shard_map/ppermute | solution.py:352
  91.6 5.3 %collective-permute-start.4 = (f32[192,256]{1,0:T(8,128)S(1)}, f32[192,256]{1,0:T(8,128)S(1)}, u32[]{:S(2)}, u32[]{:S(2)}) collective-permute-start(f32[192,256]{1,0:T(8,128)S(1)} %get-tuple-element.102.refs_0_), channel_id=1, source_target_pairs={{0,12},{1,13},{16,28},{17,29},{32,44},{33,45},{48,60},{49,61},{64,... | collective-permute-start | bytes 589832 | tf_op jit(solution)/shard_map/ppermute | solution.py:352
  92.9 8.2 %collective-permute-start.5 = (f32[192,256]{1,0:T(8,128)S(1)}, f32[192,256]{1,0:T(8,128)S(1)}, u32[]{:S(2)}, u32[]{:S(2)}) collective-permute-start(f32[192,256]{1,0:T(8,128)S(1)} %get-tuple-element.102.refs_0_), channel_id=1, source_target_pairs={{0,2},{1,3},{16,18},{17,19},{32,34},{33,35},{48,50},{49,51},{64,66... | collective-permute-start | bytes 589832 | tf_op jit(solution)/shard_map/ppermute | solution.py:352
  94.3 6.8 %collective-permute-start.6 = (f32[192,256]{1,0:T(8,128)S(1)}, f32[192,256]{1,0:T(8,128)S(1)}, u32[]{:S(2)}, u32[]{:S(2)}) collective-permute-start(f32[192,256]{1,0:T(8,128)S(1)} %get-tuple-element.102.refs_0_), channel_id=1, source_target_pairs={{0,14},{1,15},{16,30},{17,31},{32,46},{33,47},{48,62},{49,63},{64,... | collective-permute-start | bytes 589832 | tf_op jit(solution)/shard_map/ppermute | solution.py:352
  102.6 11.2 %all-to-all-start.3 = ((f32[4,144,256]{2,1,0:T(8,128)}), f32[4,144,256]{2,1,0:T(8,128)S(1)}, u32[]{:S(2)}, u32[]{:S(2)}) async-start(f32[4,144,256]{2,1,0:T(8,128)} %shard_map.49), calls=%async_computation.3 | async-start | bytes 1179648 | tf_op jit(solution)/shard_map/all_to_all | solution.py:357
  113.9 14.7 %collective-permute-start.14 = (f32[4,144,256]{2,1,0:T(8,128)S(1)}, f32[4,144,256]{2,1,0:T(8,128)S(1)}, u32[]{:S(2)}, u32[]{:S(2)}) collective-permute-start(f32[4,144,256]{2,1,0:T(8,128)S(1)} %all-to-all-done.3.mine_ref), channel_id=1, source_target_pairs={{0,1},{1,0},{2,3},{3,2},{4,5},{5,4},{6,7},{7,6},{8,9},{9,8},{10,11... | collective-permute-start | bytes 1769480 | tf_op jit(solution)/shard_map/ppermute | solution.py:363
  123.7 4.9 %copy-start = (f32[1536,256]{1,0:T(8,128)S(1)}, f32[1536,256]{1,0:T(8,128)}, u32[]{:S(2)}) copy-start(f32[1536,256]{1,0:T(8,128)} %all-gather.2.cloned.1.call-done) | copy-start | bytes 4718596
  123.7 4.9 %copy-start.4 = (f32[2,256,256]{2,1,0:T(8,128)S(1)}, f32[2,256,256]{2,1,0:T(8,128)}, u32[]{:S(2)}) copy-start(f32[2,256,256]{2,1,0:T(8,128)} %ui_ref.1) | copy-start | bytes 1572868
  123.7 4.9 %copy-start.8 = (f32[2,256,256]{2,1,0:T(8,128)S(1)}, f32[2,256,256]{2,1,0:T(8,128)}, u32[]{:S(2)}) copy-start(f32[2,256,256]{2,1,0:T(8,128)} %li_ref.3) | copy-start | bytes 1572868
Sparse Core Ops, SparseCore 0:
  44.4 43.8 all-gather.1
where the time goes:
time: 145 us; the launch traced here: 144 us
  starting transfers between devices  58.8 us (41%)
  waiting for transfers between devices  23.7 us (16%)
  Pallas kernels  21.9 us (15%)
  blocking collectives  19.5 us (13%)
  between operations  14.4 us (10%)
  local copies, waits for them, and re-layouts  4.56 us (3%)
  other arithmetic  1.55 us (1%)
    pallas_call x6, Pallas kernels, call(): pl.pallas_call(kernel, out_shape=outs, in_specs=smem + [vmem] * len(args)...  21.9 us
    all_to_all x1, blocking collectives, fast(): main_z = lax.all_to_all(send, 'z', 0, 0)  19.5 us
    ppermute x7, starting transfers between devices, fast(): parts = [lax.ppermute(side, 'y', [(0, k)]) for k in AROUND]  15.4 us
    all_to_all x1, starting transfers between devices, fast(): rows_in = lax.all_to_all(rows.reshape(NP, 5, 2, RD), PROW, 0, 0)  13.7 us
    ppermute x7, starting transfers between devices, fast(): piece = piece + lax.ppermute(panel[part * k:part * (k + 1)], 'y', [(0, k)])  13 us
    all_to_all x1, waiting for transfers between devices, fast(): rows_in = lax.all_to_all(rows.reshape(NP, 5, 2, RD), PROW, 0, 0)  9.26 us
    ppermute x1, starting transfers between devices, fast(): there = lax.ppermute(mine, 'core', [(0, 1), (1, 0)])  8.35 us
    all_to_all x1, waiting for transfers between devices, fast(): mine = lax.all_to_all(side_send, 'x', 0, 0)  7.27 us
  transfers between devices with their start and end apart: 19, of which 6 were waited for; matrix products, arithmetic and copies ran while one was open for 1% of the time, Pallas kernels for 6%

commit v1 on v0

--- a/solution.py
+++ b/solution.py
@@ -49,7 +49,7 @@
 
 def index_math(pr, pc):
     p0r, p1r = pr[0:1, :], pr[1:2, :]
-    p0c, p1c = pc[:, 0:1], pc[:, 1:2]
+    p0c, p1c = pc
     sub, lane = iota((NB, NB), 0), iota((NB, NB), 1)
     lr, lc = iota((1, NB), 1), iota((NB, 1), 0)
     m_kj = f(p0c == lane + RD)
@@ -130,14 +130,22 @@
     return bdot(p, hi) + (bdot(p, mid) + bdot(p, low))
 
 
-def pack_kernel(ids, pr_ref, pc_ref, a_ref, send_ref, ir_ref, ic_ref):
+def pack_kernel(ids, p_ref, a_ref, send_ref, ir_ref, ic_ref, most_ref, *piece_refs):
     me = ids[0]
-    rows, cols = index_math(pr_ref[...], pc_ref[...])
+    for n, r in enumerate(piece_refs):
+        rows_n = r.shape[0]
+        r[...] = a_ref[rows_n * n : rows_n * (n + 1), 0:NB]
+    pr = p_ref[...]
+    eye = iota((NB, NB), 0) == iota((NB, NB), 1)
+    turned = [sum_cols(jnp.where(eye, pr[n : n + 1, :].astype(F32), F32(0.0))) for n in range(2)]
+    rows, cols = index_math(pr, [t.astype(jnp.int32) for t in turned])
     for n, v in enumerate(rows):
         ir_ref[n : n + 1, :] = v
     ir_ref[6:8, :] = jnp.zeros((2, NB), jnp.int32)
     for n, v in enumerate(cols):
         ic_ref[:, n : n + 1] = v
+    counts = [sum_rows(f(cols[3 * g + 1] == iota((NB, NP), 1))) for g in range(2)]
+    most_ref[0] = jnp.max(jnp.maximum(counts[0], counts[1])).astype(jnp.int32)
     line = iota((NB, NB), 0)
     rank = jnp.where(me == 1, rows[3], rows[0])
     perm = f(rank == (line >> 3) + NP * (line & 7))
@@ -151,12 +159,18 @@
         pick = pick + bdot(s.astype(BF16), t.astype(BF16))
     ext = pick3(pick, a_ref[...])
     for m in range(NP):
-        send_ref[m, 0:8, :] = old[8 * m : 8 * m + 8]
-        send_ref[m, 8:10, :] = ext[2 * m : 2 * m + 2]
-
-
-def turn_kernel(ids, ir_ref, ic_ref, ext_ref, old0_ref, old1_ref, send_ref):
+        for q in range(4):
+            send_ref[m, q] = old[8 * m + 2 * q : 8 * m + 2 * q + 2]
+        send_ref[m, 4] = ext[2 * m : 2 * m + 2]
+
+
+def turn_kernel(ids, ir_ref, ic_ref, in_ref, send_ref, side_ref, old_ref, ext_ref):
     me = ids[0]
+    for q in range(4):
+        old_ref[2 * q : 2 * q + 2, :] = in_ref[0, q]
+        old_ref[8 + 2 * q : 10 + 2 * q, :] = in_ref[1, q]
+    for m in range(NP):
+        ext_ref[2 * m : 2 * m + 2, :] = in_ref[m, 4]
     line = iota((16, NB), 0)
     want = me + NP * (line & 7)
     own = jnp.zeros((16, 1), F32)
@@ -164,7 +178,7 @@
         hit = f((ir_ref[3 * g : 3 * g + 1, :] == want) & ((line >> 3) == g))
         own = own + sum_cols(hit * ir_ref[3 * g + 1 : 3 * g + 2, :].astype(F32))
     own = own.astype(jnp.int32)
-    old = jnp.concatenate([old0_ref[...], old1_ref[...]], axis=0)
+    old = old_ref[...]
     lane = iota((16, 2 * NP), 1)
     pick = f((own == (lane >> 1)) & ((iota((16, 2 * NP), 0) >> 3) == (lane & 1)))
     slots = jnp.where(own == NP, old, pick3(pick, ext_ref[...]))
@@ -180,19 +194,8 @@
     for z in range(8):
         send_ref[z, 0:16, :] = slots
         send_ref[z, 16:24, :] = back[8 * z : 8 * z + 8]
-
-
-def arrange(get, out_ref):
-    for x in range(4):
-        for z in range(8):
-            out_ref[x, 16 * z : 16 * z + 16, :] = get(z, 0, 16)
-            out_ref[x, 128 + 2 * z : 130 + 2 * z, :] = get(z, 16 + 2 * x, 18 + 2 * x)
-
-
-def mid_kernel(in_ref, out_ref, side_ref):
-    arrange(lambda z, a, b: in_ref[z, a:b, :], out_ref)
-    for z in range(8):
-        side_ref[24 * z : 24 * z + 24, :] = in_ref[z, :, 0:NB]
+    side_ref[0:16, :] = slots[:, 0:NB]
+    side_ref[16:80, :] = back[:, 0:NB]
 
 
 def side_kernel(ids, *refs):
@@ -201,18 +204,35 @@
     for r in refs[1:8]:
         total = total + r[...]
     sums[...] = total
-    arrange(lambda z, a, b: sums[24 * z + a : 24 * z + b, :], out)
-
-
-def slots_of(ref):
-    return jnp.concatenate([ref[x, 0:128, :] for x in range(4)], axis=0)
-
-
-def back_of(ref):
-    return jnp.concatenate([ref[x, 128:144, :] for x in range(4)], axis=0)
-
-
-def main_kernel(ids, ir_ref, ic_ref, a_ref, x_ref, li_ref, base_ref, put_ref, new0_ref, new1_ref, u0_ref):
+    for m in range(NP):
+        for h in range(2):
+            cut = slice(128 * h, 128 * h + 128)
+            out[m, 16 * h : 16 * h + 16, :] = sums[0:16, cut]
+            out[m, 32 + 2 * h : 34 + 2 * h, :] = sums[16 + 2 * m : 18 + 2 * m, cut]
+        out[m, 36:40, :] = jnp.zeros((4, 128), F32)
+
+
+def mid_kernel(ids, in_ref, *out_refs):
+    for s, out_ref in enumerate(out_refs):
+        to = (ids[0] + s) & 3
+        for z in range(8):
+            out_ref[16 * z : 16 * z + 16, :] = in_ref[z, 0:16, :]
+            back = in_ref[z, 16:18, :]
+            for x in range(1, 4):
+                back = jnp.where(to == x, in_ref[z, 16 + 2 * x : 18 + 2 * x, :], back)
+            out_ref[128 + 2 * z : 130 + 2 * z, :] = back
+
+
+def pre_kernel(raw_ref, ui_ref, low0_ref, end1_ref):
+    for n, out in enumerate((low0_ref, end1_ref)):
+        raw = jnp.concatenate([raw_ref[y, n] for y in range(8)], axis=0)
+        out[...] = dot3(raw, ui_ref[n])
+
+
+def main_kernel(
+    ids, ir_ref, ic_ref, a_ref, x0_ref, x1_ref, x2_ref, x3_ref, low0_ref, li_ref,
+    base_ref, put_ref, back_ref, new0_ref, new1_ref, u0_ref,
+):
     me = ids[0]
     put = jnp.zeros((RD, 2 * NP), F32)
     lane = iota((NB, 2 * NP), 1)
@@ -223,63 +243,66 @@
         s = f(((ic_ref[:, 3 * g : 3 * g + 1] & 31) == m) & ((lane & 1) == g))
         put = put + bdot(t.astype(BF16), s.astype(BF16))
     put_ref[...] = put
-    x = slots_of(x_ref)
-    new = []
-    for n in range(2):
-        new.append(pick3(f(ic_ref[:, 6 + n : 7 + n] == iota((NB, 2 * NB), 1)), x))
-    new0_ref[...], new1_ref[...] = new
-    u0_ref[...] = dot3(li_ref[0], new[0])
-    back = back_of(x_ref)
+    blocks = (x0_ref, x1_ref, x2_ref, x3_ref)
+    slots = jnp.concatenate([r[0:128, :] for r in blocks], axis=0)
+    for x in range(4):
+        s = (me - x) & 3
+        back = blocks[0][128:144, :]
+        for k in range(1, 4):
+            back = jnp.where(s == k, blocks[k][128:144, :], back)
+        back_ref[16 * x : 16 * x + 16, :] = back
+    lane = iota((NB, 2 * NB), 1)
+    slot = ((me - (lane >> 7)) & 3) * 128 + (lane & 127)
+    new0 = pick3(f(ic_ref[:, 6:7] == slot), slots)
+    new1_ref[...] = pick3(f(ic_ref[:, 7:8] == slot), slots)
+    new0_ref[...] = new0[:, 0:NB]
+    u0 = dot3(li_ref[0], new0)
+    u0_ref[...] = u0
     for r in range(3):
-        part = put[NB * r : NB * r + NB]
         rows = pl.ds(NB * r, NB)
-        base_ref[rows, :] = jnp.where(sum_cols(part) > 0, pick3(part, back), a_ref[rows, :])
+        base_ref[rows, :] = a_ref[rows, :] - dot3(low0_ref[rows, :], u0)
 
 
 def final_kernel(
-    ids, ic_ref, raw_ref, mine_ref, there_ref, base_ref, put_ref, new0_ref, new1_ref, u0_ref,
-    li_ref, ui_ref, out_ref, low_ref, up_ref,
+    ids, ic_ref, mine_ref, there_ref, base_ref, put_ref, back_ref, new0_ref, new1_ref, u0_ref,
+    low0_ref, end1_ref, li_ref, ui_ref, out_ref, slots_ref, rows_ref,
 ):
     me, col, core = ids[0], ids[1], ids[3]
-    mine, there = mine_ref[...], there_ref[...]
-    s0 = jnp.where(core == 0, mine, there)
-    s1 = jnp.where(core == 0, there, mine)
-    slots0, slots1 = slots_of(s0), slots_of(s1)
-    back0, back1 = back_of(s0), back_of(s1)
+    for x in range(4):
+        for z in range(8):
+            m, n = 4 * z + x, 8 * x + z
+            mine, there = mine_ref[m], there_ref[m]
+            for k in range(2):
+                got = jnp.where(core == k, mine, there)
+                for h in range(2):
+                    cut = slice(128 * h, 128 * h + 128)
+                    slots_ref[k, 16 * n : 16 * n + 16, cut] = got[16 * h : 16 * h + 16]
+                    rows_ref[k, 2 * n : 2 * n + 2, cut] = got[32 + 2 * h : 34 + 2 * h]
+    u0 = u0_ref[...]
     perm0 = f(ic_ref[:, 6:7] == iota((NB, 2 * NB), 1))
     perm1 = f(ic_ref[:, 7:8] == iota((NB, 2 * NB), 1))
-    u0 = u0_ref[...]
-    u0c1 = dot3(li_ref[0], pick2(perm0, slots1))
-    diag = dot3(pick2(perm1, slots0), ui_ref[0])
+    diag = dot3(pick2(perm1, slots_ref[0]), ui_ref[0])
     next1 = new1_ref[...] - dot3(diag, u0)
     u1 = dot3(li_ref[1], next1)
-    for n, u in enumerate((u0, u1)):
-        hi, lo = halves(u)
-        for k, v in enumerate((hi, lo, hi)):
-            up_ref[NB * (3 * n + k) : NB * (3 * n + k + 1), :] = v
-    raw0 = jnp.concatenate([raw_ref[y, 0] for y in range(8)], axis=0)
-    raw1 = jnp.concatenate([raw_ref[y, 1] for y in range(8)], axis=0)
+    fill = dot3(dot3(li_ref[0], pick2(perm0, slots_ref[1])), ui_ref[1])
+    low0_back = dot3(rows_ref[0], ui_ref[0])
+    low1_back = dot3(rows_ref[1], ui_ref[1]) - dot3(low0_back, fill)
+    back = back_ref[...] - dot3(low0_back, u0) - dot3(low1_back, u1)
     for r in range(3):
         rows = pl.ds(NB * r, NB)
-        part = put_ref[rows, :]
-        moved = sum_cols(part) > 0
-        c0 = jnp.where(moved, pick2(part, back0), raw0[NB * r : NB * r + NB])
-        c1 = jnp.where(moved, pick2(part, back1), raw1[NB * r : NB * r + NB])
-        low0 = dot3(c0, ui_ref[0])
-        low1 = dot3(c1 - dot3(low0, u0c1), ui_ref[1])
-        for n, low in enumerate((low0, low1)):
-            hi, lo = halves(low)
-            for k, v in enumerate((hi, hi, lo)):
-                low_ref[:, NB * (3 * n + k) : NB * (3 * n + k + 1)] = v
-        out_ref[rows, :] = base_ref[rows, :] - bdot(low_ref[...], up_ref[...])
+        put = put_ref[rows, :]
+        moved = sum_cols(put) > 0
+        low0 = low0_ref[rows, :]
+        low1 = end1_ref[rows, :] - dot3(low0, fill)
+        out_ref[rows, :] = jnp.where(moved, pick2(put, back), base_ref[rows, :] - dot3(low1, u1))
 
         @pl.when(col == 0)
         def _():
-            out_ref[rows, 0:NB] = low0
+            out_ref[rows, 0:NB] = jnp.where(moved, pick2(put, low0_back), low0)
 
         @pl.when(col == 1)
         def _():
-            out_ref[rows, 0:NB] = low1
+            out_ref[rows, 0:NB] = jnp.where(moved, pick2(put, low1_back), low1)
 
     @pl.when(me == 0)
     def _():
@@ -287,7 +310,7 @@
 
         @pl.when(col == 0)
         def _():
-            out_ref[0:NB, 0:NB] = new0_ref[:, 0:NB]
+            out_ref[0:NB, 0:NB] = new0_ref[...]
 
     @pl.when(me == 1)
     def _():
@@ -302,18 +325,21 @@
             out_ref[0:NB, 0:NB] = next1[:, 0:NB]
 
 
+SCALAR = pl.BlockSpec(memory_space=pltpu.SMEM)
+
+
 def call(kernel, outs, ids, *args, scratch=(), flops=0):
     vmem = pl.BlockSpec(memory_space=pltpu.VMEM)
-    smem = [] if ids is None else [pl.BlockSpec(memory_space=pltpu.SMEM)]
+    smem = [] if ids is None else [SCALAR]
     sizes = [4 * o.size for o in jax.tree.leaves((outs, args))]
     return pl.pallas_call(
         kernel,
         out_shape=outs,
         in_specs=smem + [vmem] * len(args),
-        out_specs=jax.tree.map(lambda _: vmem, outs),
+        out_specs=jax.tree.map(lambda o: SCALAR if o.shape == (1,) else vmem, outs),
         scratch_shapes=scratch,
         compiler_params=pltpu.CompilerParams(vmem_limit_bytes=40 * 1024 * 1024),
-        cost_estimate=pl.CostEstimate(flops=flops, bytes_accessed=sum(sizes), transcendentals=0),
+        cost_estimate=pl.CostEstimate(flops=flops, bytes_accessed=min(sizes), transcendentals=0),
     )(*([] if ids is None else [ids]), *args)
 
 
@@ -329,43 +355,54 @@
     pcol_idx = lax.axis_index(PCOL).astype(jnp.int32)
     y_idx, core_idx = lax.axis_index("y"), lax.axis_index("core")
     ids = jnp.stack([prow_idx, pcol_idx, y_idx, core_idx]).astype(jnp.int32)
-    rows, ir, ic = call(
+    part = RD // 8
+    rows, ir, ic, most, *panel = call(
         pack_kernel,
-        (shape(NP, 10, RD), shape(8, NB, dtype=jnp.int32), shape(NB, 8, dtype=jnp.int32)),
-        ids, pivots, pivots.T, matrix, flops=2 * 10**9,
-    )
-    part = RD // 8
-    panel, rows = lax.optimization_barrier((matrix[:, :NB], rows))
-    piece = jnp.where(y_idx == 0, panel[:part], F32(0.0))
+        (
+            shape(NP, 5, 2, RD), shape(8, NB, dtype=jnp.int32), shape(NB, 8, dtype=jnp.int32),
+            shape(1, dtype=jnp.int32), *[shape(part, NB)] * 8,
+        ),
+        ids, pivots, matrix, flops=10**6,
+    )
+    rows_in = lax.all_to_all(rows, PROW, 0, 0)
+    piece = jnp.where(y_idx == 0, panel[0], F32(0.0))
     for k in AROUND:
-        piece = piece + lax.ppermute(panel[part * k : part * (k + 1)], "y", [(0, k)])
+        piece = piece + lax.ppermute(panel[k], "y", [(0, k)])
+    rows_in, piece = lax.optimization_barrier((rows_in, piece))
     raw = lax.all_gather(piece, PCOL, tiled=True).reshape(8, 2, part, NB)
-    rows_in = lax.all_to_all(rows.reshape(NP, 5, 2, RD), PROW, 0, 0)
-    old_in = rows_in[:2, :4].reshape(2, 8, RD)
-    ext_in = rows_in[:, 4].reshape(2 * NP, RD)
-    send = call(
-        turn_kernel, shape(8, 24, RD), ids, ir, ic, ext_in, old_in[0], old_in[1], flops=10**8
+    send, side = call(
+        turn_kernel, (shape(8, 24, RD), shape(80, NB)), ids, ir, ic, rows_in,
+        scratch=[pltpu.VMEM((16, RD), F32), pltpu.VMEM((2 * NP, RD), F32)], flops=10**6,
     )
     main_z = lax.all_to_all(send, "z", 0, 0)
-    main_send, side = call(mid_kernel, (shape(4, 144, RD), shape(192, NB)), None, main_z)
-    main_x = lax.all_to_all(main_send, "x", 0, 0)
     parts = [lax.ppermute(side, "y", [(0, k)]) for k in AROUND]
     side_send = call(
-        side_kernel, shape(4, 144, NB), ids, side, *parts, scratch=[pltpu.VMEM((192, NB), F32)]
-    )
-    side_send, main_x, raw = lax.optimization_barrier((side_send, main_x, raw))
-    mine = lax.all_to_all(side_send, "x", 0, 0)
-    base, put, new0, new1, u0 = call(
+        side_kernel, shape(NP, 40, 128), ids, side, *parts, scratch=[pltpu.VMEM((80, NB), F32)]
+    )
+    main_send = call(mid_kernel, [shape(144, RD)] * 4, ids, main_z)
+    side_send, main_send = lax.optimization_barrier((side_send, main_send))
+    mine = lax.all_to_all(side_send, PROW, 0, 0)
+    main_x = [main_send[0]] + [
+        lax.ppermute(main_send[k], "x", [(i, (i + k) % 4) for i in range(4)]) for k in range(1, 4)
+    ]
+    mine, main_x, raw = lax.optimization_barrier((mine, main_x, raw))
+    low0, end1 = call(pre_kernel, (shape(RD, NB), shape(RD, NB)), None, raw, upper_inv, flops=10**6)
+    base, put, back, new0, new1, u0 = call(
         main_kernel,
-        (shape(RD, RD), shape(RD, 2 * NP), shape(NB, RD), shape(NB, RD), shape(NB, RD)),
-        ids, ir, ic, matrix, main_x, lower_inv, flops=5 * 10**9,
+        (
+            shape(RD, RD), shape(RD, 2 * NP), shape(2 * NP, RD), shape(NB, NB), shape(NB, RD),
+            shape(NB, RD),
+        ),
+        ids, ir, ic, matrix, *main_x, low0, lower_inv, flops=10**6,
     )
     there = lax.ppermute(mine, "core", [(0, 1), (1, 0)])
-    return call(
-        final_kernel, shape(RD, RD), ids, ic, raw, mine, there, base, put, new0, new1, u0,
-        lower_inv, upper_inv, scratch=[pltpu.VMEM((NB, 6 * NB), BF16), pltpu.VMEM((6 * NB, RD), BF16)],
-        flops=6 * 10**9,
-    )
+    out = call(
+        final_kernel, shape(RD, RD), ids, ic, mine, there, base, put, back, new0, new1, u0,
+        low0, end1, lower_inv, upper_inv,
+        scratch=[pltpu.VMEM((2, 2 * NB, NB), F32), pltpu.VMEM((2, 2 * NP, NB), F32)],
+        flops=10**6,
+    )
+    return out, most[0]
 
 
 def broadcast(value, axis, root):
@@ -413,17 +450,12 @@
 
 
 def local(matrix, pivots, lower_inv, upper_inv):
-    rows = jnp.arange(NB, dtype=jnp.int32)
-    moves = jnp.stack([pivots[0] != rows, pivots[1] != rows + RD])
-    owners = jnp.where(moves, pivots // RD, NP)
-    counts = jnp.sum(owners.reshape(-1, 1) == jnp.arange(NP)[None, :], axis=0)
-    fits = jnp.max(counts) <= NP
     def body(state):
         out = general(with_layout_constraint(matrix, ROW_MAJOR), pivots, lower_inv, upper_inv)
         return jnp.zeros((), bool), with_layout_constraint(out, ROW_MAJOR)
 
-    quick = fast(matrix, pivots, lower_inv, upper_inv)
-    return lax.while_loop(lambda state: state[0], body, (~fits, quick))[1]
+    quick, most = fast(matrix, pivots, lower_inv, upper_inv)
+    return lax.while_loop(lambda state: state[0], body, (most > NP, quick))[1]
 
 
 def solution(mesh):

time: 145 us -> 144 us (level)
  blocking collectives: 19.5 us -> 0 us
  starting transfers between devices: 58.8 us -> 70.7 us
  waiting for transfers between devices: 23.7 us -> 32.4 us
  local copies, waits for them, and re-layouts: 4.56 us -> 1.66 us
  Pallas kernels: 21.9 us -> 23.5 us
    ppermute x7 -> x10, waiting for transfers between devices: 1.59 us -> 21.9 us  [the longest x3 20.3 us: fast(): lax.ppermute(main_send[k], 'x', [(i, (i + k) % 4) for i in range(4)])]
    all_to_all x1 -> x0, blocking collectives: 19.5 us -> none  [fast(): main_z = lax.all_to_all(send, 'z', 0, 0)]
    ppermute x7 -> x10, starting transfers between devices: 13 us -> 25.8 us  [the longest x7 15.2 us: fast(): piece = piece + lax.ppermute(panel[k], 'y', [(0, k)])]
    all_to_all x3, waiting for transfers between devices: 16.5 us -> 7.15 us  [the longest x1 7.15 us: fast(): rows_in = lax.all_to_all(rows, PROW, 0, 0)]
    all_to_all x3, starting transfers between devices: 22 us -> 28.2 us  [the longest x1 13.7 us: fast(): rows_in = lax.all_to_all(rows, PROW, 0, 0)]
    ppermute x1, starting transfers between devices: 8.35 us -> 3.86 us  [fast(): there = lax.ppermute(mine, 'core', [(0, 1), (1, 0)])]
    ppermute x7, starting transfers between devices: 15.4 us -> 12.8 us  [fast(): parts = [lax.ppermute(side, 'y', [(0, k)]) for k in AROUND]]
    ppermute x7, waiting for transfers between devices: 5.52 us -> 3.32 us  [fast(): parts = [lax.ppermute(side, 'y', [(0, k)]) for k in AROUND]]
  transfers between devices with their start and end apart: 19 -> 22, of which waited for: 6 -> 8; matrix products, arithmetic and copies ran while one was open for 1% -> 0% of each run, Pallas kernels for 6% -> 8%
where the time goes in v1:
time: 144 us; the launch traced here: 143 us
  starting transfers between devices  70.7 us (49%)
  waiting for transfers between devices  32.4 us (22%)
  Pallas kernels  23.5 us (16%)
  between operations  14.4 us (10%)
  local copies, waits for them, and re-layouts  1.66 us (1%)
    pallas_call x7, Pallas kernels, call(): pl.pallas_call(kernel, out_shape=outs, in_specs=smem + [vmem] * len(args)...  23.5 us
    ppermute x3, waiting for transfers between devices, fast(): lax.ppermute(main_send[k], 'x', [(i, (i + k) % 4) for i in range(4)])  20.3 us
    ppermute x7, starting transfers between devices, fast(): piece = piece + lax.ppermute(panel[k], 'y', [(0, k)])  15.2 us
    all_to_all x1, starting transfers between devices, fast(): rows_in = lax.all_to_all(rows, PROW, 0, 0)  13.7 us
    ppermute x7, starting transfers between devices, fast(): parts = [lax.ppermute(side, 'y', [(0, k)]) for k in AROUND]  12.8 us
    ppermute x3, starting transfers between devices, fast(): lax.ppermute(main_send[k], 'x', [(i, (i + k) % 4) for i in range(4)])  10.5 us
    all_to_all x1, starting transfers between devices, fast(): mine = lax.all_to_all(side_send, PROW, 0, 0)  10.4 us
    all_to_all x1, waiting for transfers between devices, fast(): rows_in = lax.all_to_all(rows, PROW, 0, 0)  7.15 us
  transfers between devices with their start and end apart: 22, of which 8 were waited for; matrix products, arithmetic and copies ran while one was open for 0% of the time, Pallas kernels for 8%

profile of v1, /device:TPU:1, one launch (start us, length us, event | category | flops | bytes accessed | tf_op | source)
XLA Modules:
  0.0 143.3 jit_solution(16592555024514417235)
XLA Ops:
  6.6 5.1 %shard_map.46 = (f32[32,5,2,768]{3,2,1,0:T(2,128)}, s32[8,256]{1,0:T(8,128)S(1)}, s32[256,8]{1,0:T(8,128)S(1)}, s32[1]{0:T(128)}, f32[96,256]{1,0:T(8,128)S(1)},...) custom-call(s32[4]{0:T(128)S(1)} %pad_add_fusion.ids, ...), custom_call_target="tpu_custom_call" | custom-call | flops 1000000 | bytes 4 | tf_op jit(solution)/shard_map/pallas_call | solution.py:335
  11.7 13.7 %all-to-all-start = ((f32[32,5,2,768]{3,2,1,0:T(2,128)}), f32[32,5,2,768]{3,2,1,0:T(2,128)S(1)}, u32[]{:S(2)}, u32[]{:S(2)}) async-start(f32[32,5,2,768]{3,2,1,0:T(2,128)} %get-tuple-element.125), calls=%async_computation | async-start | bytes 1966080 | tf_op jit(solution)/shard_map/all_to_all | solution.py:367
  25.5 7.5 %collective-permute-start = (f32[96,256]{1,0:T(8,128)S(1)}, f32[96,256]{1,0:T(8,128)S(1)}, u32[]{:S(2)}, u32[]{:S(2)}) collective-permute-start(f32[96,256]{1,0:T(8,128)S(1)} %get-tuple-element.127), channel_id=1, source_target_pairs={{0,8},{1,9},{16,24},{17,25},{32,40},{33,41},{48,56},{49,57},{64,72... | collective-permute-start | bytes 294920 | tf_op jit(solution)/shard_map/ppermute | solution.py:370
  32.9 1.3 collective-permute-start.1
  34.2 1.3 collective-permute-start.2
  35.5 1.3 collective-permute-start.3
  36.8 1.3 collective-permute-start.4
  38.2 1.3 collective-permute-start.5
  39.5 1.3 collective-permute-start.6
  41.1 1.3 collective-permute-done.6
  43.1 7.1 %all-to-all-done.in_ref = f32[32,5,2,768]{3,2,1,0:T(2,128)S(1)} async-done(((f32[32,5,2,768]{3,2,1,0:T(2,128)}), f32[32,5,2,768]{3,2,1,0:T(2,128)S(1)}, u32[]{:S(2)}, u32[]{:S(2)}) %all-to-all-start) | async-done | bytes 983072 | tf_op jit(solution)/shard_map/all_to_all | solution.py:367
  50.3 2.0 %shard_map.47 = (f32[8,24,768]{2,1,0:T(8,128)}, f32[80,256]{1,0:T(8,128)S(1)}) custom-call(s32[4]{0:T(128)S(1)} %pad_add_fusion.ids, s32[8,256]{1,0:T(8,128)S(1)} %get-tuple-element.124.ir_ref, s32[256,8]{1,0:T(8,128)S(1)} %get-tuple-element.123.ic_ref, f32[32,5,2,768]{3,2,1,0:T(2,128)S(1)} %all-to-all-done.in_ref), custom_call_target="tpu_custom_call" | custom-call | flops 1000000 | bytes 8192 | tf_op jit(solution)/shard_map/pallas_call | solution.py:335
  52.2 4.1 %all-to-all-start.1 = ((f32[8,24,768]{2,1,0:T(8,128)}), f32[8,24,768]{2,1,0:T(8,128)S(1)}, u32[]{:S(2)}, u32[]{:S(2)}) async-start(f32[8,24,768]{2,1,0:T(8,128)} %get-tuple-element.136), calls=%async_computation.1 | async-start | bytes 1179648 | tf_op jit(solution)/shard_map/all_to_all | solution.py:377
  56.3 5.1 %collective-permute-start.13 = (f32[80,256]{1,0:T(8,128)S(1)}, f32[80,256]{1,0:T(8,128)S(1)}, u32[]{:S(2)}, u32[]{:S(2)}) collective-permute-start(f32[80,256]{1,0:T(8,128)S(1)} %get-tuple-element.135.refs_0_), channel_id=1, source_target_pairs={{0,14},{1,15},{16,30},{17,31},{32,46},{33,47},{48,62},{49,63},{64,... | collective-permute-start | bytes 245768 | tf_op jit(solution)/shard_map/ppermute | solution.py:378
  61.4 1.3 collective-permute-start.12
  62.7 1.3 collective-permute-start.11
  64.0 1.3 collective-permute-start.10
  65.3 1.3 collective-permute-start.9
  67.9 1.3 collective-permute-start.7
  70.2 2.3 %collective-permute-done.7.refs_1_ = f32[80,256]{1,0:T(8,128)S(1)} collective-permute-done((f32[80,256]{1,0:T(8,128)S(1)}, f32[80,256]{1,0:T(8,128)S(1)}, u32[]{:S(2)}, u32[]{:S(2)}) %collective-permute-start.7) | collective-permute-done | bytes 81952 | tf_op jit(solution)/shard_map/ppermute | solution.py:378
  72.6 1.5 %shard_map.48 = f32[32,40,128]{2,1,0:T(8,128)} custom-call(s32[4]{0:T(128)S(1)} %pad_add_fusion.ids, f32[80,256]{1,0:T(8,128)S(1)} %get-tuple-element.135.refs_0_, f32[80,256]{1,0:T(8,128)S(1)} %collective-permute-done.7.refs_1_, f32[80,256]{1,0:T(8,128)S(1)} %collective-permute-done.8.refs_2_, f32[80,256]{1,0:T(8,128)S(1)} %collective-permute-done.9.refs_3_, ...), custom_call_target="tpu_custom_call" | custom-call | bytes 81920 | tf_op jit(solution)/shard_map/pallas_call | solution.py:335
  74.0 1.8 %shard_map.49 = (f32[144,768]{1,0:T(8,128)S(1)}, f32[144,768]{1,0:T(8,128)}, f32[144,768]{1,0:T(8,128)}, f32[144,768]{1,0:T(8,128)S(1)}) custom-call(s32[4]{0:T(128)S(1)} %pad_add_fusion.ids, f32[8,24,768]{2,1,0:T(8,128)S(1)} %all-to-all-done.1.in_ref), custom_call_target="tpu_custom_call" | custom-call | bytes 442368 | tf_op jit(solution)/shard_map/pallas_call | solution.py:335
  75.8 10.4 %all-to-all-start.2 = ((f32[32,40,128]{2,1,0:T(8,128)}), f32[32,40,128]{2,1,0:T(8,128)S(1)}, u32[]{:S(2)}, u32[]{:S(2)}) async-start(f32[32,40,128]{2,1,0:T(8,128)} %shard_map.48), calls=%async_computation.2 | async-start | bytes 1310720 | tf_op jit(solution)/shard_map/all_to_all | solution.py:384
  86.2 3.1 %collective-permute-start.14 = (f32[144,768]{1,0:T(8,128)}, f32[144,768]{1,0:T(8,128)S(1)}, u32[]{:S(2)}, u32[]{:S(2)}) collective-permute-start(f32[144,768]{1,0:T(8,128)} %get-tuple-element.143), channel_id=1, source_target_pairs={{0,16},{16,32},{32,48},{48,0},{1,17},{17,33},{33,49},{49,1},{2,18}... | collective-permute-start | bytes 1327112 | tf_op jit(solution)/shard_map/ppermute | solution.py:386
  89.3 4.3 %collective-permute-start.15 = (f32[144,768]{1,0:T(8,128)}, f32[144,768]{1,0:T(8,128)S(1)}, u32[]{:S(2)}, u32[]{:S(2)}) collective-permute-start(f32[144,768]{1,0:T(8,128)} %get-tuple-element.144), channel_id=1, source_target_pairs={{0,32},{16,48},{32,0},{48,16},{1,33},{17,49},{33,1},{49,17},{2,34}... | collective-permute-start | bytes 1327112 | tf_op jit(solution)/shard_map/ppermute | solution.py:386
  93.7 3.1 %collective-permute-start.16 = (f32[144,768]{1,0:T(8,128)S(1)}, f32[144,768]{1,0:T(8,128)S(1)}, u32[]{:S(2)}, u32[]{:S(2)}) collective-permute-start(f32[144,768]{1,0:T(8,128)S(1)} %get-tuple-element.145), channel_id=1, source_target_pairs={{0,48},{16,0},{32,16},{48,32},{1,49},{17,1},{33,17},{49,33},{2,50}... | collective-permute-start | bytes 1327112 | tf_op jit(solution)/shard_map/ppermute | solution.py:386
  96.8 10.1 %collective-permute-done.14.x1_ref = f32[144,768]{1,0:T(8,128)S(1)} collective-permute-done((f32[144,768]{1,0:T(8,128)}, f32[144,768]{1,0:T(8,128)S(1)}, u32[]{:S(2)}, u32[]{:S(2)}) %collective-permute-start.14) | collective-permute-done | bytes 442400 | tf_op jit(solution)/shard_map/ppermute | solution.py:386
  106.9 9.8 %collective-permute-done.15.x2_ref = f32[144,768]{1,0:T(8,128)S(1)} collective-permute-done((f32[144,768]{1,0:T(8,128)}, f32[144,768]{1,0:T(8,128)S(1)}, u32[]{:S(2)}, u32[]{:S(2)}) %collective-permute-start.15) | collective-permute-done | bytes 442400 | tf_op jit(solution)/shard_map/ppermute | solution.py:386
  117.0 3.9 %collective-permute-start.17 = (f32[32,40,128]{2,1,0:T(8,128)S(1)}, f32[32,40,128]{2,1,0:T(8,128)S(1)}, u32[]{:S(2)}, u32[]{:S(2)}) collective-permute-start(f32[32,40,128]{2,1,0:T(8,128)S(1)} %all-to-all-done.2.mine_ref), channel_id=1, source_target_pairs={{0,1},{1,0},{2,3},{3,2},{4,5},{5,4},{6,7},{7,6},{8,9},{9,8},{10,11... | collective-permute-start | bytes 1966088 | tf_op jit(solution)/shard_map/ppermute | solution.py:398
  121.6 1.4 copy-done
  124.0 4.8 %shard_map.51 = (f32[768,768]{1,0:T(8,128)S(1)}, f32[768,64]{1,0:T(8,128)S(1)}, f32[64,768]{1,0:T(8,128)S(1)}, f32[256,256]{1,0:T(8,128)S(1)}, f32[256,768]{1,0:T(8,128)S(1)}, /*index=5*/f32[256,768]{1,0:T(8,128)S(1)}) custom-call(s32[4]{0:T(128)S(1)} %pad_add_fusion.ids, s32[8,256]{1,0:T(8,128)S(1)} %get-tuple-element.124.ir_ref, ...), custom_call_target="tpu_custom_call" | custom-call | flops 1000000 | bytes 8192 | tf_op jit(solution)/shard_map/pallas_call | solution.py:335
  128.9 7.6 %shard_map.52 = f32[768,768]{1,0:T(8,128)} custom-call(s32[4]{0:T(128)S(1)} %pad_add_fusion.ids, s32[256,8]{1,0:T(8,128)S(1)} %get-tuple-element.123.ic_ref, f32[32,40,128]{2,1,0:T(8,128)S(1)} %all-to-all-done.2.mine_ref, f32[32,40,128]{2,1,0:T(8,128)S(1)} %collective-permute-done.17.there_ref, f32[768,768]{1,0:T(8,128)S(1)} %get-tuple-element.154.base_ref, ...), custom_call_target="tpu_custom_call" | custom-call | flops 1000000 | bytes 8192 | tf_op jit(solution)/shard_map/pallas_call | solution.py:335
  (31 shorter events, 4.8 us)
Async XLA Ops:
  11.7 38.5 %all-to-all-start = ((f32[32,5,2,768]{3,2,1,0:T(2,128)}), f32[32,5,2,768]{3,2,1,0:T(2,128)S(1)}, u32[]{:S(2)}, u32[]{:S(2)}) async-start(f32[32,5,2,768]{3,2,1,0:T(2,128)} %get-tuple-element.125), calls=%async_computation | async-start | bytes 1966080 | tf_op jit(solution)/shard_map/all_to_all | solution.py:367
  25.4 91.6 %all-gather.2.cloned.1.call-start = ((), (), s32[]{:S(2)}) async-start(), calls=%async_computation.7 | async-start | bytes 1671168 | tf_op jit(solution)/shard_map/all_gather | solution.py:372
  25.5 12.7 %collective-permute-start = (f32[96,256]{1,0:T(8,128)S(1)}, f32[96,256]{1,0:T(8,128)S(1)}, u32[]{:S(2)}, u32[]{:S(2)}) collective-permute-start(f32[96,256]{1,0:T(8,128)S(1)} %get-tuple-element.127), channel_id=1, source_target_pairs={{0,8},{1,9},{16,24},{17,25},{32,40},{33,41},{48,56},{49,57},{64,72... | collective-permute-start | bytes 294920 | tf_op jit(solution)/shard_map/ppermute | solution.py:370
  32.9 6.5 %collective-permute-start.1 = (f32[96,256]{1,0:T(8,128)S(1)}, f32[96,256]{1,0:T(8,128)S(1)}, u32[]{:S(2)}, u32[]{:S(2)}) collective-permute-start(f32[96,256]{1,0:T(8,128)S(1)} %get-tuple-element.128), channel_id=1, source_target_pairs={{0,6},{1,7},{16,22},{17,23},{32,38},{33,39},{48,54},{49,55},{64,70... | collective-permute-start | bytes 294920 | tf_op jit(solution)/shard_map/ppermute | solution.py:370
  34.2 6.5 %collective-permute-start.2 = (f32[96,256]{1,0:T(8,128)S(1)}, f32[96,256]{1,0:T(8,128)S(1)}, u32[]{:S(2)}, u32[]{:S(2)}) collective-permute-start(f32[96,256]{1,0:T(8,128)S(1)} %get-tuple-element.129), channel_id=1, source_target_pairs={{0,10},{1,11},{16,26},{17,27},{32,42},{33,43},{48,58},{49,59},{64,... | collective-permute-start | bytes 294920 | tf_op jit(solution)/shard_map/ppermute | solution.py:370
  35.5 5.3 %collective-permute-start.3 = (f32[96,256]{1,0:T(8,128)S(1)}, f32[96,256]{1,0:T(8,128)S(1)}, u32[]{:S(2)}, u32[]{:S(2)}) collective-permute-start(f32[96,256]{1,0:T(8,128)S(1)} %get-tuple-element.130), channel_id=1, source_target_pairs={{0,4},{1,5},{16,20},{17,21},{32,36},{33,37},{48,52},{49,53},{64,68... | collective-permute-start | bytes 294920 | tf_op jit(solution)/shard_map/ppermute | solution.py:370
  36.8 4.0 %collective-permute-start.4 = (f32[96,256]{1,0:T(8,128)S(1)}, f32[96,256]{1,0:T(8,128)S(1)}, u32[]{:S(2)}, u32[]{:S(2)}) collective-permute-start(f32[96,256]{1,0:T(8,128)S(1)} %get-tuple-element.131), channel_id=1, source_target_pairs={{0,12},{1,13},{16,28},{17,29},{32,44},{33,45},{48,60},{49,61},{64,... | collective-permute-start | bytes 294920 | tf_op jit(solution)/shard_map/ppermute | solution.py:370
  38.2 2.9 %collective-permute-start.5 = (f32[96,256]{1,0:T(8,128)S(1)}, f32[96,256]{1,0:T(8,128)S(1)}, u32[]{:S(2)}, u32[]{:S(2)}) collective-permute-start(f32[96,256]{1,0:T(8,128)S(1)} %get-tuple-element.132), channel_id=1, source_target_pairs={{0,2},{1,3},{16,18},{17,19},{32,34},{33,35},{48,50},{49,51},{64,66... | collective-permute-start | bytes 294920 | tf_op jit(solution)/shard_map/ppermute | solution.py:370
  39.5 2.9 %collective-permute-start.6 = (f32[96,256]{1,0:T(8,128)S(1)}, f32[96,256]{1,0:T(8,128)S(1)}, u32[]{:S(2)}, u32[]{:S(2)}) collective-permute-start(f32[96,256]{1,0:T(8,128)S(1)} %get-tuple-element.133), channel_id=1, source_target_pairs={{0,14},{1,15},{16,30},{17,31},{32,46},{33,47},{48,62},{49,63},{64,... | collective-permute-start | bytes 294920 | tf_op jit(solution)/shard_map/ppermute | solution.py:370
  52.2 69.3 %copy-start.4 = (f32[2,256,256]{2,1,0:T(8,128)S(1)}, f32[2,256,256]{2,1,0:T(8,128)}, u32[]{:S(2)}) copy-start(f32[2,256,256]{2,1,0:T(8,128)} %ui_ref.3) | copy-start | bytes 1572868
  52.2 21.8 %all-to-all-start.1 = ((f32[8,24,768]{2,1,0:T(8,128)}), f32[8,24,768]{2,1,0:T(8,128)S(1)}, u32[]{:S(2)}, u32[]{:S(2)}) async-start(f32[8,24,768]{2,1,0:T(8,128)} %get-tuple-element.136), calls=%async_computation.1 | async-start | bytes 1179648 | tf_op jit(solution)/shard_map/all_to_all | solution.py:377
  56.3 10.3 %collective-permute-start.13 = (f32[80,256]{1,0:T(8,128)S(1)}, f32[80,256]{1,0:T(8,128)S(1)}, u32[]{:S(2)}, u32[]{:S(2)}) collective-permute-start(f32[80,256]{1,0:T(8,128)S(1)} %get-tuple-element.135.refs_0_), channel_id=1, source_target_pairs={{0,14},{1,15},{16,30},{17,31},{32,46},{33,47},{48,62},{49,63},{64,... | collective-permute-start | bytes 245768 | tf_op jit(solution)/shard_map/ppermute | solution.py:378
  61.4 6.5 %collective-permute-start.12 = (f32[80,256]{1,0:T(8,128)S(1)}, f32[80,256]{1,0:T(8,128)S(1)}, u32[]{:S(2)}, u32[]{:S(2)}) collective-permute-start(f32[80,256]{1,0:T(8,128)S(1)} %get-tuple-element.135.refs_0_), channel_id=1, source_target_pairs={{0,2},{1,3},{16,18},{17,19},{32,34},{33,35},{48,50},{49,51},{64,66... | collective-permute-start | bytes 245768 | tf_op jit(solution)/shard_map/ppermute | solution.py:378
  62.7 6.5 %collective-permute-start.11 = (f32[80,256]{1,0:T(8,128)S(1)}, f32[80,256]{1,0:T(8,128)S(1)}, u32[]{:S(2)}, u32[]{:S(2)}) collective-permute-start(f32[80,256]{1,0:T(8,128)S(1)} %get-tuple-element.135.refs_0_), channel_id=1, source_target_pairs={{0,12},{1,13},{16,28},{17,29},{32,44},{33,45},{48,60},{49,61},{64,... | collective-permute-start | bytes 245768 | tf_op jit(solution)/shard_map/ppermute | solution.py:378
  64.0 5.2 %collective-permute-start.10 = (f32[80,256]{1,0:T(8,128)S(1)}, f32[80,256]{1,0:T(8,128)S(1)}, u32[]{:S(2)}, u32[]{:S(2)}) collective-permute-start(f32[80,256]{1,0:T(8,128)S(1)} %get-tuple-element.135.refs_0_), channel_id=1, source_target_pairs={{0,4},{1,5},{16,20},{17,21},{32,36},{33,37},{48,52},{49,53},{64,68... | collective-permute-start | bytes 245768 | tf_op jit(solution)/shard_map/ppermute | solution.py:378
  65.3 4.0 %collective-permute-start.9 = (f32[80,256]{1,0:T(8,128)S(1)}, f32[80,256]{1,0:T(8,128)S(1)}, u32[]{:S(2)}, u32[]{:S(2)}) collective-permute-start(f32[80,256]{1,0:T(8,128)S(1)} %get-tuple-element.135.refs_0_), channel_id=1, source_target_pairs={{0,10},{1,11},{16,26},{17,27},{32,42},{33,43},{48,58},{49,59},{64,... | collective-permute-start | bytes 245768 | tf_op jit(solution)/shard_map/ppermute | solution.py:378
  66.6 3.6 %collective-permute-start.8 = (f32[80,256]{1,0:T(8,128)S(1)}, f32[80,256]{1,0:T(8,128)S(1)}, u32[]{:S(2)}, u32[]{:S(2)}) collective-permute-start(f32[80,256]{1,0:T(8,128)S(1)} %get-tuple-element.135.refs_0_), channel_id=1, source_target_pairs={{0,6},{1,7},{16,22},{17,23},{32,38},{33,39},{48,54},{49,55},{64,70... | collective-permute-start | bytes 245768 | tf_op jit(solution)/shard_map/ppermute | solution.py:378
  67.9 4.6 %collective-permute-start.7 = (f32[80,256]{1,0:T(8,128)S(1)}, f32[80,256]{1,0:T(8,128)S(1)}, u32[]{:S(2)}, u32[]{:S(2)}) collective-permute-start(f32[80,256]{1,0:T(8,128)S(1)} %get-tuple-element.135.refs_0_), channel_id=1, source_target_pairs={{0,8},{1,9},{16,24},{17,25},{32,40},{33,41},{48,56},{49,57},{64,72... | collective-permute-start | bytes 245768 | tf_op jit(solution)/shard_map/ppermute | solution.py:378
  75.8 41.2 %all-to-all-start.2 = ((f32[32,40,128]{2,1,0:T(8,128)}), f32[32,40,128]{2,1,0:T(8,128)S(1)}, u32[]{:S(2)}, u32[]{:S(2)}) async-start(f32[32,40,128]{2,1,0:T(8,128)} %shard_map.48), calls=%async_computation.2 | async-start | bytes 1310720 | tf_op jit(solution)/shard_map/all_to_all | solution.py:384
  86.2 20.7 %collective-permute-start.14 = (f32[144,768]{1,0:T(8,128)}, f32[144,768]{1,0:T(8,128)S(1)}, u32[]{:S(2)}, u32[]{:S(2)}) collective-permute-start(f32[144,768]{1,0:T(8,128)} %get-tuple-element.143), channel_id=1, source_target_pairs={{0,16},{16,32},{32,48},{48,0},{1,17},{17,33},{33,49},{49,1},{2,18}... | collective-permute-start | bytes 1327112 | tf_op jit(solution)/shard_map/ppermute | solution.py:386
  89.3 27.4 %collective-permute-start.15 = (f32[144,768]{1,0:T(8,128)}, f32[144,768]{1,0:T(8,128)S(1)}, u32[]{:S(2)}, u32[]{:S(2)}) collective-permute-start(f32[144,768]{1,0:T(8,128)} %get-tuple-element.144), channel_id=1, source_target_pairs={{0,32},{16,48},{32,0},{48,16},{1,33},{17,49},{33,1},{49,17},{2,34}... | collective-permute-start | bytes 1327112 | tf_op jit(solution)/shard_map/ppermute | solution.py:386
  93.7 23.4 %collective-permute-start.16 = (f32[144,768]{1,0:T(8,128)S(1)}, f32[144,768]{1,0:T(8,128)S(1)}, u32[]{:S(2)}, u32[]{:S(2)}) collective-permute-start(f32[144,768]{1,0:T(8,128)S(1)} %get-tuple-element.145), channel_id=1, source_target_pairs={{0,48},{16,0},{32,16},{48,32},{1,49},{17,1},{33,17},{49,33},{2,50}... | collective-permute-start | bytes 1327112 | tf_op jit(solution)/shard_map/ppermute | solution.py:386
  117.0 11.8 %collective-permute-start.17 = (f32[32,40,128]{2,1,0:T(8,128)S(1)}, f32[32,40,128]{2,1,0:T(8,128)S(1)}, u32[]{:S(2)}, u32[]{:S(2)}) collective-permute-start(f32[32,40,128]{2,1,0:T(8,128)S(1)} %all-to-all-done.2.mine_ref), channel_id=1, source_target_pairs={{0,1},{1,0},{2,3},{3,2},{4,5},{5,4},{6,7},{7,6},{8,9},{9,8},{10,11... | collective-permute-start | bytes 1966088 | tf_op jit(solution)/shard_map/ppermute | solution.py:398
  121.6 1.4 copy-start
  123.0 1.0 copy-start.6
  128.8 7.6 %copy-start.9 = (s32[2,256]{1,0:T(2,128)S(1)}, s32[2,256]{1,0:T(2,128)}, u32[]{:S(2)}) copy-start(s32[2,256]{1,0:T(2,128)} %p_ref.1) | copy-start | bytes 6148
Sparse Core Ops, SparseCore 0:
  50.4 40.9 all-gather.1

commit v2 on v1

--- a/solution.py
+++ b/solution.py
@@ -199,17 +199,33 @@
 
 
 def side_kernel(ids, *refs):
-    own, out, sums = refs[0], refs[8], refs[9]
+    own, outs, sums = refs[0], refs[8:12], refs[12]
     total = jnp.where(ids[2] == 0, own[...], F32(0.0))
     for r in refs[1:8]:
         total = total + r[...]
     sums[...] = total
-    for m in range(NP):
+    for s, out in enumerate(outs):
+        to = (ids[0] + s) & 3
         for h in range(2):
             cut = slice(128 * h, 128 * h + 128)
-            out[m, 16 * h : 16 * h + 16, :] = sums[0:16, cut]
-            out[m, 32 + 2 * h : 34 + 2 * h, :] = sums[16 + 2 * m : 18 + 2 * m, cut]
-        out[m, 36:40, :] = jnp.zeros((4, 128), F32)
+            out[16 * h : 16 * h + 16, :] = sums[0:16, cut]
+            for z in range(8):
+                back = sums[16 + 8 * z : 18 + 8 * z, cut]
+                for x in range(1, 4):
+                    at = 16 + 8 * z + 2 * x
+                    back = jnp.where(to == x, sums[at : at + 2, cut], back)
+                at = 32 + 16 * h + 2 * z
+                out[at : at + 2, :] = back
+
+
+def join_kernel(*refs):
+    blocks, out = refs[:4], refs[4]
+    for z in range(8):
+        for s, block in enumerate(blocks):
+            for h in range(2):
+                out[z, 64 * h + 16 * s : 64 * h + 16 * s + 16, :] = block[16 * h : 16 * h + 16, :]
+                at = 32 + 16 * h + 2 * z
+                out[z, 128 + 8 * h + 2 * s : 130 + 8 * h + 2 * s, :] = block[at : at + 2, :]
 
 
 def mid_kernel(ids, in_ref, *out_refs):
@@ -223,20 +239,16 @@
             out_ref[128 + 2 * z : 130 + 2 * z, :] = back
 
 
-def pre_kernel(raw_ref, ui_ref, low0_ref, end1_ref):
-    for n, out in enumerate((low0_ref, end1_ref)):
-        raw = jnp.concatenate([raw_ref[y, n] for y in range(8)], axis=0)
-        out[...] = dot3(raw, ui_ref[n])
-
-
 def main_kernel(
-    ids, ir_ref, ic_ref, a_ref, x0_ref, x1_ref, x2_ref, x3_ref, low0_ref, li_ref,
-    base_ref, put_ref, back_ref, new0_ref, new1_ref, u0_ref,
+    ids, ir_ref, ic_ref, a_ref, x0_ref, x1_ref, x2_ref, x3_ref, li_ref, ui_ref, raw_ref,
+    base_ref, put_ref, back_ref, new0_ref, new1_ref, u0_ref, low0_ref, end1_ref, held_ref, sem,
 ):
     me = ids[0]
+    fetch = pltpu.make_async_copy(raw_ref, held_ref, sem)
+    fetch.start()
     put = jnp.zeros((RD, 2 * NP), F32)
     lane = iota((NB, 2 * NP), 1)
-    m = ((lane >> 1) & 7) * 4 + (lane >> 4)
+    m = (lane >> 3) * 4 + ((me - ((lane >> 1) & 3)) & 3)
     for g in range(2):
         own, loc = ir_ref[3 * g + 1 : 3 * g + 2, :], ir_ref[3 * g + 2 : 3 * g + 3, :]
         t = f((own == me) & (loc == iota((RD, NB), 0)))
@@ -245,19 +257,21 @@
     put_ref[...] = put
     blocks = (x0_ref, x1_ref, x2_ref, x3_ref)
     slots = jnp.concatenate([r[0:128, :] for r in blocks], axis=0)
-    for x in range(4):
-        s = (me - x) & 3
-        back = blocks[0][128:144, :]
-        for k in range(1, 4):
-            back = jnp.where(s == k, blocks[k][128:144, :], back)
-        back_ref[16 * x : 16 * x + 16, :] = back
+    for z in range(8):
+        for s in range(4):
+            at = 8 * z + 2 * s
+            back_ref[at : at + 2, :] = blocks[s][128 + 2 * z : 130 + 2 * z, :]
     lane = iota((NB, 2 * NB), 1)
     slot = ((me - (lane >> 7)) & 3) * 128 + (lane & 127)
-    new0 = pick3(f(ic_ref[:, 6:7] == slot), slots)
-    new1_ref[...] = pick3(f(ic_ref[:, 7:8] == slot), slots)
+    new0 = pick2(f(ic_ref[:, 6:7] == slot), slots)
+    new1_ref[...] = pick2(f(ic_ref[:, 7:8] == slot), slots)
     new0_ref[...] = new0[:, 0:NB]
     u0 = dot3(li_ref[0], new0)
     u0_ref[...] = u0
+    fetch.wait()
+    for n, out in enumerate((low0_ref, end1_ref)):
+        raw = jnp.concatenate([held_ref[y, n] for y in range(8)], axis=0)
+        out[...] = dot3(raw, ui_ref[n])
     for r in range(3):
         rows = pl.ds(NB * r, NB)
         base_ref[rows, :] = a_ref[rows, :] - dot3(low0_ref[rows, :], u0)
@@ -265,78 +279,85 @@
 
 def final_kernel(
     ids, ic_ref, mine_ref, there_ref, base_ref, put_ref, back_ref, new0_ref, new1_ref, u0_ref,
-    low0_ref, end1_ref, li_ref, ui_ref, out_ref, slots_ref, rows_ref,
+    low0_ref, end1_ref, li_ref, ui_ref, out_ref, done_ref, slots_ref, rows_ref, sem,
 ):
     me, col, core = ids[0], ids[1], ids[3]
-    for x in range(4):
-        for z in range(8):
-            m, n = 4 * z + x, 8 * x + z
-            mine, there = mine_ref[m], there_ref[m]
-            for k in range(2):
-                got = jnp.where(core == k, mine, there)
-                for h in range(2):
-                    cut = slice(128 * h, 128 * h + 128)
-                    slots_ref[k, 16 * n : 16 * n + 16, cut] = got[16 * h : 16 * h + 16]
-                    rows_ref[k, 2 * n : 2 * n + 2, cut] = got[32 + 2 * h : 34 + 2 * h]
+    for z in range(8):
+        mine, there = mine_ref[z], there_ref[z]
+        for k in range(2):
+            got = jnp.where(core == k, mine, there)
+            for h in range(2):
+                cut = slice(128 * h, 128 * h + 128)
+                slots_ref[k, 64 * z : 64 * z + 64, cut] = got[64 * h : 64 * h + 64]
+                rows_ref[k, 8 * z : 8 * z + 8, cut] = got[128 + 8 * h : 136 + 8 * h]
     u0 = u0_ref[...]
-    perm0 = f(ic_ref[:, 6:7] == iota((NB, 2 * NB), 1))
-    perm1 = f(ic_ref[:, 7:8] == iota((NB, 2 * NB), 1))
-    diag = dot3(pick2(perm1, slots_ref[0]), ui_ref[0])
+    lane = iota((NB, 2 * NB), 1)
+    slot = ((me - (lane >> 4)) & 3) * 128 + (lane >> 6) * 16 + (lane & 15)
+    diag = dot3(pick2(f(ic_ref[:, 7:8] == slot), slots_ref[0]), ui_ref[0])
     next1 = new1_ref[...] - dot3(diag, u0)
     u1 = dot3(li_ref[1], next1)
-    fill = dot3(dot3(li_ref[0], pick2(perm0, slots_ref[1])), ui_ref[1])
+    new0_c1 = pick2(f(ic_ref[:, 6:7] == slot), slots_ref[1])
+    fill = dot3(dot3(li_ref[0], new0_c1), ui_ref[1])
     low0_back = dot3(rows_ref[0], ui_ref[0])
     low1_back = dot3(rows_ref[1], ui_ref[1]) - dot3(low0_back, fill)
     back = back_ref[...] - dot3(low0_back, u0) - dot3(low1_back, u1)
-    for r in range(3):
+    copies = []
+    for r in (2, 1, 0):
         rows = pl.ds(NB * r, NB)
         put = put_ref[rows, :]
         moved = sum_cols(put) > 0
         low0 = low0_ref[rows, :]
         low1 = end1_ref[rows, :] - dot3(low0, fill)
-        out_ref[rows, :] = jnp.where(moved, pick2(put, back), base_ref[rows, :] - dot3(low1, u1))
+        done_ref[rows, :] = jnp.where(moved, pick2(put, back), base_ref[rows, :] - dot3(low1, u1))
 
         @pl.when(col == 0)
         def _():
-            out_ref[rows, 0:NB] = jnp.where(moved, pick2(put, low0_back), low0)
+            done_ref[rows, 0:NB] = jnp.where(moved, pick2(put, low0_back), low0)
 
         @pl.when(col == 1)
         def _():
-            out_ref[rows, 0:NB] = jnp.where(moved, pick2(put, low1_back), low1)
-
-    @pl.when(me == 0)
-    def _():
-        out_ref[0:NB, :] = u0
-
-        @pl.when(col == 0)
-        def _():
-            out_ref[0:NB, 0:NB] = new0_ref[...]
-
-    @pl.when(me == 1)
-    def _():
-        out_ref[0:NB, :] = u1
-
-        @pl.when(col == 0)
-        def _():
-            out_ref[0:NB, 0:NB] = diag
-
-        @pl.when(col == 1)
-        def _():
-            out_ref[0:NB, 0:NB] = next1[:, 0:NB]
+            done_ref[rows, 0:NB] = jnp.where(moved, pick2(put, low1_back), low1)
+
+        if r == 0:
+
+            @pl.when(me == 0)
+            def _():
+                done_ref[0:NB, :] = u0
+
+                @pl.when(col == 0)
+                def _():
+                    done_ref[0:NB, 0:NB] = new0_ref[...]
+
+            @pl.when(me == 1)
+            def _():
+                done_ref[0:NB, :] = u1
+
+                @pl.when(col == 0)
+                def _():
+                    done_ref[0:NB, 0:NB] = diag
+
+                @pl.when(col == 1)
+                def _():
+                    done_ref[0:NB, 0:NB] = next1[:, 0:NB]
+
+        copies.append(pltpu.make_async_copy(done_ref.at[rows, :], out_ref.at[rows, :], sem.at[r]))
+        copies[-1].start()
+    for copy in copies:
+        copy.wait()
 
 
 SCALAR = pl.BlockSpec(memory_space=pltpu.SMEM)
 
 
-def call(kernel, outs, ids, *args, scratch=(), flops=0):
-    vmem = pl.BlockSpec(memory_space=pltpu.VMEM)
+def call(kernel, outs, ids, *args, scratch=(), flops=0, far=(), far_out=False):
+    vmem, anywhere = pl.BlockSpec(memory_space=pltpu.VMEM), pl.BlockSpec(memory_space=pl.ANY)
     smem = [] if ids is None else [SCALAR]
     sizes = [4 * o.size for o in jax.tree.leaves((outs, args))]
     return pl.pallas_call(
         kernel,
         out_shape=outs,
-        in_specs=smem + [vmem] * len(args),
-        out_specs=jax.tree.map(lambda o: SCALAR if o.shape == (1,) else vmem, outs),
+        in_specs=smem + [anywhere if n in far else vmem for n in range(len(args))],
+        out_specs=jax.tree.map(lambda o: SCALAR if o.shape == (1,) else anywhere if far_out else vmem, outs),
         scratch_shapes=scratch,
         compiler_params=pltpu.CompilerParams(vmem_limit_bytes=40 * 1024 * 1024),
         cost_estimate=pl.CostEstimate(flops=flops, bytes_accessed=min(sizes), transcendentals=0),
@@ -348,6 +369,12 @@
 
 
 AROUND = (4, 3, 5, 2, 6, 1, 7)
+
+
+def along_x(blocks):
+    return [blocks[0]] + [
+        lax.ppermute(blocks[s], "x", [(i, (i + s) % 4) for i in range(4)]) for s in range(1, 4)
+    ]
 
 
 def fast(matrix, pivots, lower_inv, upper_inv):
@@ -377,30 +404,29 @@
     main_z = lax.all_to_all(send, "z", 0, 0)
     parts = [lax.ppermute(side, "y", [(0, k)]) for k in AROUND]
     side_send = call(
-        side_kernel, shape(NP, 40, 128), ids, side, *parts, scratch=[pltpu.VMEM((80, NB), F32)]
-    )
-    main_send = call(mid_kernel, [shape(144, RD)] * 4, ids, main_z)
-    side_send, main_send = lax.optimization_barrier((side_send, main_send))
-    mine = lax.all_to_all(side_send, PROW, 0, 0)
-    main_x = [main_send[0]] + [
-        lax.ppermute(main_send[k], "x", [(i, (i + k) % 4) for i in range(4)]) for k in range(1, 4)
-    ]
+        side_kernel, [shape(64, 128)] * 4, ids, side, *parts, scratch=[pltpu.VMEM((80, NB), F32)]
+    )
+    side_x = along_x(side_send)
+    main_x = along_x(call(mid_kernel, [shape(144, RD)] * 4, ids, main_z))
+    mine = lax.all_to_all(call(join_kernel, shape(8, 144, 128), None, *side_x), "z", 0, 0)
     mine, main_x, raw = lax.optimization_barrier((mine, main_x, raw))
-    low0, end1 = call(pre_kernel, (shape(RD, NB), shape(RD, NB)), None, raw, upper_inv, flops=10**6)
-    base, put, back, new0, new1, u0 = call(
+    there = lax.ppermute(mine, "core", [(0, 1), (1, 0)])
+    base, put, back, new0, new1, u0, low0, end1 = call(
         main_kernel,
         (
             shape(RD, RD), shape(RD, 2 * NP), shape(2 * NP, RD), shape(NB, NB), shape(NB, RD),
-            shape(NB, RD),
+            shape(NB, RD), shape(RD, NB), shape(RD, NB),
         ),
-        ids, ir, ic, matrix, *main_x, low0, lower_inv, flops=10**6,
-    )
-    there = lax.ppermute(mine, "core", [(0, 1), (1, 0)])
+        ids, ir, ic, matrix, *main_x, lower_inv, upper_inv, raw, far=(9,),
+        scratch=[pltpu.VMEM((8, 2, part, NB), F32), pltpu.SemaphoreType.DMA],
+    )
     out = call(
         final_kernel, shape(RD, RD), ids, ic, mine, there, base, put, back, new0, new1, u0,
-        low0, end1, lower_inv, upper_inv,
-        scratch=[pltpu.VMEM((2, 2 * NB, NB), F32), pltpu.VMEM((2, 2 * NP, NB), F32)],
-        flops=10**6,
+        low0, end1, lower_inv, upper_inv, far_out=True,
+        scratch=[
+            pltpu.VMEM((RD, RD), F32), pltpu.VMEM((2, 2 * NB, NB), F32),
+            pltpu.VMEM((2, 2 * NP, NB), F32), pltpu.SemaphoreType.DMA((3,)),
+        ],
     )
     return out, most[0]
 

time: 144 us -> 147 us (1.021)
  starting transfers between devices: 70.7 us -> 77 us
  waiting for transfers between devices: 32.4 us -> 29.4 us
    ppermute x3 -> x6, starting transfers between devices: 10.5 us -> 19.5 us  [along_x(): lax.ppermute(blocks[s], 'x', [(i, (i + s) % 4) for i in range(4)])]
    ppermute x3 -> x6, waiting for transfers between devices: 20.3 us -> 15 us  [along_x(): lax.ppermute(blocks[s], 'x', [(i, (i + s) % 4) for i in range(4)])]
    all_to_all x1, starting transfers between devices: 10.4 us -> 6.32 us  [fast(): lax.all_to_all(call(join_kernel, shape(8, 144, 128), None, *side_x), 'z',...]
    all_to_all x1, waiting for transfers between devices: 0.01 us -> 3.23 us  [fast(): lax.all_to_all(call(join_kernel, shape(8, 144, 128), None, *side_x), 'z',...]
  transfers between devices with their start and end apart: 22 -> 25, of which waited for: 8 -> 9; matrix products, arithmetic and copies ran while one was open for 0% -> 0% of each run, Pallas kernels for 8% -> 8%
where the time goes in v2:
time: 147 us; the launch traced here: 146 us
  starting transfers between devices  77 us (52%)
  waiting for transfers between devices  29.4 us (20%)
  Pallas kernels  23.2 us (16%)
  between operations  14.4 us (10%)
    pallas_call x7, Pallas kernels, call(): pl.pallas_call(kernel, out_shape=outs, in_specs=smem + [anywhere if n in...  23.2 us
    ppermute x6, starting transfers between devices, along_x(): lax.ppermute(blocks[s], 'x', [(i, (i + s) % 4) for i in range(4)])  19.5 us
    ppermute x7, starting transfers between devices, fast(): piece = piece + lax.ppermute(panel[k], 'y', [(0, k)])  15.2 us
    ppermute x6, waiting for transfers between devices, along_x(): lax.ppermute(blocks[s], 'x', [(i, (i + s) % 4) for i in range(4)])  15 us
    all_to_all x1, starting transfers between devices, fast(): rows_in = lax.all_to_all(rows, PROW, 0, 0)  13.7 us
    ppermute x7, starting transfers between devices, fast(): parts = [lax.ppermute(side, 'y', [(0, k)]) for k in AROUND]  13 us
    all_to_all x1, waiting for transfers between devices, fast(): rows_in = lax.all_to_all(rows, PROW, 0, 0)  7.16 us
    all_to_all x1, starting transfers between devices, fast(): lax.all_to_all(call(join_kernel, shape(8, 144, 128), None, *side_x), 'z',...  6.32 us
  transfers between devices with their start and end apart: 25, of which 9 were waited for; matrix products, arithmetic and copies ran while one was open for 0% of the time, Pallas kernels for 8%

profile of v2, /device:TPU:1, one launch (start us, length us, event | category | flops | bytes accessed | tf_op | source)
XLA Modules:
  0.0 146.4 jit_solution(4024183550861085203)
XLA Ops:
  6.6 5.1 %shard_map.46 = (f32[32,5,2,768]{3,2,1,0:T(2,128)}, s32[8,256]{1,0:T(8,128)S(1)}, s32[256,8]{1,0:T(8,128)S(1)}, s32[1]{0:T(128)}, f32[96,256]{1,0:T(8,128)S(1)},...) custom-call(s32[4]{0:T(128)S(1)} %pad_add_fusion.ids, ...), custom_call_target="tpu_custom_call" | custom-call | flops 1000000 | bytes 4 | tf_op jit(solution)/shard_map/pallas_call | solution.py:356
  11.7 13.7 %all-to-all-start = ((f32[32,5,2,768]{3,2,1,0:T(2,128)}), f32[32,5,2,768]{3,2,1,0:T(2,128)S(1)}, u32[]{:S(2)}, u32[]{:S(2)}) async-start(f32[32,5,2,768]{3,2,1,0:T(2,128)} %get-tuple-element.124), calls=%async_computation | async-start | bytes 1966080 | tf_op jit(solution)/shard_map/all_to_all | solution.py:394
  25.5 7.5 %collective-permute-start = (f32[96,256]{1,0:T(8,128)S(1)}, f32[96,256]{1,0:T(8,128)S(1)}, u32[]{:S(2)}, u32[]{:S(2)}) collective-permute-start(f32[96,256]{1,0:T(8,128)S(1)} %get-tuple-element.126), channel_id=1, source_target_pairs={{0,8},{1,9},{16,24},{17,25},{32,40},{33,41},{48,56},{49,57},{64,72... | collective-permute-start | bytes 294920 | tf_op jit(solution)/shard_map/ppermute | solution.py:397
  32.9 1.3 collective-permute-start.1
  34.2 1.3 collective-permute-start.2
  35.5 1.3 collective-permute-start.3
  36.8 1.3 collective-permute-start.4
  38.2 1.3 collective-permute-start.5
  39.5 1.3 collective-permute-start.6
  41.1 1.3 collective-permute-done.6
  43.1 7.2 %all-to-all-done.in_ref = f32[32,5,2,768]{3,2,1,0:T(2,128)S(1)} async-done(((f32[32,5,2,768]{3,2,1,0:T(2,128)}), f32[32,5,2,768]{3,2,1,0:T(2,128)S(1)}, u32[]{:S(2)}, u32[]{:S(2)}) %all-to-all-start) | async-done | bytes 983072 | tf_op jit(solution)/shard_map/all_to_all | solution.py:394
  50.3 2.0 %shard_map.47 = (f32[8,24,768]{2,1,0:T(8,128)}, f32[80,256]{1,0:T(8,128)S(1)}) custom-call(s32[4]{0:T(128)S(1)} %pad_add_fusion.ids, s32[8,256]{1,0:T(8,128)S(1)} %get-tuple-element.123.ir_ref, s32[256,8]{1,0:T(8,128)S(1)} %get-tuple-element.122.ic_ref, f32[32,5,2,768]{3,2,1,0:T(2,128)S(1)} %all-to-all-done.in_ref), custom_call_target="tpu_custom_call" | custom-call | flops 1000000 | bytes 8192 | tf_op jit(solution)/shard_map/pallas_call | solution.py:356
  52.2 3.9 %all-to-all-start.2 = ((f32[8,24,768]{2,1,0:T(8,128)}), f32[8,24,768]{2,1,0:T(8,128)S(1)}, u32[]{:S(2)}, u32[]{:S(2)}) async-start(f32[8,24,768]{2,1,0:T(8,128)} %get-tuple-element.139), calls=%async_computation.2 | async-start | bytes 1179648 | tf_op jit(solution)/shard_map/all_to_all | solution.py:404
  56.2 4.2 %collective-permute-start.10 = (f32[80,256]{1,0:T(8,128)S(1)}, f32[80,256]{1,0:T(8,128)S(1)}, u32[]{:S(2)}, u32[]{:S(2)}) collective-permute-start(f32[80,256]{1,0:T(8,128)S(1)} %get-tuple-element.134.refs_0_), channel_id=1, source_target_pairs={{0,4},{1,5},{16,20},{17,21},{32,36},{33,37},{48,52},{49,53},{64,68... | collective-permute-start | bytes 245768 | tf_op jit(solution)/shard_map/ppermute | solution.py:405
  60.4 2.4 %collective-permute-start.11 = (f32[80,256]{1,0:T(8,128)S(1)}, f32[80,256]{1,0:T(8,128)S(1)}, u32[]{:S(2)}, u32[]{:S(2)}) collective-permute-start(f32[80,256]{1,0:T(8,128)S(1)} %get-tuple-element.134.refs_0_), channel_id=1, source_target_pairs={{0,12},{1,13},{16,28},{17,29},{32,44},{33,45},{48,60},{49,61},{64,... | collective-permute-start | bytes 245768 | tf_op jit(solution)/shard_map/ppermute | solution.py:405
  69.3 1.6 %collective-permute-done.8.refs_2_ = f32[80,256]{1,0:T(8,128)S(1)} collective-permute-done((f32[80,256]{1,0:T(8,128)S(1)}, f32[80,256]{1,0:T(8,128)S(1)}, u32[]{:S(2)}, u32[]{:S(2)}) %collective-permute-start.8) | collective-permute-done | bytes 81952 | tf_op jit(solution)/shard_map/ppermute | solution.py:405
  72.4 4.4 %collective-permute-start.14 = (f32[64,128]{1,0:T(8,128)S(1)}, f32[64,128]{1,0:T(8,128)S(1)}, u32[]{:S(2)}, u32[]{:S(2)}) collective-permute-start(f32[64,128]{1,0:T(8,128)S(1)} %get-tuple-element.136), channel_id=1, source_target_pairs={{0,16},{16,32},{32,48},{48,0},{1,17},{17,33},{33,49},{49,1},{2,18}... | collective-permute-start | bytes 98312 | tf_op jit(solution)/shard_map/ppermute | solution.py:376
  76.8 3.8 %collective-permute-start.15 = (f32[64,128]{1,0:T(8,128)S(1)}, f32[64,128]{1,0:T(8,128)S(1)}, u32[]{:S(2)}, u32[]{:S(2)}) collective-permute-start(f32[64,128]{1,0:T(8,128)S(1)} %get-tuple-element.137), channel_id=1, source_target_pairs={{0,32},{16,48},{32,0},{48,16},{1,33},{17,49},{33,1},{49,17},{2,34}... | collective-permute-start | bytes 98312 | tf_op jit(solution)/shard_map/ppermute | solution.py:376
  80.5 2.7 %collective-permute-start.16 = (f32[64,128]{1,0:T(8,128)S(1)}, f32[64,128]{1,0:T(8,128)S(1)}, u32[]{:S(2)}, u32[]{:S(2)}) collective-permute-start(f32[64,128]{1,0:T(8,128)S(1)} %get-tuple-element.138), channel_id=1, source_target_pairs={{0,48},{16,0},{32,16},{48,32},{1,49},{17,1},{33,17},{49,33},{2,50}... | collective-permute-start | bytes 98312 | tf_op jit(solution)/shard_map/ppermute | solution.py:376
  83.3 2.3 %collective-permute-done.16.refs_3_ = f32[64,128]{1,0:T(8,128)S(1)} collective-permute-done((f32[64,128]{1,0:T(8,128)S(1)}, f32[64,128]{1,0:T(8,128)S(1)}, u32[]{:S(2)}, u32[]{:S(2)}) %collective-permute-start.16) | collective-permute-done | bytes 32800 | tf_op jit(solution)/shard_map/ppermute | solution.py:376
  86.5 6.3 %all-to-all-start.1 = ((f32[8,144,128]{2,1,0:T(8,128)}), f32[8,144,128]{2,1,0:T(8,128)S(1)}, u32[]{:S(2)}, u32[]{:S(2)}) async-start(f32[8,144,128]{2,1,0:T(8,128)} %shard_map.49), calls=%async_computation.1 | async-start | bytes 1179648 | tf_op jit(solution)/shard_map/all_to_all | solution.py:411
  92.8 1.8 %shard_map.50 = (f32[144,768]{1,0:T(8,128)S(1)}, f32[144,768]{1,0:T(8,128)}, f32[144,768]{1,0:T(8,128)}, f32[144,768]{1,0:T(8,128)S(1)}) custom-call(s32[4]{0:T(128)S(1)} %pad_add_fusion.ids, f32[8,24,768]{2,1,0:T(8,128)S(1)} %all-to-all-done.2.in_ref), custom_call_target="tpu_custom_call" | custom-call | bytes 442368 | tf_op jit(solution)/shard_map/pallas_call | solution.py:356
  94.6 1.9 %collective-permute-start.17 = (f32[144,768]{1,0:T(8,128)}, f32[144,768]{1,0:T(8,128)S(1)}, u32[]{:S(2)}, u32[]{:S(2)}) collective-permute-start(f32[144,768]{1,0:T(8,128)} %get-tuple-element.141), channel_id=1, source_target_pairs={{0,16},{16,32},{32,48},{48,0},{1,17},{17,33},{33,49},{49,1},{2,18}... | collective-permute-start | bytes 1327112 | tf_op jit(solution)/shard_map/ppermute | solution.py:376
  96.5 4.8 %collective-permute-start.18 = (f32[144,768]{1,0:T(8,128)}, f32[144,768]{1,0:T(8,128)S(1)}, u32[]{:S(2)}, u32[]{:S(2)}) collective-permute-start(f32[144,768]{1,0:T(8,128)} %get-tuple-element.142), channel_id=1, source_target_pairs={{0,32},{16,48},{32,0},{48,16},{1,33},{17,49},{33,1},{49,17},{2,34}... | collective-permute-start | bytes 1327112 | tf_op jit(solution)/shard_map/ppermute | solution.py:376
  101.3 2.0 %collective-permute-start.19 = (f32[144,768]{1,0:T(8,128)S(1)}, f32[144,768]{1,0:T(8,128)S(1)}, u32[]{:S(2)}, u32[]{:S(2)}) collective-permute-start(f32[144,768]{1,0:T(8,128)S(1)} %get-tuple-element.143), channel_id=1, source_target_pairs={{0,48},{16,0},{32,16},{48,32},{1,49},{17,1},{33,17},{49,33},{2,50}... | collective-permute-start | bytes 1327112 | tf_op jit(solution)/shard_map/ppermute | solution.py:376
  103.3 3.2 %all-to-all-done.1.mine_ref = f32[8,144,128]{2,1,0:T(8,128)S(1)} async-done(((f32[8,144,128]{2,1,0:T(8,128)}), f32[8,144,128]{2,1,0:T(8,128)S(1)}, u32[]{:S(2)}, u32[]{:S(2)}) %all-to-all-start.1) | async-done | bytes 589856 | tf_op jit(solution)/shard_map/all_to_all | solution.py:411
  106.5 7.1 %collective-permute-done.18.x2_ref = f32[144,768]{1,0:T(8,128)S(1)} collective-permute-done((f32[144,768]{1,0:T(8,128)}, f32[144,768]{1,0:T(8,128)S(1)}, u32[]{:S(2)}, u32[]{:S(2)}) %collective-permute-start.18) | collective-permute-done | bytes 442400 | tf_op jit(solution)/shard_map/ppermute | solution.py:376
  113.6 5.5 %collective-permute-done.19.x3_ref = f32[144,768]{1,0:T(8,128)S(1)} collective-permute-done((f32[144,768]{1,0:T(8,128)S(1)}, f32[144,768]{1,0:T(8,128)S(1)}, u32[]{:S(2)}, u32[]{:S(2)}) %collective-permute-start.19) | collective-permute-done | bytes 442400 | tf_op jit(solution)/shard_map/ppermute | solution.py:376
  119.1 5.2 %collective-permute-start.20 = (f32[8,144,128]{2,1,0:T(8,128)S(1)}, f32[8,144,128]{2,1,0:T(8,128)S(1)}, u32[]{:S(2)}, u32[]{:S(2)}) collective-permute-start(f32[8,144,128]{2,1,0:T(8,128)S(1)} %all-to-all-done.1.mine_ref), channel_id=1, source_target_pairs={{0,1},{1,0},{2,3},{3,2},{4,5},{5,4},{6,7},{7,6},{8,9},{9,8},{10,11... | collective-permute-start | bytes 1769480 | tf_op jit(solution)/shard_map/ppermute | solution.py:413
  125.0 1.4 copy-done
  126.4 5.8 %shard_map.51 = (f32[768,768]{1,0:T(8,128)S(1)}, f32[768,64]{1,0:T(8,128)S(1)}, f32[64,768]{1,0:T(8,128)S(1)}, f32[256,256]{1,0:T(8,128)S(1)}, f32[256,768]{1,0:...) custom-call(s32[4]{0:T(128)S(1)} %pad_add_fusion.ids, ...), custom_call_target="tpu_custom_call" | custom-call | bytes 8192 | tf_op jit(solution)/shard_map/pallas_call | solution.py:356
  132.3 7.1 %shard_map.52 = f32[768,768]{1,0:T(8,128)} custom-call(s32[4]{0:T(128)S(1)} %pad_add_fusion.ids, s32[256,8]{1,0:T(8,128)S(1)} %get-tuple-element.122.ic_ref, f32[8,144,128]{2,1,0:T(8,128)S(1)} %all-to-all-done.1.mine_ref, f32[8,144,128]{2,1,0:T(8,128)S(1)} %collective-permute-done.20.there_ref, f32[768,768]{1,0:T(8,128)S(1)} %get-tuple-element.151.base_ref, ...), custom_call_target="tpu_custom_call" | custom-call | bytes 8192 | tf_op jit(solution)/shard_map/pallas_call | solution.py:356
  (37 shorter events, 10.3 us)
Async XLA Ops:
  11.7 38.5 %all-to-all-start = ((f32[32,5,2,768]{3,2,1,0:T(2,128)}), f32[32,5,2,768]{3,2,1,0:T(2,128)S(1)}, u32[]{:S(2)}, u32[]{:S(2)}) async-start(f32[32,5,2,768]{3,2,1,0:T(2,128)} %get-tuple-element.124), calls=%async_computation | async-start | bytes 1966080 | tf_op jit(solution)/shard_map/all_to_all | solution.py:394
  25.4 93.7 %all-gather.2.cloned.1.call-start = ((), (), s32[]{:S(2)}) async-start(), calls=%async_computation.7 | async-start | bytes 1671168 | tf_op jit(solution)/shard_map/all_gather | solution.py:399
  25.5 12.7 %collective-permute-start = (f32[96,256]{1,0:T(8,128)S(1)}, f32[96,256]{1,0:T(8,128)S(1)}, u32[]{:S(2)}, u32[]{:S(2)}) collective-permute-start(f32[96,256]{1,0:T(8,128)S(1)} %get-tuple-element.126), channel_id=1, source_target_pairs={{0,8},{1,9},{16,24},{17,25},{32,40},{33,41},{48,56},{49,57},{64,72... | collective-permute-start | bytes 294920 | tf_op jit(solution)/shard_map/ppermute | solution.py:397
  32.9 6.5 %collective-permute-start.1 = (f32[96,256]{1,0:T(8,128)S(1)}, f32[96,256]{1,0:T(8,128)S(1)}, u32[]{:S(2)}, u32[]{:S(2)}) collective-permute-start(f32[96,256]{1,0:T(8,128)S(1)} %get-tuple-element.127), channel_id=1, source_target_pairs={{0,6},{1,7},{16,22},{17,23},{32,38},{33,39},{48,54},{49,55},{64,70... | collective-permute-start | bytes 294920 | tf_op jit(solution)/shard_map/ppermute | solution.py:397
  34.2 6.5 %collective-permute-start.2 = (f32[96,256]{1,0:T(8,128)S(1)}, f32[96,256]{1,0:T(8,128)S(1)}, u32[]{:S(2)}, u32[]{:S(2)}) collective-permute-start(f32[96,256]{1,0:T(8,128)S(1)} %get-tuple-element.128), channel_id=1, source_target_pairs={{0,10},{1,11},{16,26},{17,27},{32,42},{33,43},{48,58},{49,59},{64,... | collective-permute-start | bytes 294920 | tf_op jit(solution)/shard_map/ppermute | solution.py:397
  35.5 5.3 %collective-permute-start.3 = (f32[96,256]{1,0:T(8,128)S(1)}, f32[96,256]{1,0:T(8,128)S(1)}, u32[]{:S(2)}, u32[]{:S(2)}) collective-permute-start(f32[96,256]{1,0:T(8,128)S(1)} %get-tuple-element.129), channel_id=1, source_target_pairs={{0,4},{1,5},{16,20},{17,21},{32,36},{33,37},{48,52},{49,53},{64,68... | collective-permute-start | bytes 294920 | tf_op jit(solution)/shard_map/ppermute | solution.py:397
  36.8 4.0 %collective-permute-start.4 = (f32[96,256]{1,0:T(8,128)S(1)}, f32[96,256]{1,0:T(8,128)S(1)}, u32[]{:S(2)}, u32[]{:S(2)}) collective-permute-start(f32[96,256]{1,0:T(8,128)S(1)} %get-tuple-element.130), channel_id=1, source_target_pairs={{0,12},{1,13},{16,28},{17,29},{32,44},{33,45},{48,60},{49,61},{64,... | collective-permute-start | bytes 294920 | tf_op jit(solution)/shard_map/ppermute | solution.py:397
  38.2 2.9 %collective-permute-start.5 = (f32[96,256]{1,0:T(8,128)S(1)}, f32[96,256]{1,0:T(8,128)S(1)}, u32[]{:S(2)}, u32[]{:S(2)}) collective-permute-start(f32[96,256]{1,0:T(8,128)S(1)} %get-tuple-element.131), channel_id=1, source_target_pairs={{0,2},{1,3},{16,18},{17,19},{32,34},{33,35},{48,50},{49,51},{64,66... | collective-permute-start | bytes 294920 | tf_op jit(solution)/shard_map/ppermute | solution.py:397
  39.5 2.9 %collective-permute-start.6 = (f32[96,256]{1,0:T(8,128)S(1)}, f32[96,256]{1,0:T(8,128)S(1)}, u32[]{:S(2)}, u32[]{:S(2)}) collective-permute-start(f32[96,256]{1,0:T(8,128)S(1)} %get-tuple-element.132), channel_id=1, source_target_pairs={{0,14},{1,15},{16,30},{17,31},{32,46},{33,47},{48,62},{49,63},{64,... | collective-permute-start | bytes 294920 | tf_op jit(solution)/shard_map/ppermute | solution.py:397
  52.2 34.2 %all-to-all-start.2 = ((f32[8,24,768]{2,1,0:T(8,128)}), f32[8,24,768]{2,1,0:T(8,128)S(1)}, u32[]{:S(2)}, u32[]{:S(2)}) async-start(f32[8,24,768]{2,1,0:T(8,128)} %get-tuple-element.139), calls=%async_computation.2 | async-start | bytes 1179648 | tf_op jit(solution)/shard_map/all_to_all | solution.py:404
  56.2 10.5 %collective-permute-start.10 = (f32[80,256]{1,0:T(8,128)S(1)}, f32[80,256]{1,0:T(8,128)S(1)}, u32[]{:S(2)}, u32[]{:S(2)}) collective-permute-start(f32[80,256]{1,0:T(8,128)S(1)} %get-tuple-element.134.refs_0_), channel_id=1, source_target_pairs={{0,4},{1,5},{16,20},{17,21},{32,36},{33,37},{48,52},{49,53},{64,68... | collective-permute-start | bytes 245768 | tf_op jit(solution)/shard_map/ppermute | solution.py:405
  60.4 7.6 %collective-permute-start.11 = (f32[80,256]{1,0:T(8,128)S(1)}, f32[80,256]{1,0:T(8,128)S(1)}, u32[]{:S(2)}, u32[]{:S(2)}) collective-permute-start(f32[80,256]{1,0:T(8,128)S(1)} %get-tuple-element.134.refs_0_), channel_id=1, source_target_pairs={{0,12},{1,13},{16,28},{17,29},{32,44},{33,45},{48,60},{49,61},{64,... | collective-permute-start | bytes 245768 | tf_op jit(solution)/shard_map/ppermute | solution.py:405
  62.7 6.5 %collective-permute-start.12 = (f32[80,256]{1,0:T(8,128)S(1)}, f32[80,256]{1,0:T(8,128)S(1)}, u32[]{:S(2)}, u32[]{:S(2)}) collective-permute-start(f32[80,256]{1,0:T(8,128)S(1)} %get-tuple-element.134.refs_0_), channel_id=1, source_target_pairs={{0,2},{1,3},{16,18},{17,19},{32,34},{33,35},{48,50},{49,51},{64,66... | collective-permute-start | bytes 245768 | tf_op jit(solution)/shard_map/ppermute | solution.py:405
  64.0 5.2 %collective-permute-start.13 = (f32[80,256]{1,0:T(8,128)S(1)}, f32[80,256]{1,0:T(8,128)S(1)}, u32[]{:S(2)}, u32[]{:S(2)}) collective-permute-start(f32[80,256]{1,0:T(8,128)S(1)} %get-tuple-element.134.refs_0_), channel_id=1, source_target_pairs={{0,14},{1,15},{16,30},{17,31},{32,46},{33,47},{48,62},{49,63},{64,... | collective-permute-start | bytes 245768 | tf_op jit(solution)/shard_map/ppermute | solution.py:405
  65.3 4.0 %collective-permute-start.7 = (f32[80,256]{1,0:T(8,128)S(1)}, f32[80,256]{1,0:T(8,128)S(1)}, u32[]{:S(2)}, u32[]{:S(2)}) collective-permute-start(f32[80,256]{1,0:T(8,128)S(1)} %get-tuple-element.134.refs_0_), channel_id=1, source_target_pairs={{0,8},{1,9},{16,24},{17,25},{32,40},{33,41},{48,56},{49,57},{64,72... | collective-permute-start | bytes 245768 | tf_op jit(solution)/shard_map/ppermute | solution.py:405
  66.6 4.2 %collective-permute-start.8 = (f32[80,256]{1,0:T(8,128)S(1)}, f32[80,256]{1,0:T(8,128)S(1)}, u32[]{:S(2)}, u32[]{:S(2)}) collective-permute-start(f32[80,256]{1,0:T(8,128)S(1)} %get-tuple-element.134.refs_0_), channel_id=1, source_target_pairs={{0,6},{1,7},{16,22},{17,23},{32,38},{33,39},{48,54},{49,55},{64,70... | collective-permute-start | bytes 245768 | tf_op jit(solution)/shard_map/ppermute | solution.py:405
  68.0 3.8 %collective-permute-start.9 = (f32[80,256]{1,0:T(8,128)S(1)}, f32[80,256]{1,0:T(8,128)S(1)}, u32[]{:S(2)}, u32[]{:S(2)}) collective-permute-start(f32[80,256]{1,0:T(8,128)S(1)} %get-tuple-element.134.refs_0_), channel_id=1, source_target_pairs={{0,10},{1,11},{16,26},{17,27},{32,42},{33,43},{48,58},{49,59},{64,... | collective-permute-start | bytes 245768 | tf_op jit(solution)/shard_map/ppermute | solution.py:405
  72.4 10.9 %collective-permute-start.14 = (f32[64,128]{1,0:T(8,128)S(1)}, f32[64,128]{1,0:T(8,128)S(1)}, u32[]{:S(2)}, u32[]{:S(2)}) collective-permute-start(f32[64,128]{1,0:T(8,128)S(1)} %get-tuple-element.136), channel_id=1, source_target_pairs={{0,16},{16,32},{32,48},{48,0},{1,17},{17,33},{33,49},{49,1},{2,18}... | collective-permute-start | bytes 98312 | tf_op jit(solution)/shard_map/ppermute | solution.py:376
  76.8 6.5 %collective-permute-start.15 = (f32[64,128]{1,0:T(8,128)S(1)}, f32[64,128]{1,0:T(8,128)S(1)}, u32[]{:S(2)}, u32[]{:S(2)}) collective-permute-start(f32[64,128]{1,0:T(8,128)S(1)} %get-tuple-element.137), channel_id=1, source_target_pairs={{0,32},{16,48},{32,0},{48,16},{1,33},{17,49},{33,1},{49,17},{2,34}... | collective-permute-start | bytes 98312 | tf_op jit(solution)/shard_map/ppermute | solution.py:376
  80.5 5.1 %collective-permute-start.16 = (f32[64,128]{1,0:T(8,128)S(1)}, f32[64,128]{1,0:T(8,128)S(1)}, u32[]{:S(2)}, u32[]{:S(2)}) collective-permute-start(f32[64,128]{1,0:T(8,128)S(1)} %get-tuple-element.138), channel_id=1, source_target_pairs={{0,48},{16,0},{32,16},{48,32},{1,49},{17,1},{33,17},{49,33},{2,50}... | collective-permute-start | bytes 98312 | tf_op jit(solution)/shard_map/ppermute | solution.py:376
  86.5 20.0 %all-to-all-start.1 = ((f32[8,144,128]{2,1,0:T(8,128)}), f32[8,144,128]{2,1,0:T(8,128)S(1)}, u32[]{:S(2)}, u32[]{:S(2)}) async-start(f32[8,144,128]{2,1,0:T(8,128)} %shard_map.49), calls=%async_computation.1 | async-start | bytes 1179648 | tf_op jit(solution)/shard_map/all_to_all | solution.py:411
  94.6 11.9 %collective-permute-start.17 = (f32[144,768]{1,0:T(8,128)}, f32[144,768]{1,0:T(8,128)S(1)}, u32[]{:S(2)}, u32[]{:S(2)}) collective-permute-start(f32[144,768]{1,0:T(8,128)} %get-tuple-element.141), channel_id=1, source_target_pairs={{0,16},{16,32},{32,48},{48,0},{1,17},{17,33},{33,49},{49,1},{2,18}... | collective-permute-start | bytes 1327112 | tf_op jit(solution)/shard_map/ppermute | solution.py:376
  96.5 17.2 %collective-permute-start.18 = (f32[144,768]{1,0:T(8,128)}, f32[144,768]{1,0:T(8,128)S(1)}, u32[]{:S(2)}, u32[]{:S(2)}) collective-permute-start(f32[144,768]{1,0:T(8,128)} %get-tuple-element.142), channel_id=1, source_target_pairs={{0,32},{16,48},{32,0},{48,16},{1,33},{17,49},{33,1},{49,17},{2,34}... | collective-permute-start | bytes 1327112 | tf_op jit(solution)/shard_map/ppermute | solution.py:376
  101.3 17.8 %collective-permute-start.19 = (f32[144,768]{1,0:T(8,128)S(1)}, f32[144,768]{1,0:T(8,128)S(1)}, u32[]{:S(2)}, u32[]{:S(2)}) collective-permute-start(f32[144,768]{1,0:T(8,128)S(1)} %get-tuple-element.143), channel_id=1, source_target_pairs={{0,48},{16,0},{32,16},{48,32},{1,49},{17,1},{33,17},{49,33},{2,50}... | collective-permute-start | bytes 1327112 | tf_op jit(solution)/shard_map/ppermute | solution.py:376
  119.1 13.1 %collective-permute-start.20 = (f32[8,144,128]{2,1,0:T(8,128)S(1)}, f32[8,144,128]{2,1,0:T(8,128)S(1)}, u32[]{:S(2)}, u32[]{:S(2)}) collective-permute-start(f32[8,144,128]{2,1,0:T(8,128)S(1)} %all-to-all-done.1.mine_ref), channel_id=1, source_target_pairs={{0,1},{1,0},{2,3},{3,2},{4,5},{5,4},{6,7},{7,6},{8,9},{9,8},{10,11... | collective-permute-start | bytes 1769480 | tf_op jit(solution)/shard_map/ppermute | solution.py:413
  125.0 1.4 copy-start
  126.4 5.8 %copy-start.4 = (f32[2,256,256]{2,1,0:T(8,128)S(1)}, f32[2,256,256]{2,1,0:T(8,128)}, u32[]{:S(2)}) copy-start(f32[2,256,256]{2,1,0:T(8,128)} %ui_ref.3) | copy-start | bytes 1572868
  126.4 5.8 %copy-start.8 = (f32[2,256,256]{2,1,0:T(8,128)S(1)}, f32[2,256,256]{2,1,0:T(8,128)}, u32[]{:S(2)}) copy-start(f32[2,256,256]{2,1,0:T(8,128)} %li_ref.3) | copy-start | bytes 1572868
  132.2 7.1 %copy-start.11 = (s32[2,256]{1,0:T(2,128)S(1)}, s32[2,256]{1,0:T(2,128)}, u32[]{:S(2)}) copy-start(s32[2,256]{1,0:T(2,128)} %p_ref.1) | copy-start | bytes 6148
Sparse Core Ops, SparseCore 0:
  50.4 40.9 all-gather.1

commit v3 on v2

--- a/solution.py
+++ b/solution.py
@@ -164,7 +164,7 @@
         send_ref[m, 4] = ext[2 * m : 2 * m + 2]
 
 
-def turn_kernel(ids, ir_ref, ic_ref, in_ref, send_ref, side_ref, old_ref, ext_ref):
+def turn_kernel(ids, ir_ref, ic_ref, in_ref, send_ref, old_ref, ext_ref):
     me = ids[0]
     for q in range(4):
         old_ref[2 * q : 2 * q + 2, :] = in_ref[0, q]
@@ -194,121 +194,123 @@
     for z in range(8):
         send_ref[z, 0:16, :] = slots
         send_ref[z, 16:24, :] = back[8 * z : 8 * z + 8]
-    side_ref[0:16, :] = slots[:, 0:NB]
-    side_ref[16:80, :] = back[:, 0:NB]
+
+
+def arrange(get, out_ref):
+    for x in range(4):
+        for z in range(8):
+            out_ref[x, 16 * z : 16 * z + 16, :] = get(z, 0, 16)
+            out_ref[x, 128 + 2 * z : 130 + 2 * z, :] = get(z, 16 + 2 * x, 18 + 2 * x)
+
+
+def mid_kernel(in_ref, out_ref, side_ref):
+    arrange(lambda z, a, b: in_ref[z, a:b, :], out_ref)
+    for z in range(8):
+        side_ref[24 * z : 24 * z + 24, :] = in_ref[z, :, 0:NB]
 
 
 def side_kernel(ids, *refs):
-    own, outs, sums = refs[0], refs[8:12], refs[12]
+    own, out, sums = refs[0], refs[8], refs[9]
     total = jnp.where(ids[2] == 0, own[...], F32(0.0))
     for r in refs[1:8]:
         total = total + r[...]
     sums[...] = total
-    for s, out in enumerate(outs):
-        to = (ids[0] + s) & 3
-        for h in range(2):
-            cut = slice(128 * h, 128 * h + 128)
-            out[16 * h : 16 * h + 16, :] = sums[0:16, cut]
-            for z in range(8):
-                back = sums[16 + 8 * z : 18 + 8 * z, cut]
-                for x in range(1, 4):
-                    at = 16 + 8 * z + 2 * x
-                    back = jnp.where(to == x, sums[at : at + 2, cut], back)
-                at = 32 + 16 * h + 2 * z
-                out[at : at + 2, :] = back
-
-
-def join_kernel(*refs):
-    blocks, out = refs[:4], refs[4]
-    for z in range(8):
-        for s, block in enumerate(blocks):
-            for h in range(2):
-                out[z, 64 * h + 16 * s : 64 * h + 16 * s + 16, :] = block[16 * h : 16 * h + 16, :]
-                at = 32 + 16 * h + 2 * z
-                out[z, 128 + 8 * h + 2 * s : 130 + 8 * h + 2 * s, :] = block[at : at + 2, :]
-
-
-def mid_kernel(ids, in_ref, *out_refs):
-    for s, out_ref in enumerate(out_refs):
-        to = (ids[0] + s) & 3
-        for z in range(8):
-            out_ref[16 * z : 16 * z + 16, :] = in_ref[z, 0:16, :]
-            back = in_ref[z, 16:18, :]
-            for x in range(1, 4):
-                back = jnp.where(to == x, in_ref[z, 16 + 2 * x : 18 + 2 * x, :], back)
-            out_ref[128 + 2 * z : 130 + 2 * z, :] = back
-
-
-def main_kernel(
-    ids, ir_ref, ic_ref, a_ref, x0_ref, x1_ref, x2_ref, x3_ref, li_ref, ui_ref, raw_ref,
-    base_ref, put_ref, back_ref, new0_ref, new1_ref, u0_ref, low0_ref, end1_ref, held_ref, sem,
-):
+    arrange(lambda z, a, b: sums[24 * z + a : 24 * z + b, :], out)
+
+
+KEPT = {
+    "base": (RD, RD), "new1": (NB, RD), "u0": (NB, RD), "low0": (RD, NB), "end1": (RD, NB),
+    "put": (RD, 2 * NP), "back": (2 * NP, RD), "new0": (NB, NB),
+}
+
+
+def main_kernel(ids, ir_ref, ic_ref, a_ref, x_ref, li_ref, ui_ref, raw_ref, *refs):
     me = ids[0]
-    fetch = pltpu.make_async_copy(raw_ref, held_ref, sem)
-    fetch.start()
+    count = len(KEPT)
+    held_ref, here_ref, fetch_sem, store_sem = refs[2 * count :]
+    far = dict(zip(KEPT, refs[:count]))
+    near = dict(zip(KEPT, refs[count : 2 * count]))
+    fetches = [
+        pltpu.make_async_copy(raw_ref, held_ref, fetch_sem.at[0]),
+        pltpu.make_async_copy(a_ref, here_ref, fetch_sem.at[1]),
+    ]
+    for fetch in fetches:
+        fetch.start()
+    stores = []
+
+    def keep(name, value=None):
+        if value is not None:
+            near[name][...] = value
+        stores.append(pltpu.make_async_copy(near[name], far[name], store_sem.at[len(stores)]))
+        stores[-1].start()
+
     put = jnp.zeros((RD, 2 * NP), F32)
     lane = iota((NB, 2 * NP), 1)
-    m = (lane >> 3) * 4 + ((me - ((lane >> 1) & 3)) & 3)
+    m = ((lane >> 1) & 7) * 4 + (lane >> 4)
     for g in range(2):
         own, loc = ir_ref[3 * g + 1 : 3 * g + 2, :], ir_ref[3 * g + 2 : 3 * g + 3, :]
         t = f((own == me) & (loc == iota((RD, NB), 0)))
         s = f(((ic_ref[:, 3 * g : 3 * g + 1] & 31) == m) & ((lane & 1) == g))
         put = put + bdot(t.astype(BF16), s.astype(BF16))
-    put_ref[...] = put
-    blocks = (x0_ref, x1_ref, x2_ref, x3_ref)
-    slots = jnp.concatenate([r[0:128, :] for r in blocks], axis=0)
-    for z in range(8):
-        for s in range(4):
-            at = 8 * z + 2 * s
-            back_ref[at : at + 2, :] = blocks[s][128 + 2 * z : 130 + 2 * z, :]
-    lane = iota((NB, 2 * NB), 1)
-    slot = ((me - (lane >> 7)) & 3) * 128 + (lane & 127)
+    keep("put", put)
+    keep("back", jnp.concatenate([x_ref[x, 128:144, :] for x in range(4)], axis=0))
+    slots = jnp.concatenate([x_ref[x, 0:128, :] for x in range(4)], axis=0)
+    slot = iota((NB, 2 * NB), 1)
     new0 = pick2(f(ic_ref[:, 6:7] == slot), slots)
-    new1_ref[...] = pick2(f(ic_ref[:, 7:8] == slot), slots)
-    new0_ref[...] = new0[:, 0:NB]
+    keep("new0", new0[:, 0:NB])
+    keep("new1", pick2(f(ic_ref[:, 7:8] == slot), slots))
     u0 = dot3(li_ref[0], new0)
-    u0_ref[...] = u0
-    fetch.wait()
-    for n, out in enumerate((low0_ref, end1_ref)):
+    keep("u0", u0)
+    fetches[0].wait()
+    for n, name in enumerate(("low0", "end1")):
         raw = jnp.concatenate([held_ref[y, n] for y in range(8)], axis=0)
-        out[...] = dot3(raw, ui_ref[n])
+        keep(name, dot3(raw, ui_ref[n]))
+    fetches[1].wait()
     for r in range(3):
         rows = pl.ds(NB * r, NB)
-        base_ref[rows, :] = a_ref[rows, :] - dot3(low0_ref[rows, :], u0)
-
-
-def final_kernel(
-    ids, ic_ref, mine_ref, there_ref, base_ref, put_ref, back_ref, new0_ref, new1_ref, u0_ref,
-    low0_ref, end1_ref, li_ref, ui_ref, out_ref, done_ref, slots_ref, rows_ref, sem,
-):
+        near["base"][rows, :] = here_ref[rows, :] - dot3(near["low0"][rows, :], u0)
+    keep("base")
+    for store in stores:
+        store.wait()
+
+
+def final_kernel(ids, ic_ref, mine_ref, there_ref, li_ref, ui_ref, *refs):
     me, col, core = ids[0], ids[1], ids[3]
-    for z in range(8):
-        mine, there = mine_ref[z], there_ref[z]
-        for k in range(2):
-            got = jnp.where(core == k, mine, there)
-            for h in range(2):
-                cut = slice(128 * h, 128 * h + 128)
-                slots_ref[k, 64 * z : 64 * z + 64, cut] = got[64 * h : 64 * h + 64]
-                rows_ref[k, 8 * z : 8 * z + 8, cut] = got[128 + 8 * h : 136 + 8 * h]
-    u0 = u0_ref[...]
-    lane = iota((NB, 2 * NB), 1)
-    slot = ((me - (lane >> 4)) & 3) * 128 + (lane >> 6) * 16 + (lane & 15)
-    diag = dot3(pick2(f(ic_ref[:, 7:8] == slot), slots_ref[0]), ui_ref[0])
-    next1 = new1_ref[...] - dot3(diag, u0)
+    count = len(KEPT)
+    out_ref, done_ref, sem, fetch_sem = refs[count], *refs[2 * count + 1 :]
+    near = dict(zip(KEPT, refs[count + 1 : 2 * count + 1]))
+    fetches = {}
+    order = ("u0", "new1", "back", "low0", "end1", "put", "base", "new0")
+    for n, name in enumerate(order):
+        far = refs[list(KEPT).index(name)]
+        fetches[name] = pltpu.make_async_copy(far, near[name], fetch_sem.at[n])
+        fetches[name].start()
+    mine, there = mine_ref[...], there_ref[...]
+    sides = [jnp.where(core == k, mine, there) for k in range(2)]
+    slots = [jnp.concatenate([v[x, 0:128] for x in range(4)], axis=0) for v in sides]
+    rows_back = [jnp.concatenate([v[x, 128:144] for x in range(4)], axis=0) for v in sides]
+    slot = iota((NB, 2 * NB), 1)
+    diag = dot3(pick2(f(ic_ref[:, 7:8] == slot), slots[0]), ui_ref[0])
+    new0_c1 = pick2(f(ic_ref[:, 6:7] == slot), slots[1])
+    fill = dot3(dot3(li_ref[0], new0_c1), ui_ref[1])
+    low0_back = dot3(rows_back[0], ui_ref[0])
+    low1_back = dot3(rows_back[1], ui_ref[1]) - dot3(low0_back, fill)
+    for name in order[:3]:
+        fetches[name].wait()
+    u0 = near["u0"][...]
+    next1 = near["new1"][...] - dot3(diag, u0)
     u1 = dot3(li_ref[1], next1)
-    new0_c1 = pick2(f(ic_ref[:, 6:7] == slot), slots_ref[1])
-    fill = dot3(dot3(li_ref[0], new0_c1), ui_ref[1])
-    low0_back = dot3(rows_ref[0], ui_ref[0])
-    low1_back = dot3(rows_ref[1], ui_ref[1]) - dot3(low0_back, fill)
-    back = back_ref[...] - dot3(low0_back, u0) - dot3(low1_back, u1)
+    back = near["back"][...] - dot3(low0_back, u0) - dot3(low1_back, u1)
+    for name in order[3:]:
+        fetches[name].wait()
     copies = []
     for r in (2, 1, 0):
         rows = pl.ds(NB * r, NB)
-        put = put_ref[rows, :]
+        put = near["put"][rows, :]
         moved = sum_cols(put) > 0
-        low0 = low0_ref[rows, :]
-        low1 = end1_ref[rows, :] - dot3(low0, fill)
-        done_ref[rows, :] = jnp.where(moved, pick2(put, back), base_ref[rows, :] - dot3(low1, u1))
+        low0 = near["low0"][rows, :]
+        low1 = near["end1"][rows, :] - dot3(low0, fill)
+        done_ref[rows, :] = jnp.where(moved, pick2(put, back), near["base"][rows, :] - dot3(low1, u1))
 
         @pl.when(col == 0)
         def _():
@@ -326,7 +328,7 @@
 
                 @pl.when(col == 0)
                 def _():
-                    done_ref[0:NB, 0:NB] = new0_ref[...]
+                    done_ref[0:NB, 0:NB] = near["new0"][...]
 
             @pl.when(me == 1)
             def _():
@@ -359,7 +361,7 @@
         in_specs=smem + [anywhere if n in far else vmem for n in range(len(args))],
         out_specs=jax.tree.map(lambda o: SCALAR if o.shape == (1,) else anywhere if far_out else vmem, outs),
         scratch_shapes=scratch,
-        compiler_params=pltpu.CompilerParams(vmem_limit_bytes=40 * 1024 * 1024),
+        compiler_params=pltpu.CompilerParams(vmem_limit_bytes=(60 if far_out else 40) * 1024 * 1024),
         cost_estimate=pl.CostEstimate(flops=flops, bytes_accessed=min(sizes), transcendentals=0),
     )(*([] if ids is None else [ids]), *args)
 
@@ -369,12 +371,6 @@
 
 
 AROUND = (4, 3, 5, 2, 6, 1, 7)
-
-
-def along_x(blocks):
-    return [blocks[0]] + [
-        lax.ppermute(blocks[s], "x", [(i, (i + s) % 4) for i in range(4)]) for s in range(1, 4)
-    ]
 
 
 def fast(matrix, pivots, lower_inv, upper_inv):
@@ -397,35 +393,36 @@
         piece = piece + lax.ppermute(panel[k], "y", [(0, k)])
     rows_in, piece = lax.optimization_barrier((rows_in, piece))
     raw = lax.all_gather(piece, PCOL, tiled=True).reshape(8, 2, part, NB)
-    send, side = call(
-        turn_kernel, (shape(8, 24, RD), shape(80, NB)), ids, ir, ic, rows_in,
-        scratch=[pltpu.VMEM((16, RD), F32), pltpu.VMEM((2 * NP, RD), F32)], flops=10**6,
+    send = call(
+        turn_kernel, shape(8, 24, RD), ids, ir, ic, rows_in,
+        scratch=[pltpu.VMEM((16, RD), F32), pltpu.VMEM((2 * NP, RD), F32)],
     )
     main_z = lax.all_to_all(send, "z", 0, 0)
+    main_send, side = call(mid_kernel, (shape(4, 144, RD), shape(192, NB)), None, main_z)
+    main_x = lax.all_to_all(main_send, "x", 0, 0)
     parts = [lax.ppermute(side, "y", [(0, k)]) for k in AROUND]
     side_send = call(
-        side_kernel, [shape(64, 128)] * 4, ids, side, *parts, scratch=[pltpu.VMEM((80, NB), F32)]
-    )
-    side_x = along_x(side_send)
-    main_x = along_x(call(mid_kernel, [shape(144, RD)] * 4, ids, main_z))
-    mine = lax.all_to_all(call(join_kernel, shape(8, 144, 128), None, *side_x), "z", 0, 0)
-    mine, main_x, raw = lax.optimization_barrier((mine, main_x, raw))
+        side_kernel, shape(4, 144, NB), ids, side, *parts, scratch=[pltpu.VMEM((192, NB), F32)]
+    )
+    side_send, main_x, raw = lax.optimization_barrier((side_send, main_x, raw))
+    mine = lax.all_to_all(side_send, "x", 0, 0)
+    near = [pltpu.VMEM(dims, F32) for dims in KEPT.values()]
+    kept = call(
+        main_kernel, [shape(*dims) for dims in KEPT.values()],
+        ids, ir, ic, matrix, main_x, lower_inv, upper_inv, raw, far=(2, 6), far_out=True,
+        scratch=near + [
+            pltpu.VMEM((8, 2, part, NB), F32), pltpu.VMEM((RD, RD), F32),
+            pltpu.SemaphoreType.DMA((2,)), pltpu.SemaphoreType.DMA((len(KEPT),)),
+        ],
+    )
+    mine, kept = lax.optimization_barrier((mine, kept))
     there = lax.ppermute(mine, "core", [(0, 1), (1, 0)])
-    base, put, back, new0, new1, u0, low0, end1 = call(
-        main_kernel,
-        (
-            shape(RD, RD), shape(RD, 2 * NP), shape(2 * NP, RD), shape(NB, NB), shape(NB, RD),
-            shape(NB, RD), shape(RD, NB), shape(RD, NB),
-        ),
-        ids, ir, ic, matrix, *main_x, lower_inv, upper_inv, raw, far=(9,),
-        scratch=[pltpu.VMEM((8, 2, part, NB), F32), pltpu.SemaphoreType.DMA],
-    )
     out = call(
-        final_kernel, shape(RD, RD), ids, ic, mine, there, base, put, back, new0, new1, u0,
-        low0, end1, lower_inv, upper_inv, far_out=True,
-        scratch=[
-            pltpu.VMEM((RD, RD), F32), pltpu.VMEM((2, 2 * NB, NB), F32),
-            pltpu.VMEM((2, 2 * NP, NB), F32), pltpu.SemaphoreType.DMA((3,)),
+        final_kernel, shape(RD, RD), ids, ic, mine, there, lower_inv, upper_inv, *kept,
+        far=tuple(range(5, 5 + len(KEPT))), far_out=True,
+        scratch=near + [
+            pltpu.VMEM((RD, RD), F32), pltpu.SemaphoreType.DMA((3,)),
+            pltpu.SemaphoreType.DMA((len(KEPT),)),
         ],
     )
     return out, most[0]

time: 147 us -> 137 us (0.932)
  blocking collectives: 0 us -> 18.9 us
  starting transfers between devices: 77 us -> 58.7 us
  waiting for transfers between devices: 29.4 us -> 17.8 us
  Pallas kernels: 23.2 us -> 24.8 us
    ppermute x6 -> x0, starting transfers between devices: 19.5 us -> none  [along_x(): lax.ppermute(blocks[s], 'x', [(i, (i + s) % 4) for i in range(4)])]
    all_to_all x0 -> x1, blocking collectives: none -> 18.9 us  [fast(): main_z = lax.all_to_all(send, 'z', 0, 0)]
    ppermute x6 -> x0, waiting for transfers between devices: 15 us -> none  [along_x(): lax.ppermute(blocks[s], 'x', [(i, (i + s) % 4) for i in range(4)])]
    ppermute x7, waiting for transfers between devices: 2.47 us -> 7.95 us  [fast(): parts = [lax.ppermute(side, 'y', [(0, k)]) for k in AROUND]]
    all_to_all x2, waiting for transfers between devices: 3.24 us -> 0.15 us  [the longest x1 0.14 us: fast(): mine = lax.all_to_all(side_send, 'x', 0, 0)]
    pallas_call x7 -> x6, Pallas kernels: 23.2 us -> 24.8 us  [call(): pl.pallas_call(kernel, out_shape=outs, in_specs=smem + [anywhere if n in...]
  transfers between devices with their start and end apart: 25 -> 19, of which waited for: 9 -> 8; matrix products, arithmetic and copies ran while one was open for 0% -> 1% of each run, Pallas kernels for 8% -> 8%
where the time goes in v3:
time: 137 us; the launch traced here: 136 us
  starting transfers between devices  58.7 us (43%)
  Pallas kernels  24.8 us (18%)
  blocking collectives  18.9 us (14%)
  waiting for transfers between devices  17.8 us (13%)
  between operations  14.3 us (10%)
    pallas_call x6, Pallas kernels, call(): pl.pallas_call(kernel, out_shape=outs, in_specs=smem + [anywhere if n in...  24.8 us
    all_to_all x1, blocking collectives, fast(): main_z = lax.all_to_all(send, 'z', 0, 0)  18.9 us
    ppermute x7, starting transfers between devices, fast(): piece = piece + lax.ppermute(panel[k], 'y', [(0, k)])  15.2 us
    all_to_all x1, starting transfers between devices, fast(): rows_in = lax.all_to_all(rows, PROW, 0, 0)  13.7 us
    ppermute x7, starting transfers between devices, fast(): parts = [lax.ppermute(side, 'y', [(0, k)]) for k in AROUND]  13.1 us
    ppermute x7, waiting for transfers between devices, fast(): parts = [lax.ppermute(side, 'y', [(0, k)]) for k in AROUND]  7.95 us
    all_to_all x1, waiting for transfers between devices, fast(): rows_in = lax.all_to_all(rows, PROW, 0, 0)  7.13 us
    ppermute x1, starting transfers between devices, fast(): there = lax.ppermute(mine, 'core', [(0, 1), (1, 0)])  6.64 us
  transfers between devices with their start and end apart: 19, of which 8 were waited for; matrix products, arithmetic and copies ran while one was open for 1% of the time, Pallas kernels for 8%

profile of v3, /device:TPU:1, one launch (start us, length us, event | category | flops | bytes accessed | tf_op | source)
XLA Modules:
  0.0 136.3 jit_solution(13280671552861381931)
XLA Ops:
  6.6 5.1 %shard_map.46 = (f32[32,5,2,768]{3,2,1,0:T(2,128)}, s32[8,256]{1,0:T(8,128)S(1)}, s32[256,8]{1,0:T(8,128)S(1)}, s32[1]{0:T(128)}, f32[96,256]{1,0:T(8,128)S(1)},...) custom-call(s32[4]{0:T(128)S(1)} %pad_add_fusion.ids, ...), custom_call_target="tpu_custom_call" | custom-call | flops 1000000 | bytes 4 | tf_op jit(solution)/shard_map/pallas_call | solution.py:358
  11.7 13.7 %all-to-all-start = ((f32[32,5,2,768]{3,2,1,0:T(2,128)}), f32[32,5,2,768]{3,2,1,0:T(2,128)S(1)}, u32[]{:S(2)}, u32[]{:S(2)}) async-start(f32[32,5,2,768]{3,2,1,0:T(2,128)} %get-tuple-element.122), calls=%async_computation | async-start | bytes 1966080 | tf_op jit(solution)/shard_map/all_to_all | solution.py:390
  25.5 7.5 %collective-permute-start = (f32[96,256]{1,0:T(8,128)S(1)}, f32[96,256]{1,0:T(8,128)S(1)}, u32[]{:S(2)}, u32[]{:S(2)}) collective-permute-start(f32[96,256]{1,0:T(8,128)S(1)} %get-tuple-element.124), channel_id=1, source_target_pairs={{0,8},{1,9},{16,24},{17,25},{32,40},{33,41},{48,56},{49,57},{64,72... | collective-permute-start | bytes 294920 | tf_op jit(solution)/shard_map/ppermute | solution.py:393
  33.0 1.3 collective-permute-start.1
  34.3 1.3 collective-permute-start.2
  35.6 1.3 collective-permute-start.3
  36.9 1.3 collective-permute-start.4
  38.2 1.3 collective-permute-start.5
  39.5 1.3 collective-permute-start.6
  41.1 1.3 collective-permute-done.6
  43.1 7.1 %all-to-all-done.in_ref = f32[32,5,2,768]{3,2,1,0:T(2,128)S(1)} async-done(((f32[32,5,2,768]{3,2,1,0:T(2,128)}), f32[32,5,2,768]{3,2,1,0:T(2,128)S(1)}, u32[]{:S(2)}, u32[]{:S(2)}) %all-to-all-start) | async-done | bytes 983072 | tf_op jit(solution)/shard_map/all_to_all | solution.py:390
  50.3 1.1 shard_map.47
  51.4 18.9 %all_to_all.20.in_ref = f32[8,24,768]{2,1,0:T(8,128)S(1)} all-to-all(f32[8,24,768]{2,1,0:T(8,128)S(1)} %shard_map.47), channel_id=1, replica_groups=mesh['z'=8,'x'=4,'y'=8,'core'=2] {'z'}, dimensions={0} | all-to-all | bytes 1179648 | tf_op jit(solution)/shard_map/all_to_all | solution.py:400
  70.3 1.4 %shard_map.48 = (f32[4,144,768]{2,1,0:T(8,128)}, f32[192,256]{1,0:T(8,128)S(1)}) custom-call(f32[8,24,768]{2,1,0:T(8,128)S(1)} %all_to_all.20.in_ref), custom_call_target="tpu_custom_call" | custom-call | bytes 196608 | tf_op jit(solution)/shard_map/pallas_call | solution.py:358
  71.7 5.0 %all-to-all-start.2 = ((f32[4,144,768]{2,1,0:T(8,128)}), f32[4,144,768]{2,1,0:T(8,128)}, u32[]{:S(2)}, u32[]{:S(2)}) async-start(f32[4,144,768]{2,1,0:T(8,128)} %get-tuple-element.133), calls=%async_computation.2 | async-start | bytes 3538944 | tf_op jit(solution)/shard_map/all_to_all | solution.py:402
  76.7 5.3 %collective-permute-start.13 = (f32[192,256]{1,0:T(8,128)S(1)}, f32[192,256]{1,0:T(8,128)S(1)}, u32[]{:S(2)}, u32[]{:S(2)}) collective-permute-start(f32[192,256]{1,0:T(8,128)S(1)} %get-tuple-element.132.refs_0_), channel_id=1, source_target_pairs={{0,14},{1,15},{16,30},{17,31},{32,46},{33,47},{48,62},{49,63},{64,... | collective-permute-start | bytes 589832 | tf_op jit(solution)/shard_map/ppermute | solution.py:403
  82.0 1.3 collective-permute-start.12
  83.3 1.3 collective-permute-start.11
  84.6 1.3 collective-permute-start.10
  85.9 1.3 collective-permute-start.9
  87.2 1.3 collective-permute-start.8
  88.6 1.3 collective-permute-start.7
  89.9 2.9 %collective-permute-done.9.refs_3_ = f32[192,256]{1,0:T(8,128)S(1)} collective-permute-done((f32[192,256]{1,0:T(8,128)S(1)}, f32[192,256]{1,0:T(8,128)S(1)}, u32[]{:S(2)}, u32[]{:S(2)}) %collective-permute-start.9) | collective-permute-done | bytes 196640 | tf_op jit(solution)/shard_map/ppermute | solution.py:403
  92.8 0.9 collective-permute-done.8.refs_2_
  93.6 4.2 %collective-permute-done.7.refs_1_ = f32[192,256]{1,0:T(8,128)S(1)} collective-permute-done((f32[192,256]{1,0:T(8,128)S(1)}, f32[192,256]{1,0:T(8,128)S(1)}, u32[]{:S(2)}, u32[]{:S(2)}) %collective-permute-start.7) | collective-permute-done | bytes 196640 | tf_op jit(solution)/shard_map/ppermute | solution.py:403
  97.8 1.5 %shard_map.49 = f32[4,144,256]{2,1,0:T(8,128)} custom-call(s32[4]{0:T(128)S(1)} %pad_add_fusion.ids, f32[192,256]{1,0:T(8,128)S(1)} %get-tuple-element.132.refs_0_, f32[192,256]{1,0:T(8,128)S(1)} %collective-permute-done.7.refs_1_, f32[192,256]{1,0:T(8,128)S(1)} %collective-permute-done.8.refs_2_, f32[192,256]{1,0:T(8,128)S(1)} %collective-permute-done.9.refs_3_, ...), custom_call_target="tpu_custom_call" | custom-call | bytes 196608 | tf_op jit(solution)/shard_map/pallas_call | solution.py:358
  99.3 5.0 %all-to-all-start.3 = ((f32[4,144,256]{2,1,0:T(8,128)}), f32[4,144,256]{2,1,0:T(8,128)S(1)}, u32[]{:S(2)}, u32[]{:S(2)}) async-start(f32[4,144,256]{2,1,0:T(8,128)} %shard_map.49), calls=%async_computation.3 | async-start | bytes 1179648 | tf_op jit(solution)/shard_map/all_to_all | solution.py:408
  104.3 7.1 %shard_map.50 = (f32[768,768]{1,0:T(8,128)}, f32[256,768]{1,0:T(8,128)}, f32[256,768]{1,0:T(8,128)}, f32[768,256]{1,0:T(8,128)}, f32[768,256]{1,0:T(8,128)}, /*i...) custom-call(s32[4]{0:T(128)} %copy-done.2, s32[8,256]{1,0:T(8,128)} %copy-done.1, s32[256,8]{1,0:T(8,128)} %copy-done, ...), custom_call_target="tpu_custom_call" | custom-call | bytes 8192 | tf_op jit(solution)/shard_map/pallas_call | solution.py:358
  111.6 6.6 %collective-permute-start.14 = (f32[4,144,256]{2,1,0:T(8,128)S(1)}, f32[4,144,256]{2,1,0:T(8,128)S(1)}, u32[]{:S(2)}, u32[]{:S(2)}) collective-permute-start(f32[4,144,256]{2,1,0:T(8,128)S(1)} %all-to-all-done.3.mine_ref), channel_id=1, source_target_pairs={{0,1},{1,0},{2,3},{3,2},{4,5},{5,4},{6,7},{7,6},{8,9},{9,8},{10,11... | collective-permute-start | bytes 1769480 | tf_op jit(solution)/shard_map/ppermute | solution.py:419
  118.9 1.0 collective-permute-done.14.there_ref
  119.8 0.8 copy-done.10
  120.7 8.6 %shard_map.51 = f32[768,768]{1,0:T(8,128)} custom-call(s32[4]{0:T(128)} %copy-done.2, s32[256,8]{1,0:T(8,128)} %copy-done, f32[4,144,256]{2,1,0:T(8,128)} %copy-done.9, f32[4,144,256]{2,1,0:T(8,128)} %copy-done.10, f32[2,256,256]{2,1,0:T(8,128)} %li_ref.3, f32[2,256,256]{2,1,0:T(8,128)} %ui_ref.3, f32[768,768]{1,0:T(8,128)} %get-tuple-element.147.refs_0_, ...), custom_call_target="tpu_custom_call" | custom-call | bytes 8192 | tf_op jit(solution)/shard_map/pallas_call | solution.py:358
  (31 shorter events, 1.5 us)
Async XLA Ops:
  6.6 91.2 %copy-start.2 = (s32[4]{0:T(128)}, s32[4]{0:T(128)S(1)}, u32[]{:S(2)}) copy-start(s32[4]{0:T(128)S(1)} %pad_add_fusion.ids) | copy-start | bytes 52
  11.7 58.6 %copy-start = (s32[256,8]{1,0:T(8,128)}, s32[256,8]{1,0:T(8,128)S(1)}, u32[]{:S(2)}) copy-start(s32[256,8]{1,0:T(8,128)S(1)} %get-tuple-element.120.ic_ref) | copy-start | bytes 24580
  11.7 58.6 %copy-start.1 = (s32[8,256]{1,0:T(8,128)}, s32[8,256]{1,0:T(8,128)S(1)}, u32[]{:S(2)}) copy-start(s32[8,256]{1,0:T(8,128)S(1)} %get-tuple-element.121.ir_ref) | copy-start | bytes 24580
  11.7 38.5 %all-to-all-start = ((f32[32,5,2,768]{3,2,1,0:T(2,128)}), f32[32,5,2,768]{3,2,1,0:T(2,128)S(1)}, u32[]{:S(2)}, u32[]{:S(2)}) async-start(f32[32,5,2,768]{3,2,1,0:T(2,128)} %get-tuple-element.122), calls=%async_computation | async-start | bytes 1966080 | tf_op jit(solution)/shard_map/all_to_all | solution.py:390
  25.4 73.9 %all-gather.2.cloned.1.call-start = ((), (), s32[]{:S(2)}) async-start(), calls=%async_computation.8 | async-start | bytes 1671168 | tf_op jit(solution)/shard_map/all_gather | solution.py:395
  25.5 12.7 %collective-permute-start = (f32[96,256]{1,0:T(8,128)S(1)}, f32[96,256]{1,0:T(8,128)S(1)}, u32[]{:S(2)}, u32[]{:S(2)}) collective-permute-start(f32[96,256]{1,0:T(8,128)S(1)} %get-tuple-element.124), channel_id=1, source_target_pairs={{0,8},{1,9},{16,24},{17,25},{32,40},{33,41},{48,56},{49,57},{64,72... | collective-permute-start | bytes 294920 | tf_op jit(solution)/shard_map/ppermute | solution.py:393
  33.0 6.5 %collective-permute-start.1 = (f32[96,256]{1,0:T(8,128)S(1)}, f32[96,256]{1,0:T(8,128)S(1)}, u32[]{:S(2)}, u32[]{:S(2)}) collective-permute-start(f32[96,256]{1,0:T(8,128)S(1)} %get-tuple-element.125), channel_id=1, source_target_pairs={{0,6},{1,7},{16,22},{17,23},{32,38},{33,39},{48,54},{49,55},{64,70... | collective-permute-start | bytes 294920 | tf_op jit(solution)/shard_map/ppermute | solution.py:393
  34.3 6.5 %collective-permute-start.2 = (f32[96,256]{1,0:T(8,128)S(1)}, f32[96,256]{1,0:T(8,128)S(1)}, u32[]{:S(2)}, u32[]{:S(2)}) collective-permute-start(f32[96,256]{1,0:T(8,128)S(1)} %get-tuple-element.126), channel_id=1, source_target_pairs={{0,10},{1,11},{16,26},{17,27},{32,42},{33,43},{48,58},{49,59},{64,... | collective-permute-start | bytes 294920 | tf_op jit(solution)/shard_map/ppermute | solution.py:393
  35.6 5.3 %collective-permute-start.3 = (f32[96,256]{1,0:T(8,128)S(1)}, f32[96,256]{1,0:T(8,128)S(1)}, u32[]{:S(2)}, u32[]{:S(2)}) collective-permute-start(f32[96,256]{1,0:T(8,128)S(1)} %get-tuple-element.127), channel_id=1, source_target_pairs={{0,4},{1,5},{16,20},{17,21},{32,36},{33,37},{48,52},{49,53},{64,68... | collective-permute-start | bytes 294920 | tf_op jit(solution)/shard_map/ppermute | solution.py:393
  36.9 4.0 %collective-permute-start.4 = (f32[96,256]{1,0:T(8,128)S(1)}, f32[96,256]{1,0:T(8,128)S(1)}, u32[]{:S(2)}, u32[]{:S(2)}) collective-permute-start(f32[96,256]{1,0:T(8,128)S(1)} %get-tuple-element.128), channel_id=1, source_target_pairs={{0,12},{1,13},{16,28},{17,29},{32,44},{33,45},{48,60},{49,61},{64,... | collective-permute-start | bytes 294920 | tf_op jit(solution)/shard_map/ppermute | solution.py:393
  38.2 2.9 %collective-permute-start.5 = (f32[96,256]{1,0:T(8,128)S(1)}, f32[96,256]{1,0:T(8,128)S(1)}, u32[]{:S(2)}, u32[]{:S(2)}) collective-permute-start(f32[96,256]{1,0:T(8,128)S(1)} %get-tuple-element.129), channel_id=1, source_target_pairs={{0,2},{1,3},{16,18},{17,19},{32,34},{33,35},{48,50},{49,51},{64,66... | collective-permute-start | bytes 294920 | tf_op jit(solution)/shard_map/ppermute | solution.py:393
  39.5 2.9 %collective-permute-start.6 = (f32[96,256]{1,0:T(8,128)S(1)}, f32[96,256]{1,0:T(8,128)S(1)}, u32[]{:S(2)}, u32[]{:S(2)}) collective-permute-start(f32[96,256]{1,0:T(8,128)S(1)} %get-tuple-element.130), channel_id=1, source_target_pairs={{0,14},{1,15},{16,30},{17,31},{32,46},{33,47},{48,62},{49,63},{64,... | collective-permute-start | bytes 294920 | tf_op jit(solution)/shard_map/ppermute | solution.py:393
  71.7 27.6 %all-to-all-start.2 = ((f32[4,144,768]{2,1,0:T(8,128)}), f32[4,144,768]{2,1,0:T(8,128)}, u32[]{:S(2)}, u32[]{:S(2)}) async-start(f32[4,144,768]{2,1,0:T(8,128)} %get-tuple-element.133), calls=%async_computation.2 | async-start | bytes 3538944 | tf_op jit(solution)/shard_map/all_to_all | solution.py:402
  76.7 27.6 %copy-start.4 = (f32[768,768]{1,0:T(8,128)S(1)}, f32[768,768]{1,0:T(8,128)}, u32[]{:S(2)}) copy-start(f32[768,768]{1,0:T(8,128)} %a_ref.3) | copy-start | bytes 7077892
  76.7 10.6 %collective-permute-start.13 = (f32[192,256]{1,0:T(8,128)S(1)}, f32[192,256]{1,0:T(8,128)S(1)}, u32[]{:S(2)}, u32[]{:S(2)}) collective-permute-start(f32[192,256]{1,0:T(8,128)S(1)} %get-tuple-element.132.refs_0_), channel_id=1, source_target_pairs={{0,14},{1,15},{16,30},{17,31},{32,46},{33,47},{48,62},{49,63},{64,... | collective-permute-start | bytes 589832 | tf_op jit(solution)/shard_map/ppermute | solution.py:403
  82.0 6.6 %collective-permute-start.12 = (f32[192,256]{1,0:T(8,128)S(1)}, f32[192,256]{1,0:T(8,128)S(1)}, u32[]{:S(2)}, u32[]{:S(2)}) collective-permute-start(f32[192,256]{1,0:T(8,128)S(1)} %get-tuple-element.132.refs_0_), channel_id=1, source_target_pairs={{0,2},{1,3},{16,18},{17,19},{32,34},{33,35},{48,50},{49,51},{64,66... | collective-permute-start | bytes 589832 | tf_op jit(solution)/shard_map/ppermute | solution.py:403
  83.3 6.6 %collective-permute-start.11 = (f32[192,256]{1,0:T(8,128)S(1)}, f32[192,256]{1,0:T(8,128)S(1)}, u32[]{:S(2)}, u32[]{:S(2)}) collective-permute-start(f32[192,256]{1,0:T(8,128)S(1)} %get-tuple-element.132.refs_0_), channel_id=1, source_target_pairs={{0,12},{1,13},{16,28},{17,29},{32,44},{33,45},{48,60},{49,61},{64,... | collective-permute-start | bytes 589832 | tf_op jit(solution)/shard_map/ppermute | solution.py:403
  84.6 5.3 %collective-permute-start.10 = (f32[192,256]{1,0:T(8,128)S(1)}, f32[192,256]{1,0:T(8,128)S(1)}, u32[]{:S(2)}, u32[]{:S(2)}) collective-permute-start(f32[192,256]{1,0:T(8,128)S(1)} %get-tuple-element.132.refs_0_), channel_id=1, source_target_pairs={{0,4},{1,5},{16,20},{17,21},{32,36},{33,37},{48,52},{49,53},{64,68... | collective-permute-start | bytes 589832 | tf_op jit(solution)/shard_map/ppermute | solution.py:403
  85.9 6.8 %collective-permute-start.9 = (f32[192,256]{1,0:T(8,128)S(1)}, f32[192,256]{1,0:T(8,128)S(1)}, u32[]{:S(2)}, u32[]{:S(2)}) collective-permute-start(f32[192,256]{1,0:T(8,128)S(1)} %get-tuple-element.132.refs_0_), channel_id=1, source_target_pairs={{0,10},{1,11},{16,26},{17,27},{32,42},{33,43},{48,58},{49,59},{64,... | collective-permute-start | bytes 589832 | tf_op jit(solution)/shard_map/ppermute | solution.py:403
  87.2 6.4 %collective-permute-start.8 = (f32[192,256]{1,0:T(8,128)S(1)}, f32[192,256]{1,0:T(8,128)S(1)}, u32[]{:S(2)}, u32[]{:S(2)}) collective-permute-start(f32[192,256]{1,0:T(8,128)S(1)} %get-tuple-element.132.refs_0_), channel_id=1, source_target_pairs={{0,6},{1,7},{16,22},{17,23},{32,38},{33,39},{48,54},{49,55},{64,70... | collective-permute-start | bytes 589832 | tf_op jit(solution)/shard_map/ppermute | solution.py:403
  88.6 9.3 %collective-permute-start.7 = (f32[192,256]{1,0:T(8,128)S(1)}, f32[192,256]{1,0:T(8,128)S(1)}, u32[]{:S(2)}, u32[]{:S(2)}) collective-permute-start(f32[192,256]{1,0:T(8,128)S(1)} %get-tuple-element.132.refs_0_), channel_id=1, source_target_pairs={{0,8},{1,9},{16,24},{17,25},{32,40},{33,41},{48,56},{49,57},{64,72... | collective-permute-start | bytes 589832 | tf_op jit(solution)/shard_map/ppermute | solution.py:403
  99.3 12.2 %all-to-all-start.3 = ((f32[4,144,256]{2,1,0:T(8,128)}), f32[4,144,256]{2,1,0:T(8,128)S(1)}, u32[]{:S(2)}, u32[]{:S(2)}) async-start(f32[4,144,256]{2,1,0:T(8,128)} %shard_map.49), calls=%async_computation.3 | async-start | bytes 1179648 | tf_op jit(solution)/shard_map/all_to_all | solution.py:408
  111.6 8.3 %copy-start.9 = (f32[4,144,256]{2,1,0:T(8,128)}, f32[4,144,256]{2,1,0:T(8,128)S(1)}, u32[]{:S(2)}) copy-start(f32[4,144,256]{2,1,0:T(8,128)S(1)} %all-to-all-done.3.mine_ref) | copy-start | bytes 1769476
  111.6 8.3 %collective-permute-start.14 = (f32[4,144,256]{2,1,0:T(8,128)S(1)}, f32[4,144,256]{2,1,0:T(8,128)S(1)}, u32[]{:S(2)}, u32[]{:S(2)}) collective-permute-start(f32[4,144,256]{2,1,0:T(8,128)S(1)} %all-to-all-done.3.mine_ref), channel_id=1, source_target_pairs={{0,1},{1,0},{2,3},{3,2},{4,5},{5,4},{6,7},{7,6},{8,9},{9,8},{10,11... | collective-permute-start | bytes 1769480 | tf_op jit(solution)/shard_map/ppermute | solution.py:419
  118.8 10.4 %copy-start.11 = (s32[2,256]{1,0:T(2,128)S(1)}, s32[2,256]{1,0:T(2,128)}, u32[]{:S(2)}) copy-start(s32[2,256]{1,0:T(2,128)} %p_ref.1) | copy-start | bytes 6148
  119.8 0.8 copy-start.10
Sparse Core Ops, SparseCore 0:
  50.4 41.2 all-gather.1

commit v4 on v3

--- a/solution.py
+++ b/solution.py
@@ -219,8 +219,8 @@
 
 
 KEPT = {
-    "base": (RD, RD), "new1": (NB, RD), "u0": (NB, RD), "low0": (RD, NB), "end1": (RD, NB),
-    "put": (RD, 2 * NP), "back": (2 * NP, RD), "new0": (NB, NB),
+    "base": (RD, RD), "lead1": (NB, RD), "u0": (NB, RD), "low0": (RD, NB), "end1": (RD, NB),
+    "put": (RD, 2 * NP), "back": (2 * NP, RD), "new0": (NB, NB), "new1": (NB, NB),
 }
 
 
@@ -258,9 +258,11 @@
     slot = iota((NB, 2 * NB), 1)
     new0 = pick2(f(ic_ref[:, 6:7] == slot), slots)
     keep("new0", new0[:, 0:NB])
-    keep("new1", pick2(f(ic_ref[:, 7:8] == slot), slots))
     u0 = dot3(li_ref[0], new0)
     keep("u0", u0)
+    new1 = pick2(f(ic_ref[:, 7:8] == slot), slots)
+    keep("new1", new1[:, 0:NB])
+    keep("lead1", dot3(li_ref[1], new1))
     fetches[0].wait()
     for n, name in enumerate(("low0", "end1")):
         raw = jnp.concatenate([held_ref[y, n] for y in range(8)], axis=0)
@@ -274,32 +276,45 @@
         store.wait()
 
 
-def final_kernel(ids, ic_ref, mine_ref, there_ref, li_ref, ui_ref, *refs):
+def own_kernel(ids, ic_ref, mine_ref, li_ref, ui_ref, out_ref):
+    core = ids[3]
+    slots = jnp.concatenate([mine_ref[x, 0:128] for x in range(4)], axis=0)
+    for x in range(4):
+        out_ref[NB + 16 * x : NB + 16 * x + 16, :] = mine_ref[x, 128:144]
+    place = jnp.where(core == 0, ic_ref[:, 7:8], ic_ref[:, 6:7])
+    new = pick2(f(place == iota((NB, 2 * NB), 1)), slots)
+
+    @pl.when(core == 0)
+    def _():
+        out_ref[0:NB, :] = dot3(new, ui_ref[0])
+
+    @pl.when(core == 1)
+    def _():
+        out_ref[0:NB, :] = dot3(dot3(li_ref[0], new), ui_ref[1])
+
+
+def final_kernel(ids, own_ref, there_ref, li_ref, ui_ref, *refs):
     me, col, core = ids[0], ids[1], ids[3]
     count = len(KEPT)
     out_ref, done_ref, sem, fetch_sem = refs[count], *refs[2 * count + 1 :]
     near = dict(zip(KEPT, refs[count + 1 : 2 * count + 1]))
     fetches = {}
-    order = ("u0", "new1", "back", "low0", "end1", "put", "base", "new0")
+    order = ("u0", "lead1", "back", "low0", "end1", "put", "base", "new0", "new1")
     for n, name in enumerate(order):
         far = refs[list(KEPT).index(name)]
         fetches[name] = pltpu.make_async_copy(far, near[name], fetch_sem.at[n])
         fetches[name].start()
-    mine, there = mine_ref[...], there_ref[...]
-    sides = [jnp.where(core == k, mine, there) for k in range(2)]
-    slots = [jnp.concatenate([v[x, 0:128] for x in range(4)], axis=0) for v in sides]
-    rows_back = [jnp.concatenate([v[x, 128:144] for x in range(4)], axis=0) for v in sides]
-    slot = iota((NB, 2 * NB), 1)
-    diag = dot3(pick2(f(ic_ref[:, 7:8] == slot), slots[0]), ui_ref[0])
-    new0_c1 = pick2(f(ic_ref[:, 6:7] == slot), slots[1])
-    fill = dot3(dot3(li_ref[0], new0_c1), ui_ref[1])
+    own, there = own_ref[...], there_ref[...]
+    sides = [jnp.where(core == k, own, there) for k in range(2)]
+    diag, fill = sides[0][0:NB], sides[1][0:NB]
+    rows_back = [v[NB : NB + 2 * NP] for v in sides]
+    turn1 = dot3(li_ref[1], diag)
     low0_back = dot3(rows_back[0], ui_ref[0])
     low1_back = dot3(rows_back[1], ui_ref[1]) - dot3(low0_back, fill)
     for name in order[:3]:
         fetches[name].wait()
     u0 = near["u0"][...]
-    next1 = near["new1"][...] - dot3(diag, u0)
-    u1 = dot3(li_ref[1], next1)
+    u1 = near["lead1"][...] - dot3(turn1, u0)
     back = near["back"][...] - dot3(low0_back, u0) - dot3(low1_back, u1)
     for name in order[3:]:
         fetches[name].wait()
@@ -340,7 +355,7 @@
 
                 @pl.when(col == 1)
                 def _():
-                    done_ref[0:NB, 0:NB] = next1[:, 0:NB]
+                    done_ref[0:NB, 0:NB] = near["new1"][...] - dot3(diag, u0[:, 0:NB])
 
         copies.append(pltpu.make_async_copy(done_ref.at[rows, :], out_ref.at[rows, :], sem.at[r]))
         copies[-1].start()
@@ -416,10 +431,11 @@
         ],
     )
     mine, kept = lax.optimization_barrier((mine, kept))
-    there = lax.ppermute(mine, "core", [(0, 1), (1, 0)])
+    own = call(own_kernel, shape(NB + 2 * NP, NB), ids, ic, mine, lower_inv, upper_inv)
+    there = lax.ppermute(own, "core", [(0, 1), (1, 0)])
     out = call(
-        final_kernel, shape(RD, RD), ids, ic, mine, there, lower_inv, upper_inv, *kept,
-        far=tuple(range(5, 5 + len(KEPT))), far_out=True,
+        final_kernel, shape(RD, RD), ids, own, there, lower_inv, upper_inv, *kept,
+        far=tuple(range(4, 4 + len(KEPT))), far_out=True,
         scratch=near + [
             pltpu.VMEM((RD, RD), F32), pltpu.SemaphoreType.DMA((3,)),
             pltpu.SemaphoreType.DMA((len(KEPT),)),

time: 137 us -> 138 us (level)
  Pallas kernels: 24.8 us -> 27.2 us
    pallas_call x6 -> x7, Pallas kernels: 24.8 us -> 27.2 us  [call(): pl.pallas_call(kernel, out_shape=outs, in_specs=smem + [anywhere if n in...]
  transfers between devices with their start and end apart: 19 -> 19, of which waited for: 8 -> 7; matrix products, arithmetic and copies ran while one was open for 1% -> 0% of each run, Pallas kernels for 8% -> 8%
where the time goes in v4:
time: 138 us
  starting transfers between devices  58 us (42%)
  Pallas kernels  27.2 us (20%)
  blocking collectives  18.9 us (14%)
  waiting for transfers between devices  17.2 us (12%)
  between operations  14.4 us (10%)
    pallas_call x7, Pallas kernels, call(): pl.pallas_call(kernel, out_shape=outs, in_specs=smem + [anywhere if n in...  27.2 us
    all_to_all x1, blocking collectives, fast(): main_z = lax.all_to_all(send, 'z', 0, 0)  18.9 us
    ppermute x7, starting transfers between devices, fast(): piece = piece + lax.ppermute(panel[k], 'y', [(0, k)])  15.2 us
    all_to_all x1, starting transfers between devices, fast(): rows_in = lax.all_to_all(rows, PROW, 0, 0)  13.7 us
    ppermute x7, starting transfers between devices, fast(): parts = [lax.ppermute(side, 'y', [(0, k)]) for k in AROUND]  13.1 us
    ppermute x7, waiting for transfers between devices, fast(): parts = [lax.ppermute(side, 'y', [(0, k)]) for k in AROUND]  7.95 us
    all_to_all x1, waiting for transfers between devices, fast(): rows_in = lax.all_to_all(rows, PROW, 0, 0)  7.13 us
    ppermute x1, starting transfers between devices, fast(): there = lax.ppermute(own, 'core', [(0, 1), (1, 0)])  5.98 us
  transfers between devices with their start and end apart: 19, of which 7 were waited for; matrix products, arithmetic and copies ran while one was open for 0% of the time, Pallas kernels for 8%

profile of v4, /device:TPU:1, one launch (start us, length us, event | category | flops | bytes accessed | tf_op | source)
XLA Modules:
  0.0 137.5 jit_solution(1881674998684814403)
XLA Ops:
  6.6 5.1 %shard_map.46 = (f32[32,5,2,768]{3,2,1,0:T(2,128)}, s32[8,256]{1,0:T(8,128)S(1)}, s32[256,8]{1,0:T(8,128)S(1)}, s32[1]{0:T(128)}, f32[96,256]{1,0:T(8,128)S(1)},...) custom-call(s32[4]{0:T(128)S(1)} %pad_add_fusion.ids, ...), custom_call_target="tpu_custom_call" | custom-call | flops 1000000 | bytes 4 | tf_op jit(solution)/shard_map/pallas_call | solution.py:373
  11.7 13.7 %all-to-all-start = ((f32[32,5,2,768]{3,2,1,0:T(2,128)}), f32[32,5,2,768]{3,2,1,0:T(2,128)S(1)}, u32[]{:S(2)}, u32[]{:S(2)}) async-start(f32[32,5,2,768]{3,2,1,0:T(2,128)} %get-tuple-element.124), calls=%async_computation | async-start | bytes 1966080 | tf_op jit(solution)/shard_map/all_to_all | solution.py:405
  25.5 7.5 %collective-permute-start = (f32[96,256]{1,0:T(8,128)S(1)}, f32[96,256]{1,0:T(8,128)S(1)}, u32[]{:S(2)}, u32[]{:S(2)}) collective-permute-start(f32[96,256]{1,0:T(8,128)S(1)} %get-tuple-element.126), channel_id=1, source_target_pairs={{0,8},{1,9},{16,24},{17,25},{32,40},{33,41},{48,56},{49,57},{64,72... | collective-permute-start | bytes 294920 | tf_op jit(solution)/shard_map/ppermute | solution.py:408
  33.0 1.3 collective-permute-start.1
  34.3 1.3 collective-permute-start.2
  35.6 1.3 collective-permute-start.3
  36.9 1.3 collective-permute-start.4
  38.2 1.3 collective-permute-start.5
  39.5 1.3 collective-permute-start.6
  41.1 1.3 collective-permute-done.6
  43.1 7.1 %all-to-all-done.in_ref = f32[32,5,2,768]{3,2,1,0:T(2,128)S(1)} async-done(((f32[32,5,2,768]{3,2,1,0:T(2,128)}), f32[32,5,2,768]{3,2,1,0:T(2,128)S(1)}, u32[]{:S(2)}, u32[]{:S(2)}) %all-to-all-start) | async-done | bytes 983072 | tf_op jit(solution)/shard_map/all_to_all | solution.py:405
  50.3 1.1 shard_map.47
  51.4 18.9 %all_to_all.20.in_ref = f32[8,24,768]{2,1,0:T(8,128)S(1)} all-to-all(f32[8,24,768]{2,1,0:T(8,128)S(1)} %shard_map.47), channel_id=1, replica_groups=mesh['z'=8,'x'=4,'y'=8,'core'=2] {'z'}, dimensions={0} | all-to-all | bytes 1179648 | tf_op jit(solution)/shard_map/all_to_all | solution.py:415
  70.3 1.4 shard_map.48
  71.7 5.0 %all-to-all-start.2 = ((f32[4,144,768]{2,1,0:T(8,128)}), f32[4,144,768]{2,1,0:T(8,128)}, u32[]{:S(2)}, u32[]{:S(2)}) async-start(f32[4,144,768]{2,1,0:T(8,128)} %get-tuple-element.135), calls=%async_computation.2 | async-start | bytes 3538944 | tf_op jit(solution)/shard_map/all_to_all | solution.py:417
  76.7 5.3 %collective-permute-start.13 = (f32[192,256]{1,0:T(8,128)S(1)}, f32[192,256]{1,0:T(8,128)S(1)}, u32[]{:S(2)}, u32[]{:S(2)}) collective-permute-start(f32[192,256]{1,0:T(8,128)S(1)} %get-tuple-element.134.refs_0_), channel_id=1, source_target_pairs={{0,14},{1,15},{16,30},{17,31},{32,46},{33,47},{48,62},{49,63},{64,... | collective-permute-start | bytes 589832 | tf_op jit(solution)/shard_map/ppermute | solution.py:418
  82.0 1.3 collective-permute-start.12
  83.3 1.3 collective-permute-start.11
  84.6 1.3 collective-permute-start.10
  85.9 1.3 collective-permute-start.9
  87.2 1.3 collective-permute-start.8
  88.5 1.3 collective-permute-start.7
  89.9 2.8 %collective-permute-done.9.refs_3_ = f32[192,256]{1,0:T(8,128)S(1)} collective-permute-done((f32[192,256]{1,0:T(8,128)S(1)}, f32[192,256]{1,0:T(8,128)S(1)}, u32[]{:S(2)}, u32[]{:S(2)}) %collective-permute-start.9) | collective-permute-done | bytes 196640 | tf_op jit(solution)/shard_map/ppermute | solution.py:418
  92.7 0.9 collective-permute-done.8.refs_2_
  93.6 4.2 %collective-permute-done.7.refs_1_ = f32[192,256]{1,0:T(8,128)S(1)} collective-permute-done((f32[192,256]{1,0:T(8,128)S(1)}, f32[192,256]{1,0:T(8,128)S(1)}, u32[]{:S(2)}, u32[]{:S(2)}) %collective-permute-start.7) | collective-permute-done | bytes 196640 | tf_op jit(solution)/shard_map/ppermute | solution.py:418
  97.8 1.5 %shard_map.49 = f32[4,144,256]{2,1,0:T(8,128)} custom-call(s32[4]{0:T(128)S(1)} %pad_add_fusion.ids, f32[192,256]{1,0:T(8,128)S(1)} %get-tuple-element.134.refs_0_, f32[192,256]{1,0:T(8,128)S(1)} %collective-permute-done.7.refs_1_, f32[192,256]{1,0:T(8,128)S(1)} %collective-permute-done.8.refs_2_, f32[192,256]{1,0:T(8,128)S(1)} %collective-permute-done.9.refs_3_, ...), custom_call_target="tpu_custom_call" | custom-call | bytes 196608 | tf_op jit(solution)/shard_map/pallas_call | solution.py:373
  99.3 4.9 %all-to-all-start.3 = ((f32[4,144,256]{2,1,0:T(8,128)}), f32[4,144,256]{2,1,0:T(8,128)S(1)}, u32[]{:S(2)}, u32[]{:S(2)}) async-start(f32[4,144,256]{2,1,0:T(8,128)} %shard_map.49), calls=%async_computation.3 | async-start | bytes 1179648 | tf_op jit(solution)/shard_map/all_to_all | solution.py:423
  104.3 7.6 %shard_map.50 = (f32[768,768]{1,0:T(8,128)}, f32[256,768]{1,0:T(8,128)}, f32[256,768]{1,0:T(8,128)}, f32[768,256]{1,0:T(8,128)}, f32[768,256]{1,0:T(8,128)}, /*i...) custom-call(s32[4]{0:T(128)} %copy-done.4, s32[8,256]{1,0:T(8,128)} %copy-done.3, ...), custom_call_target="tpu_custom_call" | custom-call | bytes 8192 | tf_op jit(solution)/shard_map/pallas_call | solution.py:373
  111.9 2.3 %shard_map.51.own_ref = f32[320,256]{1,0:T(8,128)S(1)} custom-call(s32[4]{0:T(128)S(1)} %copy-done.5, s32[256,8]{1,0:T(8,128)S(1)} %copy-done.2, f32[4,144,256]{2,1,0:T(8,128)S(1)} %all-to-all-done.3.mine_ref, f32[2,256,256]{2,1,0:T(8,128)} %li_ref.5, f32[2,256,256]{2,1,0:T(8,128)} %ui_ref.5), custom_call_target="tpu_custom_call" | custom-call | bytes 8192 | tf_op jit(solution)/shard_map/pallas_call | solution.py:373
  114.2 6.0 %collective-permute-start.14 = (f32[320,256]{1,0:T(8,128)S(1)}, f32[320,256]{1,0:T(8,128)S(1)}, u32[]{:S(2)}, u32[]{:S(2)}) collective-permute-start(f32[320,256]{1,0:T(8,128)S(1)} %shard_map.51.own_ref), channel_id=1, source_target_pairs={{0,1},{1,0},{2,3},{3,2},{4,5},{5,4},{6,7},{7,6},{8,9},{9,8},{10,11... | collective-permute-start | bytes 983048 | tf_op jit(solution)/shard_map/ppermute | solution.py:435
  121.4 0.7 copy-done.14
  122.2 8.2 %shard_map.52 = f32[768,768]{1,0:T(8,128)} custom-call(s32[4]{0:T(128)} %copy-done.4, f32[320,256]{1,0:T(8,128)} %copy-done, f32[320,256]{1,0:T(8,128)} %copy-done.14, f32[2,256,256]{2,1,0:T(8,128)} %li_ref.5, f32[2,256,256]{2,1,0:T(8,128)} %ui_ref.5, f32[768,768]{1,0:T(8,128)} %get-tuple-element.150.refs_0_, f32[256,768]{1,0:T(8,128)} %get-tuple-element.151.refs_1_, ...), custom_call_target="tpu_custom_call" | custom-call | bytes 196608 | tf_op jit(solution)/shard_map/pallas_call | solution.py:373
  (36 shorter events, 1.9 us)
Async XLA Ops:
  6.6 91.2 %copy-start.4 = (s32[4]{0:T(128)}, s32[4]{0:T(128)S(1)}, u32[]{:S(2)}) copy-start(s32[4]{0:T(128)S(1)} %pad_add_fusion.ids) | copy-start | bytes 52
  11.7 58.6 %copy-start.1 = (s32[256,8]{1,0:T(8,128)}, s32[256,8]{1,0:T(8,128)S(1)}, u32[]{:S(2)}) copy-start(s32[256,8]{1,0:T(8,128)S(1)} %get-tuple-element.122.ic_ref) | copy-start | bytes 24580
  11.7 58.6 %copy-start.3 = (s32[8,256]{1,0:T(8,128)}, s32[8,256]{1,0:T(8,128)S(1)}, u32[]{:S(2)}) copy-start(s32[8,256]{1,0:T(8,128)S(1)} %get-tuple-element.123.ir_ref) | copy-start | bytes 24580
  11.7 38.5 %all-to-all-start = ((f32[32,5,2,768]{3,2,1,0:T(2,128)}), f32[32,5,2,768]{3,2,1,0:T(2,128)S(1)}, u32[]{:S(2)}, u32[]{:S(2)}) async-start(f32[32,5,2,768]{3,2,1,0:T(2,128)} %get-tuple-element.124), calls=%async_computation | async-start | bytes 1966080 | tf_op jit(solution)/shard_map/all_to_all | solution.py:405
  25.4 73.9 %all-gather.2.cloned.1.call-start = ((), (), s32[]{:S(2)}) async-start(), calls=%async_computation.8 | async-start | bytes 1671168 | tf_op jit(solution)/shard_map/all_gather | solution.py:410
  25.5 12.7 %collective-permute-start = (f32[96,256]{1,0:T(8,128)S(1)}, f32[96,256]{1,0:T(8,128)S(1)}, u32[]{:S(2)}, u32[]{:S(2)}) collective-permute-start(f32[96,256]{1,0:T(8,128)S(1)} %get-tuple-element.126), channel_id=1, source_target_pairs={{0,8},{1,9},{16,24},{17,25},{32,40},{33,41},{48,56},{49,57},{64,72... | collective-permute-start | bytes 294920 | tf_op jit(solution)/shard_map/ppermute | solution.py:408
  33.0 6.5 %collective-permute-start.1 = (f32[96,256]{1,0:T(8,128)S(1)}, f32[96,256]{1,0:T(8,128)S(1)}, u32[]{:S(2)}, u32[]{:S(2)}) collective-permute-start(f32[96,256]{1,0:T(8,128)S(1)} %get-tuple-element.127), channel_id=1, source_target_pairs={{0,6},{1,7},{16,22},{17,23},{32,38},{33,39},{48,54},{49,55},{64,70... | collective-permute-start | bytes 294920 | tf_op jit(solution)/shard_map/ppermute | solution.py:408
  34.3 6.5 %collective-permute-start.2 = (f32[96,256]{1,0:T(8,128)S(1)}, f32[96,256]{1,0:T(8,128)S(1)}, u32[]{:S(2)}, u32[]{:S(2)}) collective-permute-start(f32[96,256]{1,0:T(8,128)S(1)} %get-tuple-element.128), channel_id=1, source_target_pairs={{0,10},{1,11},{16,26},{17,27},{32,42},{33,43},{48,58},{49,59},{64,... | collective-permute-start | bytes 294920 | tf_op jit(solution)/shard_map/ppermute | solution.py:408
  35.6 5.3 %collective-permute-start.3 = (f32[96,256]{1,0:T(8,128)S(1)}, f32[96,256]{1,0:T(8,128)S(1)}, u32[]{:S(2)}, u32[]{:S(2)}) collective-permute-start(f32[96,256]{1,0:T(8,128)S(1)} %get-tuple-element.129), channel_id=1, source_target_pairs={{0,4},{1,5},{16,20},{17,21},{32,36},{33,37},{48,52},{49,53},{64,68... | collective-permute-start | bytes 294920 | tf_op jit(solution)/shard_map/ppermute | solution.py:408
  36.9 4.0 %collective-permute-start.4 = (f32[96,256]{1,0:T(8,128)S(1)}, f32[96,256]{1,0:T(8,128)S(1)}, u32[]{:S(2)}, u32[]{:S(2)}) collective-permute-start(f32[96,256]{1,0:T(8,128)S(1)} %get-tuple-element.130), channel_id=1, source_target_pairs={{0,12},{1,13},{16,28},{17,29},{32,44},{33,45},{48,60},{49,61},{64,... | collective-permute-start | bytes 294920 | tf_op jit(solution)/shard_map/ppermute | solution.py:408
  38.2 2.9 %collective-permute-start.5 = (f32[96,256]{1,0:T(8,128)S(1)}, f32[96,256]{1,0:T(8,128)S(1)}, u32[]{:S(2)}, u32[]{:S(2)}) collective-permute-start(f32[96,256]{1,0:T(8,128)S(1)} %get-tuple-element.131), channel_id=1, source_target_pairs={{0,2},{1,3},{16,18},{17,19},{32,34},{33,35},{48,50},{49,51},{64,66... | collective-permute-start | bytes 294920 | tf_op jit(solution)/shard_map/ppermute | solution.py:408
  39.5 2.9 %collective-permute-start.6 = (f32[96,256]{1,0:T(8,128)S(1)}, f32[96,256]{1,0:T(8,128)S(1)}, u32[]{:S(2)}, u32[]{:S(2)}) collective-permute-start(f32[96,256]{1,0:T(8,128)S(1)} %get-tuple-element.132), channel_id=1, source_target_pairs={{0,14},{1,15},{16,30},{17,31},{32,46},{33,47},{48,62},{49,63},{64,... | collective-permute-start | bytes 294920 | tf_op jit(solution)/shard_map/ppermute | solution.py:408
  71.7 27.6 %all-to-all-start.2 = ((f32[4,144,768]{2,1,0:T(8,128)}), f32[4,144,768]{2,1,0:T(8,128)}, u32[]{:S(2)}, u32[]{:S(2)}) async-start(f32[4,144,768]{2,1,0:T(8,128)} %get-tuple-element.135), calls=%async_computation.2 | async-start | bytes 3538944 | tf_op jit(solution)/shard_map/all_to_all | solution.py:417
  76.7 27.6 %copy-start.7 = (f32[768,768]{1,0:T(8,128)S(1)}, f32[768,768]{1,0:T(8,128)}, u32[]{:S(2)}) copy-start(f32[768,768]{1,0:T(8,128)} %a_ref.3) | copy-start | bytes 7077892
  76.7 10.6 %collective-permute-start.13 = (f32[192,256]{1,0:T(8,128)S(1)}, f32[192,256]{1,0:T(8,128)S(1)}, u32[]{:S(2)}, u32[]{:S(2)}) collective-permute-start(f32[192,256]{1,0:T(8,128)S(1)} %get-tuple-element.134.refs_0_), channel_id=1, source_target_pairs={{0,14},{1,15},{16,30},{17,31},{32,46},{33,47},{48,62},{49,63},{64,... | collective-permute-start | bytes 589832 | tf_op jit(solution)/shard_map/ppermute | solution.py:418
  82.0 6.6 %collective-permute-start.12 = (f32[192,256]{1,0:T(8,128)S(1)}, f32[192,256]{1,0:T(8,128)S(1)}, u32[]{:S(2)}, u32[]{:S(2)}) collective-permute-start(f32[192,256]{1,0:T(8,128)S(1)} %get-tuple-element.134.refs_0_), channel_id=1, source_target_pairs={{0,2},{1,3},{16,18},{17,19},{32,34},{33,35},{48,50},{49,51},{64,66... | collective-permute-start | bytes 589832 | tf_op jit(solution)/shard_map/ppermute | solution.py:418
  83.3 6.6 %collective-permute-start.11 = (f32[192,256]{1,0:T(8,128)S(1)}, f32[192,256]{1,0:T(8,128)S(1)}, u32[]{:S(2)}, u32[]{:S(2)}) collective-permute-start(f32[192,256]{1,0:T(8,128)S(1)} %get-tuple-element.134.refs_0_), channel_id=1, source_target_pairs={{0,12},{1,13},{16,28},{17,29},{32,44},{33,45},{48,60},{49,61},{64,... | collective-permute-start | bytes 589832 | tf_op jit(solution)/shard_map/ppermute | solution.py:418
  84.6 5.3 %collective-permute-start.10 = (f32[192,256]{1,0:T(8,128)S(1)}, f32[192,256]{1,0:T(8,128)S(1)}, u32[]{:S(2)}, u32[]{:S(2)}) collective-permute-start(f32[192,256]{1,0:T(8,128)S(1)} %get-tuple-element.134.refs_0_), channel_id=1, source_target_pairs={{0,4},{1,5},{16,20},{17,21},{32,36},{33,37},{48,52},{49,53},{64,68... | collective-permute-start | bytes 589832 | tf_op jit(solution)/shard_map/ppermute | solution.py:418
  85.9 6.8 %collective-permute-start.9 = (f32[192,256]{1,0:T(8,128)S(1)}, f32[192,256]{1,0:T(8,128)S(1)}, u32[]{:S(2)}, u32[]{:S(2)}) collective-permute-start(f32[192,256]{1,0:T(8,128)S(1)} %get-tuple-element.134.refs_0_), channel_id=1, source_target_pairs={{0,10},{1,11},{16,26},{17,27},{32,42},{33,43},{48,58},{49,59},{64,... | collective-permute-start | bytes 589832 | tf_op jit(solution)/shard_map/ppermute | solution.py:418
  87.2 6.4 %collective-permute-start.8 = (f32[192,256]{1,0:T(8,128)S(1)}, f32[192,256]{1,0:T(8,128)S(1)}, u32[]{:S(2)}, u32[]{:S(2)}) collective-permute-start(f32[192,256]{1,0:T(8,128)S(1)} %get-tuple-element.134.refs_0_), channel_id=1, source_target_pairs={{0,6},{1,7},{16,22},{17,23},{32,38},{33,39},{48,54},{49,55},{64,70... | collective-permute-start | bytes 589832 | tf_op jit(solution)/shard_map/ppermute | solution.py:418
  88.5 9.3 %collective-permute-start.7 = (f32[192,256]{1,0:T(8,128)S(1)}, f32[192,256]{1,0:T(8,128)S(1)}, u32[]{:S(2)}, u32[]{:S(2)}) collective-permute-start(f32[192,256]{1,0:T(8,128)S(1)} %get-tuple-element.134.refs_0_), channel_id=1, source_target_pairs={{0,8},{1,9},{16,24},{17,25},{32,40},{33,41},{48,56},{49,57},{64,72... | collective-permute-start | bytes 589832 | tf_op jit(solution)/shard_map/ppermute | solution.py:418
  99.3 12.6 %all-to-all-start.3 = ((f32[4,144,256]{2,1,0:T(8,128)}), f32[4,144,256]{2,1,0:T(8,128)S(1)}, u32[]{:S(2)}, u32[]{:S(2)}) async-start(f32[4,144,256]{2,1,0:T(8,128)} %shard_map.49), calls=%async_computation.3 | async-start | bytes 1179648 | tf_op jit(solution)/shard_map/all_to_all | solution.py:423
  104.3 7.6 %copy-start.2 = (s32[256,8]{1,0:T(8,128)S(1)}, s32[256,8]{1,0:T(8,128)}, u32[]{:S(2)}) copy-start(s32[256,8]{1,0:T(8,128)} %copy-done.1) | copy-start | bytes 24580
  104.3 7.6 %copy-start.5 = (s32[4]{0:T(128)S(1)}, s32[4]{0:T(128)}, u32[]{:S(2)}) copy-start(s32[4]{0:T(128)} %copy-done.4) | copy-start | bytes 52
  114.2 7.2 %copy-start = (f32[320,256]{1,0:T(8,128)}, f32[320,256]{1,0:T(8,128)S(1)}, u32[]{:S(2)}) copy-start(f32[320,256]{1,0:T(8,128)S(1)} %shard_map.51.own_ref) | copy-start | bytes 983044
  114.2 7.2 %collective-permute-start.14 = (f32[320,256]{1,0:T(8,128)S(1)}, f32[320,256]{1,0:T(8,128)S(1)}, u32[]{:S(2)}, u32[]{:S(2)}) collective-permute-start(f32[320,256]{1,0:T(8,128)S(1)} %shard_map.51.own_ref), channel_id=1, source_target_pairs={{0,1},{1,0},{2,3},{3,2},{4,5},{5,4},{6,7},{7,6},{8,9},{9,8},{10,11... | collective-permute-start | bytes 983048 | tf_op jit(solution)/shard_map/ppermute | solution.py:435
  120.9 9.5 %copy-start.15 = (s32[2,256]{1,0:T(2,128)S(1)}, s32[2,256]{1,0:T(2,128)}, u32[]{:S(2)}) copy-start(s32[2,256]{1,0:T(2,128)} %p_ref.1) | copy-start | bytes 6148
  121.4 0.7 copy-start.14
Sparse Core Ops, SparseCore 0:
  50.4 41.2 all-gather.1

commit v5 on v3

--- a/solution.py
+++ b/solution.py
@@ -109,10 +109,18 @@
     return hi, (x - hi.astype(F32)).astype(BF16)
 
 
+def left3(a):
+    hi, lo = halves(a)
+    return jnp.concatenate([hi, hi, lo], axis=1)
+
+
+def right3(b):
+    hi, lo = halves(b)
+    return jnp.concatenate([hi, lo, hi], axis=0)
+
+
 def dot3(a, b):
-    ah, al = halves(a)
-    bh, bl = halves(b)
-    return bdot(jnp.concatenate([ah, ah, al], axis=1), jnp.concatenate([bh, bl, bh], axis=0))
+    return bdot(left3(a), right3(b))
 
 
 def pick2(p, x):
@@ -219,8 +227,8 @@
 
 
 KEPT = {
-    "base": (RD, RD), "new1": (NB, RD), "u0": (NB, RD), "low0": (RD, NB), "end1": (RD, NB),
-    "put": (RD, 2 * NP), "back": (2 * NP, RD), "new0": (NB, NB),
+    "base": (RD, RD), "lead1": (NB, RD), "u0": (NB, RD), "low0": (RD, NB), "end1": (RD, NB),
+    "put": (RD, 4 * NP), "back": (2 * NP, RD), "new0": (NB, NB), "new1": (NB, NB),
 }
 
 
@@ -244,8 +252,8 @@
         stores.append(pltpu.make_async_copy(near[name], far[name], store_sem.at[len(stores)]))
         stores[-1].start()
 
-    put = jnp.zeros((RD, 2 * NP), F32)
-    lane = iota((NB, 2 * NP), 1)
+    put = jnp.zeros((RD, 4 * NP), F32)
+    lane = iota((NB, 4 * NP), 1) & 63
     m = ((lane >> 1) & 7) * 4 + (lane >> 4)
     for g in range(2):
         own, loc = ir_ref[3 * g + 1 : 3 * g + 2, :], ir_ref[3 * g + 2 : 3 * g + 3, :]
@@ -258,17 +266,20 @@
     slot = iota((NB, 2 * NB), 1)
     new0 = pick2(f(ic_ref[:, 6:7] == slot), slots)
     keep("new0", new0[:, 0:NB])
-    keep("new1", pick2(f(ic_ref[:, 7:8] == slot), slots))
     u0 = dot3(li_ref[0], new0)
     keep("u0", u0)
+    new1 = pick2(f(ic_ref[:, 7:8] == slot), slots)
+    keep("new1", new1[:, 0:NB])
+    keep("lead1", dot3(li_ref[1], new1))
     fetches[0].wait()
     for n, name in enumerate(("low0", "end1")):
         raw = jnp.concatenate([held_ref[y, n] for y in range(8)], axis=0)
         keep(name, dot3(raw, ui_ref[n]))
     fetches[1].wait()
+    by_u0 = right3(u0)
     for r in range(3):
         rows = pl.ds(NB * r, NB)
-        near["base"][rows, :] = here_ref[rows, :] - dot3(near["low0"][rows, :], u0)
+        near["base"][rows, :] = here_ref[rows, :] - bdot(left3(near["low0"][rows, :]), by_u0)
     keep("base")
     for store in stores:
         store.wait()
@@ -280,7 +291,7 @@
     out_ref, done_ref, sem, fetch_sem = refs[count], *refs[2 * count + 1 :]
     near = dict(zip(KEPT, refs[count + 1 : 2 * count + 1]))
     fetches = {}
-    order = ("u0", "new1", "back", "low0", "end1", "put", "base", "new0")
+    order = ("u0", "lead1", "back", "low0", "end1", "put", "base", "new0", "new1")
     for n, name in enumerate(order):
         far = refs[list(KEPT).index(name)]
         fetches[name] = pltpu.make_async_copy(far, near[name], fetch_sem.at[n])
@@ -298,9 +309,13 @@
     for name in order[:3]:
         fetches[name].wait()
     u0 = near["u0"][...]
-    next1 = near["new1"][...] - dot3(diag, u0)
-    u1 = dot3(li_ref[1], next1)
-    back = near["back"][...] - dot3(low0_back, u0) - dot3(low1_back, u1)
+    by_u0 = right3(u0)
+    u1 = near["lead1"][...] - bdot(left3(dot3(li_ref[1], diag)), by_u0)
+    by_u1 = right3(u1)
+    back = near["back"][...] - bdot(left3(low0_back), by_u0) - bdot(left3(low1_back), by_u1)
+    by_u1 = jnp.concatenate([by_u1, *halves(-back)], axis=0)
+    by_fill = jnp.concatenate([right3(fill), *halves(-low1_back)], axis=0)
+    by_low0 = jnp.concatenate(halves(low0_back), axis=0)
     for name in order[3:]:
         fetches[name].wait()
     copies = []
@@ -308,17 +323,24 @@
         rows = pl.ds(NB * r, NB)
         put = near["put"][rows, :]
         moved = sum_cols(put) > 0
+        put = put.astype(BF16)
         low0 = near["low0"][rows, :]
-        low1 = near["end1"][rows, :] - dot3(low0, fill)
-        done_ref[rows, :] = jnp.where(moved, pick2(put, back), near["base"][rows, :] - dot3(low1, u1))
+        stay0 = jnp.where(moved, F32(0.0), low0)
+        low1 = jnp.where(moved, F32(0.0), near["end1"][rows, :]) - bdot(
+            jnp.concatenate([left3(stay0), put], axis=1), by_fill
+        )
+        stay1 = jnp.where(moved, F32(0.0), low1)
+        done_ref[rows, :] = jnp.where(moved, F32(0.0), near["base"][rows, :]) - bdot(
+            jnp.concatenate([left3(stay1), put], axis=1), by_u1
+        )
 
         @pl.when(col == 0)
         def _():
-            done_ref[rows, 0:NB] = jnp.where(moved, pick2(put, low0_back), low0)
+            done_ref[rows, 0:NB] = stay0 + bdot(put, by_low0)
 
         @pl.when(col == 1)
         def _():
-            done_ref[rows, 0:NB] = jnp.where(moved, pick2(put, low1_back), low1)
+            done_ref[rows, 0:NB] = low1
 
         if r == 0:
 
@@ -340,7 +362,7 @@
 
                 @pl.when(col == 1)
                 def _():
-                    done_ref[0:NB, 0:NB] = next1[:, 0:NB]
+                    done_ref[0:NB, 0:NB] = near["new1"][...] - dot3(diag, u0[:, 0:NB])
 
         copies.append(pltpu.make_async_copy(done_ref.at[rows, :], out_ref.at[rows, :], sem.at[r]))
         copies[-1].start()

time: 137 us -> 137 us (level)
  transfers between devices with their start and end apart: 19 -> 19, of which waited for: 8 -> 7; matrix products, arithmetic and copies ran while one was open for 1% -> 1% of each run, Pallas kernels for 8% -> 8%
where the time goes in v5:
time: 137 us
  starting transfers between devices  58.4 us (43%)
  Pallas kernels  25.6 us (19%)
  blocking collectives  18.9 us (14%)
  waiting for transfers between devices  17.7 us (13%)
  between operations  14.3 us (10%)
    pallas_call x6, Pallas kernels, call(): pl.pallas_call(kernel, out_shape=outs, in_specs=smem + [anywhere if n in...  25.6 us
    all_to_all x1, blocking collectives, fast(): main_z = lax.all_to_all(send, 'z', 0, 0)  18.9 us
    ppermute x7, starting transfers between devices, fast(): piece = piece + lax.ppermute(panel[k], 'y', [(0, k)])  15.2 us
    all_to_all x1, starting transfers between devices, fast(): rows_in = lax.all_to_all(rows, PROW, 0, 0)  13.7 us
    ppermute x7, starting transfers between devices, fast(): parts = [lax.ppermute(side, 'y', [(0, k)]) for k in AROUND]  13.1 us
    ppermute x7, waiting for transfers between devices, fast(): parts = [lax.ppermute(side, 'y', [(0, k)]) for k in AROUND]  7.95 us
    all_to_all x1, waiting for transfers between devices, fast(): rows_in = lax.all_to_all(rows, PROW, 0, 0)  7.13 us
    ppermute x1, starting transfers between devices, fast(): there = lax.ppermute(mine, 'core', [(0, 1), (1, 0)])  6.33 us
  transfers between devices with their start and end apart: 19, of which 7 were waited for; matrix products, arithmetic and copies ran while one was open for 1% of the time, Pallas kernels for 8%

profile of v5, /device:TPU:1, one launch (start us, length us, event | category | flops | bytes accessed | tf_op | source)
XLA Modules:
  0.0 136.7 jit_solution(8154639309908161551)
XLA Ops:
  6.6 5.1 %shard_map.46 = (f32[32,5,2,768]{3,2,1,0:T(2,128)}, s32[8,256]{1,0:T(8,128)S(1)}, s32[256,8]{1,0:T(8,128)S(1)}, s32[1]{0:T(128)}, f32[96,256]{1,0:T(8,128)S(1)},...) custom-call(s32[4]{0:T(128)S(1)} %pad_add_fusion.ids, ...), custom_call_target="tpu_custom_call" | custom-call | flops 1000000 | bytes 4 | tf_op jit(solution)/shard_map/pallas_call | solution.py:380
  11.7 13.7 %all-to-all-start = ((f32[32,5,2,768]{3,2,1,0:T(2,128)}), f32[32,5,2,768]{3,2,1,0:T(2,128)S(1)}, u32[]{:S(2)}, u32[]{:S(2)}) async-start(f32[32,5,2,768]{3,2,1,0:T(2,128)} %get-tuple-element.124), calls=%async_computation | async-start | bytes 1966080 | tf_op jit(solution)/shard_map/all_to_all | solution.py:412
  25.5 7.5 %collective-permute-start = (f32[96,256]{1,0:T(8,128)S(1)}, f32[96,256]{1,0:T(8,128)S(1)}, u32[]{:S(2)}, u32[]{:S(2)}) collective-permute-start(f32[96,256]{1,0:T(8,128)S(1)} %get-tuple-element.126), channel_id=1, source_target_pairs={{0,8},{1,9},{16,24},{17,25},{32,40},{33,41},{48,56},{49,57},{64,72... | collective-permute-start | bytes 294920 | tf_op jit(solution)/shard_map/ppermute | solution.py:415
  33.0 1.3 collective-permute-start.1
  34.3 1.3 collective-permute-start.2
  35.6 1.3 collective-permute-start.3
  36.9 1.3 collective-permute-start.4
  38.2 1.3 collective-permute-start.5
  39.5 1.3 collective-permute-start.6
  41.1 1.3 collective-permute-done.6
  43.1 7.1 %all-to-all-done.in_ref = f32[32,5,2,768]{3,2,1,0:T(2,128)S(1)} async-done(((f32[32,5,2,768]{3,2,1,0:T(2,128)}), f32[32,5,2,768]{3,2,1,0:T(2,128)S(1)}, u32[]{:S(2)}, u32[]{:S(2)}) %all-to-all-start) | async-done | bytes 983072 | tf_op jit(solution)/shard_map/all_to_all | solution.py:412
  50.3 1.1 shard_map.47
  51.4 18.9 %all_to_all.20.in_ref = f32[8,24,768]{2,1,0:T(8,128)S(1)} all-to-all(f32[8,24,768]{2,1,0:T(8,128)S(1)} %shard_map.47), channel_id=1, replica_groups=mesh['z'=8,'x'=4,'y'=8,'core'=2] {'z'}, dimensions={0} | all-to-all | bytes 1179648 | tf_op jit(solution)/shard_map/all_to_all | solution.py:422
  70.3 1.4 %shard_map.48 = (f32[4,144,768]{2,1,0:T(8,128)}, f32[192,256]{1,0:T(8,128)S(1)}) custom-call(f32[8,24,768]{2,1,0:T(8,128)S(1)} %all_to_all.20.in_ref), custom_call_target="tpu_custom_call" | custom-call | bytes 196608 | tf_op jit(solution)/shard_map/pallas_call | solution.py:380
  71.7 5.0 %all-to-all-start.2 = ((f32[4,144,768]{2,1,0:T(8,128)}), f32[4,144,768]{2,1,0:T(8,128)}, u32[]{:S(2)}, u32[]{:S(2)}) async-start(f32[4,144,768]{2,1,0:T(8,128)} %get-tuple-element.135), calls=%async_computation.2 | async-start | bytes 3538944 | tf_op jit(solution)/shard_map/all_to_all | solution.py:424
  76.7 5.3 %collective-permute-start.13 = (f32[192,256]{1,0:T(8,128)S(1)}, f32[192,256]{1,0:T(8,128)S(1)}, u32[]{:S(2)}, u32[]{:S(2)}) collective-permute-start(f32[192,256]{1,0:T(8,128)S(1)} %get-tuple-element.134.refs_0_), channel_id=1, source_target_pairs={{0,14},{1,15},{16,30},{17,31},{32,46},{33,47},{48,62},{49,63},{64,... | collective-permute-start | bytes 589832 | tf_op jit(solution)/shard_map/ppermute | solution.py:425
  82.0 1.3 collective-permute-start.12
  83.3 1.3 collective-permute-start.11
  84.6 1.3 collective-permute-start.10
  85.9 1.3 collective-permute-start.9
  87.2 1.3 collective-permute-start.8
  88.6 1.3 collective-permute-start.7
  89.9 2.9 %collective-permute-done.9.refs_3_ = f32[192,256]{1,0:T(8,128)S(1)} collective-permute-done((f32[192,256]{1,0:T(8,128)S(1)}, f32[192,256]{1,0:T(8,128)S(1)}, u32[]{:S(2)}, u32[]{:S(2)}) %collective-permute-start.9) | collective-permute-done | bytes 196640 | tf_op jit(solution)/shard_map/ppermute | solution.py:425
  92.8 0.9 collective-permute-done.8.refs_2_
  93.6 4.2 %collective-permute-done.7.refs_1_ = f32[192,256]{1,0:T(8,128)S(1)} collective-permute-done((f32[192,256]{1,0:T(8,128)S(1)}, f32[192,256]{1,0:T(8,128)S(1)}, u32[]{:S(2)}, u32[]{:S(2)}) %collective-permute-start.7) | collective-permute-done | bytes 196640 | tf_op jit(solution)/shard_map/ppermute | solution.py:425
  97.8 1.5 %shard_map.49 = f32[4,144,256]{2,1,0:T(8,128)} custom-call(s32[4]{0:T(128)S(1)} %pad_add_fusion.ids, f32[192,256]{1,0:T(8,128)S(1)} %get-tuple-element.134.refs_0_, f32[192,256]{1,0:T(8,128)S(1)} %collective-permute-done.7.refs_1_, f32[192,256]{1,0:T(8,128)S(1)} %collective-permute-done.8.refs_2_, f32[192,256]{1,0:T(8,128)S(1)} %collective-permute-done.9.refs_3_, ...), custom_call_target="tpu_custom_call" | custom-call | bytes 196608 | tf_op jit(solution)/shard_map/pallas_call | solution.py:380
  99.3 5.0 %all-to-all-start.3 = ((f32[4,144,256]{2,1,0:T(8,128)}), f32[4,144,256]{2,1,0:T(8,128)S(1)}, u32[]{:S(2)}, u32[]{:S(2)}) async-start(f32[4,144,256]{2,1,0:T(8,128)} %shard_map.49), calls=%async_computation.3 | async-start | bytes 1179648 | tf_op jit(solution)/shard_map/all_to_all | solution.py:430
  104.3 7.6 %shard_map.50 = (f32[768,768]{1,0:T(8,128)}, f32[256,768]{1,0:T(8,128)}, f32[256,768]{1,0:T(8,128)}, f32[768,256]{1,0:T(8,128)}, f32[768,256]{1,0:T(8,128)}, /*i...) custom-call(s32[4]{0:T(128)} %copy-done.2, s32[8,256]{1,0:T(8,128)} %copy-done.1, ...), custom_call_target="tpu_custom_call" | custom-call | bytes 8192 | tf_op jit(solution)/shard_map/pallas_call | solution.py:380
  111.9 6.3 %collective-permute-start.14 = (f32[4,144,256]{2,1,0:T(8,128)S(1)}, f32[4,144,256]{2,1,0:T(8,128)S(1)}, u32[]{:S(2)}, u32[]{:S(2)}) collective-permute-start(f32[4,144,256]{2,1,0:T(8,128)S(1)} %all-to-all-done.3.mine_ref), channel_id=1, source_target_pairs={{0,1},{1,0},{2,3},{3,2},{4,5},{5,4},{6,7},{7,6},{8,9},{9,8},{10,11... | collective-permute-start | bytes 1769480 | tf_op jit(solution)/shard_map/ppermute | solution.py:441
  118.9 1.0 collective-permute-done.14.there_ref
  119.8 0.8 copy-done.10
  120.7 8.9 %shard_map.51 = f32[768,768]{1,0:T(8,128)} custom-call(s32[4]{0:T(128)} %copy-done.2, s32[256,8]{1,0:T(8,128)} %copy-done, f32[4,144,256]{2,1,0:T(8,128)} %copy-done.9, f32[4,144,256]{2,1,0:T(8,128)} %copy-done.10, f32[2,256,256]{2,1,0:T(8,128)} %li_ref.3, f32[2,256,256]{2,1,0:T(8,128)} %ui_ref.3, f32[768,768]{1,0:T(8,128)} %get-tuple-element.150.refs_0_, ...), custom_call_target="tpu_custom_call" | custom-call | bytes 8192 | tf_op jit(solution)/shard_map/pallas_call | solution.py:380
  (31 shorter events, 1.4 us)
Async XLA Ops:
  6.6 91.2 %copy-start.2 = (s32[4]{0:T(128)}, s32[4]{0:T(128)S(1)}, u32[]{:S(2)}) copy-start(s32[4]{0:T(128)S(1)} %pad_add_fusion.ids) | copy-start | bytes 52
  11.7 58.6 %copy-start = (s32[256,8]{1,0:T(8,128)}, s32[256,8]{1,0:T(8,128)S(1)}, u32[]{:S(2)}) copy-start(s32[256,8]{1,0:T(8,128)S(1)} %get-tuple-element.122.ic_ref) | copy-start | bytes 24580
  11.7 58.6 %copy-start.1 = (s32[8,256]{1,0:T(8,128)}, s32[8,256]{1,0:T(8,128)S(1)}, u32[]{:S(2)}) copy-start(s32[8,256]{1,0:T(8,128)S(1)} %get-tuple-element.123.ir_ref) | copy-start | bytes 24580
  11.7 38.5 %all-to-all-start = ((f32[32,5,2,768]{3,2,1,0:T(2,128)}), f32[32,5,2,768]{3,2,1,0:T(2,128)S(1)}, u32[]{:S(2)}, u32[]{:S(2)}) async-start(f32[32,5,2,768]{3,2,1,0:T(2,128)} %get-tuple-element.124), calls=%async_computation | async-start | bytes 1966080 | tf_op jit(solution)/shard_map/all_to_all | solution.py:412
  25.4 73.9 %all-gather.2.cloned.1.call-start = ((), (), s32[]{:S(2)}) async-start(), calls=%async_computation.8 | async-start | bytes 1671168 | tf_op jit(solution)/shard_map/all_gather | solution.py:417
  25.5 12.7 %collective-permute-start = (f32[96,256]{1,0:T(8,128)S(1)}, f32[96,256]{1,0:T(8,128)S(1)}, u32[]{:S(2)}, u32[]{:S(2)}) collective-permute-start(f32[96,256]{1,0:T(8,128)S(1)} %get-tuple-element.126), channel_id=1, source_target_pairs={{0,8},{1,9},{16,24},{17,25},{32,40},{33,41},{48,56},{49,57},{64,72... | collective-permute-start | bytes 294920 | tf_op jit(solution)/shard_map/ppermute | solution.py:415
  33.0 6.5 %collective-permute-start.1 = (f32[96,256]{1,0:T(8,128)S(1)}, f32[96,256]{1,0:T(8,128)S(1)}, u32[]{:S(2)}, u32[]{:S(2)}) collective-permute-start(f32[96,256]{1,0:T(8,128)S(1)} %get-tuple-element.127), channel_id=1, source_target_pairs={{0,6},{1,7},{16,22},{17,23},{32,38},{33,39},{48,54},{49,55},{64,70... | collective-permute-start | bytes 294920 | tf_op jit(solution)/shard_map/ppermute | solution.py:415
  34.3 6.5 %collective-permute-start.2 = (f32[96,256]{1,0:T(8,128)S(1)}, f32[96,256]{1,0:T(8,128)S(1)}, u32[]{:S(2)}, u32[]{:S(2)}) collective-permute-start(f32[96,256]{1,0:T(8,128)S(1)} %get-tuple-element.128), channel_id=1, source_target_pairs={{0,10},{1,11},{16,26},{17,27},{32,42},{33,43},{48,58},{49,59},{64,... | collective-permute-start | bytes 294920 | tf_op jit(solution)/shard_map/ppermute | solution.py:415
  35.6 5.3 %collective-permute-start.3 = (f32[96,256]{1,0:T(8,128)S(1)}, f32[96,256]{1,0:T(8,128)S(1)}, u32[]{:S(2)}, u32[]{:S(2)}) collective-permute-start(f32[96,256]{1,0:T(8,128)S(1)} %get-tuple-element.129), channel_id=1, source_target_pairs={{0,4},{1,5},{16,20},{17,21},{32,36},{33,37},{48,52},{49,53},{64,68... | collective-permute-start | bytes 294920 | tf_op jit(solution)/shard_map/ppermute | solution.py:415
  36.9 4.0 %collective-permute-start.4 = (f32[96,256]{1,0:T(8,128)S(1)}, f32[96,256]{1,0:T(8,128)S(1)}, u32[]{:S(2)}, u32[]{:S(2)}) collective-permute-start(f32[96,256]{1,0:T(8,128)S(1)} %get-tuple-element.130), channel_id=1, source_target_pairs={{0,12},{1,13},{16,28},{17,29},{32,44},{33,45},{48,60},{49,61},{64,... | collective-permute-start | bytes 294920 | tf_op jit(solution)/shard_map/ppermute | solution.py:415
  38.2 2.9 %collective-permute-start.5 = (f32[96,256]{1,0:T(8,128)S(1)}, f32[96,256]{1,0:T(8,128)S(1)}, u32[]{:S(2)}, u32[]{:S(2)}) collective-permute-start(f32[96,256]{1,0:T(8,128)S(1)} %get-tuple-element.131), channel_id=1, source_target_pairs={{0,2},{1,3},{16,18},{17,19},{32,34},{33,35},{48,50},{49,51},{64,66... | collective-permute-start | bytes 294920 | tf_op jit(solution)/shard_map/ppermute | solution.py:415
  39.5 2.9 %collective-permute-start.6 = (f32[96,256]{1,0:T(8,128)S(1)}, f32[96,256]{1,0:T(8,128)S(1)}, u32[]{:S(2)}, u32[]{:S(2)}) collective-permute-start(f32[96,256]{1,0:T(8,128)S(1)} %get-tuple-element.132), channel_id=1, source_target_pairs={{0,14},{1,15},{16,30},{17,31},{32,46},{33,47},{48,62},{49,63},{64,... | collective-permute-start | bytes 294920 | tf_op jit(solution)/shard_map/ppermute | solution.py:415
  71.7 27.6 %all-to-all-start.2 = ((f32[4,144,768]{2,1,0:T(8,128)}), f32[4,144,768]{2,1,0:T(8,128)}, u32[]{:S(2)}, u32[]{:S(2)}) async-start(f32[4,144,768]{2,1,0:T(8,128)} %get-tuple-element.135), calls=%async_computation.2 | async-start | bytes 3538944 | tf_op jit(solution)/shard_map/all_to_all | solution.py:424
  76.7 27.6 %copy-start.4 = (f32[768,768]{1,0:T(8,128)S(1)}, f32[768,768]{1,0:T(8,128)}, u32[]{:S(2)}) copy-start(f32[768,768]{1,0:T(8,128)} %a_ref.3) | copy-start | bytes 7077892
  76.7 10.6 %collective-permute-start.13 = (f32[192,256]{1,0:T(8,128)S(1)}, f32[192,256]{1,0:T(8,128)S(1)}, u32[]{:S(2)}, u32[]{:S(2)}) collective-permute-start(f32[192,256]{1,0:T(8,128)S(1)} %get-tuple-element.134.refs_0_), channel_id=1, source_target_pairs={{0,14},{1,15},{16,30},{17,31},{32,46},{33,47},{48,62},{49,63},{64,... | collective-permute-start | bytes 589832 | tf_op jit(solution)/shard_map/ppermute | solution.py:425
  82.0 6.6 %collective-permute-start.12 = (f32[192,256]{1,0:T(8,128)S(1)}, f32[192,256]{1,0:T(8,128)S(1)}, u32[]{:S(2)}, u32[]{:S(2)}) collective-permute-start(f32[192,256]{1,0:T(8,128)S(1)} %get-tuple-element.134.refs_0_), channel_id=1, source_target_pairs={{0,2},{1,3},{16,18},{17,19},{32,34},{33,35},{48,50},{49,51},{64,66... | collective-permute-start | bytes 589832 | tf_op jit(solution)/shard_map/ppermute | solution.py:425
  83.3 6.6 %collective-permute-start.11 = (f32[192,256]{1,0:T(8,128)S(1)}, f32[192,256]{1,0:T(8,128)S(1)}, u32[]{:S(2)}, u32[]{:S(2)}) collective-permute-start(f32[192,256]{1,0:T(8,128)S(1)} %get-tuple-element.134.refs_0_), channel_id=1, source_target_pairs={{0,12},{1,13},{16,28},{17,29},{32,44},{33,45},{48,60},{49,61},{64,... | collective-permute-start | bytes 589832 | tf_op jit(solution)/shard_map/ppermute | solution.py:425
  84.6 5.3 %collective-permute-start.10 = (f32[192,256]{1,0:T(8,128)S(1)}, f32[192,256]{1,0:T(8,128)S(1)}, u32[]{:S(2)}, u32[]{:S(2)}) collective-permute-start(f32[192,256]{1,0:T(8,128)S(1)} %get-tuple-element.134.refs_0_), channel_id=1, source_target_pairs={{0,4},{1,5},{16,20},{17,21},{32,36},{33,37},{48,52},{49,53},{64,68... | collective-permute-start | bytes 589832 | tf_op jit(solution)/shard_map/ppermute | solution.py:425
  85.9 6.8 %collective-permute-start.9 = (f32[192,256]{1,0:T(8,128)S(1)}, f32[192,256]{1,0:T(8,128)S(1)}, u32[]{:S(2)}, u32[]{:S(2)}) collective-permute-start(f32[192,256]{1,0:T(8,128)S(1)} %get-tuple-element.134.refs_0_), channel_id=1, source_target_pairs={{0,10},{1,11},{16,26},{17,27},{32,42},{33,43},{48,58},{49,59},{64,... | collective-permute-start | bytes 589832 | tf_op jit(solution)/shard_map/ppermute | solution.py:425
  87.2 6.4 %collective-permute-start.8 = (f32[192,256]{1,0:T(8,128)S(1)}, f32[192,256]{1,0:T(8,128)S(1)}, u32[]{:S(2)}, u32[]{:S(2)}) collective-permute-start(f32[192,256]{1,0:T(8,128)S(1)} %get-tuple-element.134.refs_0_), channel_id=1, source_target_pairs={{0,6},{1,7},{16,22},{17,23},{32,38},{33,39},{48,54},{49,55},{64,70... | collective-permute-start | bytes 589832 | tf_op jit(solution)/shard_map/ppermute | solution.py:425
  88.6 9.3 %collective-permute-start.7 = (f32[192,256]{1,0:T(8,128)S(1)}, f32[192,256]{1,0:T(8,128)S(1)}, u32[]{:S(2)}, u32[]{:S(2)}) collective-permute-start(f32[192,256]{1,0:T(8,128)S(1)} %get-tuple-element.134.refs_0_), channel_id=1, source_target_pairs={{0,8},{1,9},{16,24},{17,25},{32,40},{33,41},{48,56},{49,57},{64,72... | collective-permute-start | bytes 589832 | tf_op jit(solution)/shard_map/ppermute | solution.py:425
  99.3 12.5 %all-to-all-start.3 = ((f32[4,144,256]{2,1,0:T(8,128)}), f32[4,144,256]{2,1,0:T(8,128)S(1)}, u32[]{:S(2)}, u32[]{:S(2)}) async-start(f32[4,144,256]{2,1,0:T(8,128)} %shard_map.49), calls=%async_computation.3 | async-start | bytes 1179648 | tf_op jit(solution)/shard_map/all_to_all | solution.py:430
  111.9 8.0 %copy-start.9 = (f32[4,144,256]{2,1,0:T(8,128)}, f32[4,144,256]{2,1,0:T(8,128)S(1)}, u32[]{:S(2)}) copy-start(f32[4,144,256]{2,1,0:T(8,128)S(1)} %all-to-all-done.3.mine_ref) | copy-start | bytes 1769476
  111.9 8.0 %collective-permute-start.14 = (f32[4,144,256]{2,1,0:T(8,128)S(1)}, f32[4,144,256]{2,1,0:T(8,128)S(1)}, u32[]{:S(2)}, u32[]{:S(2)}) collective-permute-start(f32[4,144,256]{2,1,0:T(8,128)S(1)} %all-to-all-done.3.mine_ref), channel_id=1, source_target_pairs={{0,1},{1,0},{2,3},{3,2},{4,5},{5,4},{6,7},{7,6},{8,9},{9,8},{10,11... | collective-permute-start | bytes 1769480 | tf_op jit(solution)/shard_map/ppermute | solution.py:441
  118.8 10.8 %copy-start.11 = (s32[2,256]{1,0:T(2,128)S(1)}, s32[2,256]{1,0:T(2,128)}, u32[]{:S(2)}) copy-start(s32[2,256]{1,0:T(2,128)} %p_ref.1) | copy-start | bytes 6148
  119.8 0.8 copy-start.10
Sparse Core Ops, SparseCore 0:
  50.4 41.2 all-gather.1
